TPU v7x, 512 devices: a whole 4x8x8 slice. The times are simulated.
512 devices in a mesh: tok: 128 (over y, z, core), head: 4 (over x).
Axes of the slice: x: 4, y: 8, z: 8, core: 2. Of those that a mesh axis runs over, the one named last changes fastest.
Arguments:
- teacher_q: bfloat16 [16384, 5120], P('tok', 'head'), may hold values from -24 to 24
- teacher_k: bfloat16 [16384, 5120], P('tok', 'head'), may hold values from -24 to 24
- teacher_v: bfloat16 [16384, 5120], P('tok', 'head'), may hold values from -24 to 24
- student_q: bfloat16 [16384, 1536], P('tok', 'head'), may hold values from -24 to 24
- student_k: bfloat16 [16384, 1536], P('tok', 'head'), may hold values from -24 to 24
- student_v: bfloat16 [16384, 1536], P('tok', 'head'), may hold values from -24 to 24
- doc_ids: int32 [16384], replicated, may hold values from 0 to 127, never falling along the last dimension, each value on 1 to 384 neighbouring positions
- row_weight: float32 [16384], replicated, may hold values from 4 to 64
Outputs:
- grad_q: float32 [16384, 1536], P('tok', 'head')
- grad_k: float32 [16384, 1536], P('tok', 'head')
- grad_v: float32 [16384, 1536], P('tok', 'head')
- loss: float32 [], replicated
Inputs may be any that keep to these rules, and one draw needn't show every extreme that they name: `doc_ids`: document ids never fall along the packed tokens.
All inputs are finite; a program needn't handle non-finite values.
Results may differ from a plain program's by a relative error of at most 0.008.
Values may be sent and summed in bfloat16 or wider, within the bound.
No kernel may reach another device: no remote copies, remote signals or barrier semaphores. Data moves between devices by JAX's collectives and lax.ppermute only.
A program may use at most 64 MiB of HBM per device.

v0:
```python
import jax
import jax.numpy as jnp
from jax import lax
from jax.sharding import PartitionSpec as P

H = 32
DT = 160
DS = 48


def from_behind(value, axis, steps):
    count = lax.axis_size(axis)
    initial, last = (max(0, -steps), min(count, count - steps))
    return lax.ppermute(value, axis, [(source, source + steps) for source in range(initial, last)])


def row_lse(score):
    top = jnp.max(score, axis=-1)
    total = jnp.sum(jnp.exp(score - top[:, None]), axis=-1)
    return jnp.log(total) + top


def head_terms(t_rows, t_keys, s_rows, s_keys, allowed, weight):
    inner = (((1,), (1,)), ((), ()))
    zt = jnp.where(
        allowed,
        lax.dot_general(t_rows, t_keys, inner, preferred_element_type=jnp.float32) * DT ** (-0.5),
        -1e30,
    )
    zs = jnp.where(
        allowed,
        lax.dot_general(s_rows, s_keys, inner, preferred_element_type=jnp.float32) * DS ** (-0.5),
        -1e30,
    )
    lt = row_lse(zt)
    ls = row_lse(zs)
    pt = jnp.exp(zt - lt[:, None])
    ps = jnp.exp(zs - ls[:, None])
    kl_rows = jnp.sum(pt * (zt - zs), axis=-1) - lt + ls
    total = jnp.sum(kl_rows * weight)
    grads = ((weight * DS ** (-0.5))[:, None] * (ps - pt)).astype(jnp.bfloat16)
    row_part = jnp.dot(grads, s_keys, preferred_element_type=jnp.float32)
    key_part = lax.dot_general(
        grads, s_rows, (((0,), (0,)), ((), ())), preferred_element_type=jnp.float32
    )
    return (total, row_part, key_part)


def block_mask(all_docs, first_key, rows):
    key_docs = lax.dynamic_slice_in_dim(all_docs, first_key + 3 * rows, 4 * rows)
    query_docs = key_docs[3 * rows :]
    key_pos = first_key + jnp.arange(4 * rows, dtype=jnp.int32)
    query_pos = first_key + 3 * rows + jnp.arange(rows, dtype=jnp.int32)
    return (
        (key_pos[None, :] <= query_pos[:, None])
        & (key_pos[None, :] >= 0)
        & (key_docs[None, :] == query_docs[:, None])
    )


def body(teacher_q, teacher_k, teacher_v, student_q, student_k, student_v, doc_ids, row_weight):
    rows = teacher_q.shape[0]
    lead = 3 * rows
    t_width = teacher_q.shape[1]
    s_width = student_q.shape[1]
    heads = s_width // DS
    device = lax.axis_index("tok")
    all_docs = jnp.concatenate([jnp.full((lead,), -1, jnp.int32), doc_ids])
    packed = jnp.concatenate(
        [teacher_q, teacher_k, teacher_v, student_q, student_k, student_v], axis=1
    )
    earlier = []
    for step in range(1, 4):
        earlier.append(from_behind(packed, "tok", step))
    window = jnp.concatenate([earlier[2], earlier[1], earlier[0], packed], axis=0)
    allowed = block_mask(all_docs, (device - 3) * rows, rows)
    weight = lax.dynamic_slice_in_dim(row_weight, device * rows, rows)
    total = jnp.zeros((), jnp.float32)
    row_grads = []
    key_grads = []
    for rel in range(3):
        row_cols = []
        key_cols = []
        for head_num in range(heads):
            t_start = rel * t_width + head_num * DT
            s_start = 3 * t_width + rel * s_width + head_num * DS
            t_keys = window[:, t_start : t_start + DT]
            s_keys = window[:, s_start : s_start + DS]
            part, row_part, key_part = head_terms(
                t_keys[lead:], t_keys, s_keys[lead:], s_keys, allowed, weight
            )
            total = total + part
            row_cols.append(row_part)
            key_cols.append(key_part)
        row_grads.append(jnp.concatenate(row_cols, axis=1))
        key_grads.append(jnp.concatenate(key_cols, axis=1))
    returned = jnp.zeros((rows, 3 * s_width), jnp.float32)
    for step in range(1, 4):
        lower = (3 - step) * rows
        piece = jnp.concatenate([g[lower : lower + rows] for g in key_grads], axis=1)
        returned = returned + from_behind(piece.astype(jnp.bfloat16), "tok", -step).astype(
            piece.dtype
        )
    outputs = []
    for rel in range(3):
        own = row_grads[rel] + key_grads[rel][lead:]
        outputs.append(own + returned[:, rel * s_width : (rel + 1) * s_width])
    whole = lax.psum(total, ("tok", "head"))
    loss = whole / (3 * H * rows * lax.axis_size("tok"))
    return (outputs[0], outputs[1], outputs[2], loss)


def solution(mesh):
    placed = (
        P("tok", "head"),
        P("tok", "head"),
        P("tok", "head"),
        P("tok", "head"),
        P("tok", "head"),
        P("tok", "head"),
        P(),
        P(),
    )
    return jax.shard_map(
        body,
        mesh=mesh,
        in_specs=placed,
        out_specs=(P("tok", "head"), P("tok", "head"), P("tok", "head"), P()),
        check_vma=False,
    )
```

profile of v0, /device:TPU:1, one launch (start us, length us, event | category | flops | bytes accessed | tf_op | source)
XLA Modules:
  0.0 277.5 jit_solution(2283212092675322455)
XLA Ops:
  0.6 1.0 constant_dynamic-update-slice_fusion.5
  1.6 1.0 constant_dynamic-update-slice_fusion.4
  2.6 1.0 constant_dynamic-update-slice_fusion.3
  3.6 0.9 constant_dynamic-update-slice_fusion.2
  4.5 0.9 constant_dynamic-update-slice_fusion.1
  5.5 0.9 constant_dynamic-update-slice_fusion
  6.4 5.4 %collective-permute-start.2 = (bf16[128,4992]{1,0:T(8,128)(2,1)S(1)}, bf16[128,4992]{1,0:T(8,128)(2,1)S(1)}, u32[]{:S(2)}, u32[]{:S(2)}) collective-permute-start(bf16[128,4992]{1,0:T(8,128)(2,1)S(1)} %constant_dynamic-update-slice_fusion), channel_id=1, source_target_pairs={{0,4},{4,8},{8,12},{12,16},{16,20},{20,24},{24,28},{28,32},{32,36}... | collective-permute-start | bytes 3833864 | tf_op jit(solution)/shard_map/ppermute | solution.py:14
  11.8 5.0 %collective-permute-start.1 = (bf16[128,4992]{1,0:T(8,128)(2,1)S(1)}, bf16[128,4992]{1,0:T(8,128)(2,1)}, u32[]{:S(2)}, u32[]{:S(2)}) collective-permute-start(bf16[128,4992]{1,0:T(8,128)(2,1)S(1)} %constant_dynamic-update-slice_fusion), channel_id=1, source_target_pairs={{0,8},{4,12},{8,16},{12,20},{16,24},{20,28},{24,32},{28,36},{32,40... | collective-permute-start | bytes 3833864 | tf_op jit(solution)/shard_map/ppermute | solution.py:14
  16.8 4.0 %collective-permute-start = (bf16[128,4992]{1,0:T(8,128)(2,1)S(1)}, bf16[128,4992]{1,0:T(8,128)(2,1)}, u32[]{:S(2)}, u32[]{:S(2)}) collective-permute-start(bf16[128,4992]{1,0:T(8,128)(2,1)S(1)} %constant_dynamic-update-slice_fusion), channel_id=1, source_target_pairs={{0,12},{4,16},{8,20},{12,24},{16,28},{20,32},{24,36},{28,40},{32,4... | collective-permute-start | bytes 3833864 | tf_op jit(solution)/shard_map/ppermute | solution.py:14
  20.9 0.8 pad_dynamic-slice_fusion
  21.7 13.6 %collective-permute-done.2 = bf16[128,4992]{1,0:T(8,128)(2,1)S(1)} collective-permute-done((bf16[128,4992]{1,0:T(8,128)(2,1)S(1)}, bf16[128,4992]{1,0:T(8,128)(2,1)S(1)}, u32[]{:S(2)}, u32[]{:S(2)}) %collective-permute-start.2) | collective-permute-done | bytes 1277984 | tf_op jit(solution)/shard_map/ppermute | solution.py:14
  35.2 27.4 %collective-permute-done.1 = bf16[128,4992]{1,0:T(8,128)(2,1)} collective-permute-done((bf16[128,4992]{1,0:T(8,128)(2,1)S(1)}, bf16[128,4992]{1,0:T(8,128)(2,1)}, u32[]{:S(2)}, u32[]{:S(2)}) %collective-permute-start.1) | collective-permute-done | bytes 1277984 | tf_op jit(solution)/shard_map/ppermute | solution.py:14
  62.6 18.2 %collective-permute-done = bf16[128,4992]{1,0:T(8,128)(2,1)} collective-permute-done((bf16[128,4992]{1,0:T(8,128)(2,1)S(1)}, bf16[128,4992]{1,0:T(8,128)(2,1)}, u32[]{:S(2)}, u32[]{:S(2)}) %collective-permute-start) | collective-permute-done | bytes 1277984 | tf_op jit(solution)/shard_map/ppermute | solution.py:14
  80.8 2.6 pad_maximum_fusion
  93.3 0.4 fusion.272
  96.9 0.5 fusion.279
  101.8 1.5 multiply_reduce_fusion.24
  105.9 0.7 multiply_reduce_fusion.36
  106.6 0.7 multiply_reduce_fusion.42
  110.1 0.7 multiply_reduce_fusion.30
  119.4 0.4 convolution_dynamic-update-slice_fusion.30
  123.8 1.3 collective-permute-start.4
  125.1 1.3 collective-permute-start.5
  126.4 1.9 collective-permute-start.3
  143.2 1.8 convolution_dynamic-update-slice_fusion.41
  145.0 123.9 %psum.7 = f32[]{:T(128)} all-reduce(f32[]{:T(128)S(6)} %add.650), channel_id=1, replica_groups=mesh['tok'=128,'head'=4] {'tok','head'}, use_global_device_ids=true, to_apply=%region_144.145 | all-reduce | flops 1 | bytes 8 | tf_op jit(solution)/shard_map/psum | solution.py:108
  269.6 1.8 convolution_dynamic-update-slice_fusion.40
  271.4 1.2 convert_add_fusion
  272.6 1.2 slice_add_fusion
  273.9 0.8 copy.14
  274.7 0.8 copy.13
  275.5 0.8 copy.12
  (205 shorter events, 34.8 us)
Async XLA Ops:
  6.4 28.9 %collective-permute-start.2 = (bf16[128,4992]{1,0:T(8,128)(2,1)S(1)}, bf16[128,4992]{1,0:T(8,128)(2,1)S(1)}, u32[]{:S(2)}, u32[]{:S(2)}) collective-permute-start(bf16[128,4992]{1,0:T(8,128)(2,1)S(1)} %constant_dynamic-update-slice_fusion), channel_id=1, source_target_pairs={{0,4},{4,8},{8,12},{12,16},{16,20},{20,24},{24,28},{28,32},{32,36}... | collective-permute-start | bytes 3833864 | tf_op jit(solution)/shard_map/ppermute | solution.py:14
  11.8 50.8 %collective-permute-start.1 = (bf16[128,4992]{1,0:T(8,128)(2,1)S(1)}, bf16[128,4992]{1,0:T(8,128)(2,1)}, u32[]{:S(2)}, u32[]{:S(2)}) collective-permute-start(bf16[128,4992]{1,0:T(8,128)(2,1)S(1)} %constant_dynamic-update-slice_fusion), channel_id=1, source_target_pairs={{0,8},{4,12},{8,16},{12,20},{16,24},{20,28},{24,32},{28,36},{32,40... | collective-permute-start | bytes 3833864 | tf_op jit(solution)/shard_map/ppermute | solution.py:14
  16.8 63.9 %collective-permute-start = (bf16[128,4992]{1,0:T(8,128)(2,1)S(1)}, bf16[128,4992]{1,0:T(8,128)(2,1)}, u32[]{:S(2)}, u32[]{:S(2)}) collective-permute-start(bf16[128,4992]{1,0:T(8,128)(2,1)S(1)} %constant_dynamic-update-slice_fusion), channel_id=1, source_target_pairs={{0,12},{4,16},{8,20},{12,24},{16,28},{20,32},{24,36},{28,40},{32,4... | collective-permute-start | bytes 3833864 | tf_op jit(solution)/shard_map/ppermute | solution.py:14
  21.6 61.7 %copy-start.4 = (bf16[128,1280]{1,0:T(8,128)(2,1)S(1)}, bf16[128,1280]{1,0:T(8,128)(2,1)}, u32[]{:S(2)}) copy-start(bf16[128,1280]{1,0:T(8,128)(2,1)} %param.10) | copy-start | bytes 983044
  21.7 62.1 %copy-start.3 = (bf16[128,384]{1,0:T(8,128)(2,1)S(1)}, bf16[128,384]{1,0:T(8,128)(2,1)}, u32[]{:S(2)}) copy-start(bf16[128,384]{1,0:T(8,128)(2,1)} %param.13) | copy-start | bytes 294916
  83.4 39.7 %copy-start = (bf16[512,4992]{1,0:T(8,128)(2,1)}, bf16[512,4992]{1,0:T(8,128)(2,1)S(1)}, u32[]{:S(2)}) copy-start(bf16[512,4992]{1,0:T(8,128)(2,1)S(1)} %pad_maximum_fusion) | copy-start | bytes 15335428
  84.5 4.5 %copy-start.5 = (bf16[128,1280]{1,0:T(8,128)(2,1)S(1)}, bf16[128,1280]{1,0:T(8,128)(2,1)}, u32[]{:S(2)}) copy-start(bf16[128,1280]{1,0:T(8,128)(2,1)} %param.9) | copy-start | bytes 983044
  84.8 4.6 %copy-start.2 = (bf16[128,384]{1,0:T(8,128)(2,1)S(1)}, bf16[128,384]{1,0:T(8,128)(2,1)}, u32[]{:S(2)}) copy-start(bf16[128,384]{1,0:T(8,128)(2,1)} %param.12) | copy-start | bytes 294916
  90.1 4.5 %copy-start.6 = (bf16[128,1280]{1,0:T(8,128)(2,1)S(1)}, bf16[128,1280]{1,0:T(8,128)(2,1)}, u32[]{:S(2)}) copy-start(bf16[128,1280]{1,0:T(8,128)(2,1)} %param.8) | copy-start | bytes 983044
  90.5 4.6 %copy-start.1 = (bf16[128,384]{1,0:T(8,128)(2,1)S(1)}, bf16[128,384]{1,0:T(8,128)(2,1)}, u32[]{:S(2)}) copy-start(bf16[128,384]{1,0:T(8,128)(2,1)} %param.11) | copy-start | bytes 294916
  114.3 14.1 %copy-start.8 = (f32[128,384]{0,1:T(8,128)}, f32[128,384]{0,1:T(8,128)S(1)}, u32[]{:S(2)}) copy-start(f32[128,384]{0,1:T(8,128)S(1)} %convolution_dynamic-update-slice_fusion.42) | copy-start | bytes 589828
  119.0 4.6 %copy-start.7 = (f32[128,384]{0,1:T(8,128)}, f32[128,384]{0,1:T(8,128)S(1)}, u32[]{:S(2)}) copy-start(f32[128,384]{0,1:T(8,128)S(1)} %convolution_dynamic-update-slice_fusion.32) | copy-start | bytes 589828
  123.4 5.0 %copy-start.9 = (f32[128,384]{0,1:T(8,128)}, f32[128,384]{0,1:T(8,128)S(1)}, u32[]{:S(2)}) copy-start(f32[128,384]{0,1:T(8,128)S(1)} %convolution_dynamic-update-slice_fusion.24) | copy-start | bytes 589828
  123.8 147.6 %collective-permute-start.4 = (bf16[128,1152]{0,1:T(8,128)(2,1)S(1)}, bf16[128,1152]{0,1:T(8,128)(2,1)}, u32[]{:S(2)}, u32[]{:S(2)}) collective-permute-start(bf16[128,1152]{0,1:T(8,128)(2,1)S(1)} %pad_maximum_fusion.2), channel_id=1, source_target_pairs={{8,0},{12,4},{16,8},{20,12},{24,16},{28,20},{32,24},{36,28},{40,32... | collective-permute-start | bytes 884744 | tf_op jit(solution)/shard_map/ppermute | solution.py:14
  125.1 146.3 %collective-permute-start.5 = (bf16[128,1152]{0,1:T(8,128)(2,1)S(1)}, bf16[128,1152]{0,1:T(8,128)(2,1)}, u32[]{:S(2)}, u32[]{:S(2)}) collective-permute-start(bf16[128,1152]{0,1:T(8,128)(2,1)S(1)} %pad_maximum_fusion.3), channel_id=1, source_target_pairs={{12,0},{16,4},{20,8},{24,12},{28,16},{32,20},{36,24},{40,28},{44,3... | collective-permute-start | bytes 884744 | tf_op jit(solution)/shard_map/ppermute | solution.py:14
  126.4 145.0 %collective-permute-start.3 = (bf16[128,1152]{0,1:T(8,128)(2,1)S(1)}, bf16[128,1152]{0,1:T(8,128)(2,1)}, u32[]{:S(2)}, u32[]{:S(2)}) collective-permute-start(bf16[128,1152]{0,1:T(8,128)(2,1)S(1)} %pad_maximum_fusion.1), channel_id=1, source_target_pairs={{4,0},{8,4},{12,8},{16,12},{20,16},{24,20},{28,24},{32,28},{36,32}... | collective-permute-start | bytes 884744 | tf_op jit(solution)/shard_map/ppermute | solution.py:14
where the time goes:
time: 278 us; the launch traced here: 277 us
  blocking collectives  124 us (45%)
  waiting for transfers between devices  59.1 us (21%)
  matrix products  32.1 us (12%)
  starting transfers between devices  19 us (7%)
  between operations  18.1 us (7%)
  other arithmetic  16.8 us (6%)
  local copies, waits for them, and re-layouts  8.38 us (3%)
    psum x1, blocking collectives, body(): whole = lax.psum(total, ('tok', 'head'))  124 us
    ppermute x6, waiting for transfers between devices, from_behind(): lax.ppermute(value, axis, [(source, source + steps) for source in range(i...  59.1 us
    ppermute x6, starting transfers between devices, from_behind(): lax.ppermute(value, axis, [(source, source + steps) for source in range(i...  19 us
    dot_general x24, matrix products, head_terms(): row_part = jnp.dot(grads, s_keys, preferred_element_type=jnp.float32)  9.46 us
    dot_general x24, matrix products, head_terms(): lax.dot_general(t_rows, t_keys, inner, preferred_element_type=jnp.float32)  9.02 us
    dot_general x24, matrix products, head_terms(): lax.dot_general(s_rows, s_keys, inner, preferred_element_type=jnp.float32)  7.99 us
    unnamed x28, local copies, waits for them, and re-layouts  7.3 us
    dot_general x24, matrix products, head_terms(): lax.dot_general(grads, s_rows, (((0,), (0,)), ((), ())), preferred_elemen...  5.65 us
  transfers between devices with their start and end apart: 6, of which 3 were waited for; matrix products, arithmetic and copies ran while one was open for 2% of the time, Pallas kernels for 0%

commit v1 on v0

v1 whole, which is shorter than its diff:
```python
import functools
import math

import jax
import jax.numpy as jnp
from jax import lax
from jax.experimental import pallas as pl
from jax.experimental.pallas import tpu as pltpu
from jax.sharding import Mesh
from jax.sharding import PartitionSpec as P

H = 32
DT = 160
DS = 48
SPAN = 384

BLOCK = 128
OWN = 2 * BLOCK
HALO = 192
WINDOW = OWN + 2 * HALO
FIRST_QUERY = WINDOW - OWN
HEADS = 4
TW = HEADS * DT
SW = HEADS * DS
SP = 256
REL = TW + SP
CT = DT ** (-0.5) * math.log2(math.e)
CS = DS ** (-0.5) * math.log2(math.e)
NT = (((1,), (1,)), ((), ()))
VMEM = pl.BlockSpec(memory_space=pltpu.VMEM)
SMEM = pl.BlockSpec(memory_space=pltpu.SMEM)
F32 = jnp.float32
BF16 = jnp.bfloat16


def call(kernel, out_shape, n_smem, n_vmem, scratch=(), flops=0, moved=0, exps=0):
    return pl.pallas_call(
        kernel,
        out_shape=out_shape,
        in_specs=[SMEM] * n_smem + [VMEM] * n_vmem,
        out_specs=jax.tree.map(lambda _: VMEM, out_shape),
        scratch_shapes=list(scratch),
        compiler_params=pltpu.CompilerParams(vmem_limit_bytes=40 * 1024 * 1024),
        cost_estimate=pl.CostEstimate(flops=flops, bytes_accessed=moved, transcendentals=exps),
    )


def split_kernel(core, tq, tk, tv, sq, sk, sv, send_first, send_rest, keep):
    me = core[0]
    lane = lax.broadcasted_iota(jnp.int32, (BLOCK, SP), 1)
    for rel, (teacher, student) in enumerate(((tq, sq), (tk, sk), (tv, sv))):
        send, at = (send_first, 0) if rel == 0 else (send_rest, (rel - 1) * REL)
        mine = pl.ds(pl.multiple_of(me * TW, 128), TW)
        other = pl.ds(pl.multiple_of((1 - me) * TW, 128), TW)
        keep[:, rel * REL : rel * REL + TW] = teacher[:, mine]
        send[:, at : at + TW] = teacher[:, other]
        low = jnp.where(lane < SW, student[:, :SP].astype(F32), 0.0)
        high = pltpu.roll(student[:, 128:].astype(F32), SP - (SW - 128), 1)
        high = jnp.where(lane < SW, high, 0.0)
        keep[:, rel * REL + TW : (rel + 1) * REL] = jnp.where(me == 0, low, high).astype(BF16)
        send[:, at + TW : at + REL] = jnp.where(me == 0, high, low).astype(BF16)


def edges_kernel(rels, keep_at, core, keep, recv, *outs):
    half = HALO - BLOCK
    for slot in range(rels):
        after, before = outs[2 * slot], outs[2 * slot + 1]
        ours = slice(keep_at + slot * REL, keep_at + (slot + 1) * REL)
        theirs = slice(slot * REL, (slot + 1) * REL)

        def write(first, first_at, second, second_at):
            after[:half, :] = first[BLOCK - half :, first_at]
            after[half:, :] = second[:, second_at]
            before[:BLOCK, :] = first[:, first_at]
            before[BLOCK:, :] = second[:half, second_at]

        @pl.when(core[0] == 0)
        def _():
            write(keep, ours, recv, theirs)

        @pl.when(core[0] != 0)
        def _():
            write(recv, theirs, keep, ours)


def fold(value, op):
    rows, lanes = value.shape
    return op(value.reshape(rows // 8, 8, lanes), axis=0)


def relation_kernel(
    keep_at,
    recv_at,
    core,
    starts,
    weights,
    loss_in,
    left,
    keep,
    recv,
    right,
    grad_left,
    grad_own,
    grad_right,
    loss_out,
    win,
    bias,
    rt,
    rs,
    gt,
    qs,
    bt,
):
    me = core[0]
    win[:HALO, :] = left[...]
    win[pl.ds(pl.multiple_of(HALO + me * BLOCK, 64), BLOCK), :] = keep[:, keep_at : keep_at + REL]
    win[pl.ds(pl.multiple_of(HALO + (1 - me) * BLOCK, 64), BLOCK), :] = recv[
        :, recv_at : recv_at + REL
    ]
    win[HALO + OWN :, :] = right[...]

    key = lax.broadcasted_iota(jnp.int32, (WINDOW, OWN), 0)
    query = lax.broadcasted_iota(jnp.int32, (WINDOW, OWN), 1) + FIRST_QUERY
    bias[...] = jnp.where((key >= starts[...]) & (key <= query), 0.0, -1e30)

    lane = lax.broadcasted_iota(jnp.int32, (OWN, SP), 1)
    student = slice(TW, REL)
    row = lax.broadcasted_iota(jnp.int32, (SP, SP), 0)
    col = lax.broadcasted_iota(jnp.int32, (SP, SP), 1)
    unit = jnp.where(row == col, 1.0, 0.0).astype(BF16)
    bt[...] = lax.dot_general(unit, win[:, student], NT, preferred_element_type=F32).astype(BF16)

    gt[:BLOCK, :] = jnp.zeros((BLOCK, HEADS * OWN), BF16)
    gt[WINDOW - BLOCK :, :] = jnp.zeros((BLOCK, HEADS * OWN), BF16)
    total = jnp.zeros((1, BLOCK), F32)
    step = 64
    for head in range(HEADS):
        start = head * DT // 128 * 128
        inside = (lane >= head * DT - start) & (lane < (head + 1) * DT - start)
        t_cols = slice(start, start + 256)
        t_query = win[FIRST_QUERY:, t_cols] * jnp.where(inside, 1.0, 0.0).astype(BF16)
        inside = (lane >= head * DS) & (lane < (head + 1) * DS)
        s_query = win[FIRST_QUERY:, student] * jnp.where(inside, 1.0, 0.0).astype(BF16)
        qs[head * OWN : (head + 1) * OWN, :] = s_query
        rt[...] = (
            lax.dot_general(win[:, t_cols], t_query, NT, preferred_element_type=F32) + bias[...]
        )
        rs[...] = (
            lax.dot_general(win[:, student], s_query, NT, preferred_element_type=F32) + bias[...]
        )
        for tile in range(2):
            first = tile * BLOCK
            lanes = slice(tile * BLOCK, (tile + 1) * BLOCK)
            parts = [slice(first + at, first + at + step) for at in range(0, SPAN + BLOCK, step)]
            top_t = fold(rt[parts[0], lanes], jnp.max)
            top_s = fold(rs[parts[0], lanes], jnp.max)
            for part in parts[1:]:
                top_t = jnp.maximum(top_t, fold(rt[part, lanes], jnp.max))
                top_s = jnp.maximum(top_s, fold(rs[part, lanes], jnp.max))
            top_t = jnp.max(top_t, axis=0, keepdims=True) * CT
            top_s = jnp.max(top_s, axis=0, keepdims=True) * CS
            sum_t = jnp.zeros((8, BLOCK), F32)
            sum_s = jnp.zeros((8, BLOCK), F32)
            cross = jnp.zeros((8, BLOCK), F32)
            for part in parts:
                ut = rt[part, lanes] * CT - top_t
                us = rs[part, lanes] * CS - top_s
                et = jnp.exp2(ut)
                es = jnp.exp2(us)
                sum_t = sum_t + fold(et, jnp.sum)
                sum_s = sum_s + fold(es, jnp.sum)
                cross = cross + fold(et * (ut - us), jnp.sum)
                rt[part, lanes] = et
                rs[part, lanes] = es
            sum_t = jnp.sum(sum_t, axis=0, keepdims=True)
            sum_s = jnp.sum(sum_s, axis=0, keepdims=True)
            cross = jnp.sum(cross, axis=0, keepdims=True)
            weight = weights[:, lanes]
            total = total + weight * (cross / sum_t - jnp.log2(sum_t) + jnp.log2(sum_s))
            scale_t = weight * DS ** (-0.5) / sum_t
            scale_s = weight * DS ** (-0.5) / sum_s
            g_cols = slice(head * OWN + tile * BLOCK, head * OWN + (tile + 1) * BLOCK)
            for part in parts:
                gt[part, g_cols] = (rs[part, lanes] * scale_s - rt[part, lanes] * scale_t).astype(
                    BF16
                )

    loss_out[...] = loss_in[...] + total * math.log(2.0)
    key_grad = jnp.dot(gt[...], qs[...], preferred_element_type=F32)
    row_grads = [
        jnp.dot(
            bt[head * DS : (head + 1) * DS, :],
            gt[:, head * OWN : (head + 1) * OWN],
            preferred_element_type=F32,
        )
        for head in range(HEADS)
    ]
    row_grads.append(jnp.zeros((SP - SW, OWN), F32))
    row_grad = jnp.concatenate(row_grads, axis=0).T
    late = HALO + OWN - FIRST_QUERY
    grad_left[...] = key_grad[:HALO].astype(BF16)
    grad_own[: OWN - late, :] = key_grad[HALO:FIRST_QUERY]
    grad_own[OWN - late :, :] = key_grad[FIRST_QUERY : HALO + OWN] + row_grad[:late]
    grad_right[...] = (key_grad[HALO + OWN :] + row_grad[late:]).astype(BF16)


def join_kernel(loss, l0, l1, l2, r0, r1, r2, to_before, to_after, copies):
    copies[...] = jnp.broadcast_to(loss[...], copies.shape)
    for rel, (left, right) in enumerate(((l0, r0), (l1, r1), (l2, r2))):
        to_before[:, rel * SP : (rel + 1) * SP] = left[...]
        to_after[:, rel * SP : (rel + 1) * SP] = right[...]


def merge_kernel(core, losses, o0, o1, o2, from_after, from_before, keep, send, copies, acc):
    me = core[0]
    copies[...] = jnp.broadcast_to(jnp.sum(losses[...], axis=0, keepdims=True), copies.shape)
    for rel, own in enumerate((o0, o1, o2)):
        acc[:, rel * SP : (rel + 1) * SP] = own[...]
    acc[OWN - HALO :, :] = acc[OWN - HALO :, :] + from_after[...].astype(F32)
    acc[:HALO, :] = acc[:HALO, :] + from_before[...].astype(F32)
    keep[...] = acc[pl.ds(pl.multiple_of(me * BLOCK, 128), BLOCK), :]
    send[...] = acc[pl.ds(pl.multiple_of((1 - me) * BLOCK, 128), BLOCK), :]


def place_kernel(tokens, core, losses, keep, recv, oq, ok, ov, loss):
    me = core[0]
    total = jnp.sum(jnp.sum(losses[...], axis=0, keepdims=True), axis=1, keepdims=True)
    loss[...] = total * (1.0 / (3 * H * tokens))
    empty = jnp.zeros((BLOCK, 2 * SW - SP), F32)
    for rel, out in enumerate((oq, ok, ov)):
        ours = jnp.concatenate([keep[:, rel * SP : (rel + 1) * SP], empty], axis=1)
        theirs = jnp.concatenate([recv[:, rel * SP : (rel + 1) * SP], empty], axis=1)
        low = jnp.where(me == 0, ours, theirs)
        high = jnp.where(me == 0, theirs, ours)
        out[...] = low + pltpu.roll(high, SW, 1)


def shape(rows, cols, dtype):
    return jax.ShapeDtypeStruct((rows, cols), dtype)


def body(teacher_q, teacher_k, teacher_v, student_q, student_k, student_v, doc_ids, row_weight):
    tok = ("y", "z", "core")
    count = lax.axis_size("y") * lax.axis_size("z") * 2
    core = lax.axis_index("core").astype(jnp.int32).reshape(1)
    chip = lax.axis_index("y") * lax.axis_size("z") + lax.axis_index("z")

    def other_core(value):
        return lax.ppermute(value, "core", [(0, 1), (1, 0)])

    def next_chip(value, chips):
        step = 2 * chips
        return lax.ppermute(value, tok, [(i, (i + step) % count) for i in range(count)])

    packed = [shape(BLOCK, n * REL, BF16) for n in (1, 2, 3)]
    send_first, send_rest, keep = call(split_kernel, packed, 1, 6, moved=4 << 20)(
        core, teacher_q, teacher_k, teacher_v, student_q, student_k, student_v
    )
    recv_first = other_core(send_first)
    recv_rest = other_core(send_rest)
    edge = shape(HALO, REL, BF16)
    edges = list(
        call(functools.partial(edges_kernel, 1, 0), [edge] * 2, 1, 2, moved=1 << 20)(
            core, keep, recv_first
        )
    )
    edges += call(functools.partial(edges_kernel, 2, REL), [edge] * 4, 1, 2, moved=2 << 20)(
        core, keep, recv_rest
    )
    lefts = [next_chip(edges[2 * rel], 1) for rel in range(3)]
    rights = [next_chip(edges[2 * rel + 1], -1) for rel in range(3)]

    doc_ids, row_weight, _ = lax.optimization_barrier((doc_ids, row_weight, edges[0]))
    far = 1 << 20
    docs = jnp.concatenate([doc_ids[-HALO:] - far, doc_ids, doc_ids[:HALO] + far])
    docs = lax.dynamic_slice_in_dim(docs, chip * OWN, WINDOW)
    weight = jnp.concatenate([row_weight, row_weight[:HALO]])
    weight = lax.dynamic_slice_in_dim(weight, chip * OWN + HALO, OWN)[None, :]
    starts = jnp.sum(docs[:, None] < docs[None, FIRST_QUERY:], axis=0, dtype=jnp.int32)[None, :]

    loss = jnp.zeros((1, BLOCK), F32)
    grads = []
    for rel in range(3):
        recv, recv_at = (recv_first, 0) if rel == 0 else (recv_rest, (rel - 1) * REL)
        out = call(
            functools.partial(relation_kernel, rel * REL, recv_at),
            [
                shape(HALO, SP, BF16),
                shape(OWN, SP, F32),
                shape(HALO, SP, BF16),
                shape(1, BLOCK, F32),
            ],
            1,
            7,
            scratch=[
                pltpu.VMEM((WINDOW, REL), BF16),
                pltpu.VMEM((WINDOW, OWN), F32),
                pltpu.VMEM((WINDOW, OWN), F32),
                pltpu.VMEM((WINDOW, OWN), F32),
                pltpu.VMEM((WINDOW, HEADS * OWN), BF16),
                pltpu.VMEM((HEADS * OWN, SP), BF16),
                pltpu.VMEM((SP, WINDOW), BF16),
            ],
            flops=2 * 16 * WINDOW * OWN * 256,
            moved=2 << 20,
            exps=2 * HEADS * WINDOW * OWN,
        )(core, starts, weight, loss, lefts[rel], keep, recv, rights[rel])
        grads.append(out[:3])
        loss = out[3]

    stages = (("z", "core"), ("y", "head"))
    copies = [shape(lax.axis_size(axes), BLOCK, F32) for axes in stages]

    def exchange(value, axes):
        return lax.all_to_all(value, axes, 0, 0, tiled=True)

    returned = shape(HALO, 3 * SP, BF16)
    to_before, to_after, partial = call(
        join_kernel, [returned] * 2 + [copies[0]], 0, 7, moved=1 << 20
    )(loss, *(g[0] for g in grads), *(g[2] for g in grads))
    from_after = next_chip(to_before, -1)
    from_before = next_chip(to_after, 1)
    partial = exchange(partial, stages[0])

    third = shape(BLOCK, 3 * SP, F32)
    kept, sent, partial = call(
        merge_kernel,
        [third] * 2 + [copies[1]],
        1,
        6,
        scratch=[pltpu.VMEM((OWN, 3 * SP), F32)],
        moved=2 << 20,
    )(core, partial, *(g[1] for g in grads), from_after, from_before)
    received = other_core(sent)
    partial = exchange(partial, stages[1])
    out = shape(BLOCK, 2 * SW, F32)
    grad_q, grad_k, grad_v, loss = call(
        functools.partial(place_kernel, doc_ids.shape[0]),
        [out] * 3 + [shape(1, 1, F32)],
        1,
        3,
        moved=1 << 20,
    )(core, partial, kept, received)
    return grad_q, grad_k, grad_v, loss[0, 0]


def solution(mesh):
    tok, head = mesh.devices.shape
    y = 8 if tok == 128 else 2
    fine = Mesh(mesh.devices.reshape(y, tok // (2 * y), 2, head), ("y", "z", "core", "head"))
    rows = ("y", "z", "core")
    placed = (P(rows, "head"),) * 6 + (P(), P())
    return jax.shard_map(
        body,
        mesh=fine,
        in_specs=placed,
        out_specs=(P(rows, "head"),) * 3 + (P(),),
        check_vma=False,
    )
```

time: 278 us -> 98.7 us (0.36)
  blocking collectives: 124 us -> 28.7 us
  waiting for transfers between devices: 59.1 us -> 1.47 us
  matrix products: 32.1 us -> 0 us
  starting transfers between devices: 19 us -> 49.4 us
  between operations: 18.1 us -> 0.89 us
  other arithmetic: 16.8 us -> 0.32 us
  Pallas kernels: 0 us -> 11.4 us
    psum x1 -> x0, blocking collectives: 124 us -> none  [body(): whole = lax.psum(total, ('tok', 'head'))]
    ppermute x6 -> x11, waiting for transfers between devices: 59.1 us -> 1.47 us  [the longest x3 1.45 us: other_core(): return lax.ppermute(value, 'core', [(0, 1), (1, 0)])]
    dot_general x96 -> x0, matrix products: 32.1 us -> none  [the longest x24 9.46 us: head_terms(): row_part = jnp.dot(grads, s_keys, preferred_element_type=jnp.float32)]
    ppermute x6 -> x11, starting transfers between devices: 19 us -> 49.4 us  [the longest x8 36 us: next_chip(): lax.ppermute(value, tok, [(i, (i + step) % count) for i in range(count)])]
    all_to_all x0 -> x2, blocking collectives: none -> 28.7 us  [exchange(): return lax.all_to_all(value, axes, 0, 0, tiled=True)]
    pallas_call x0 -> x9, Pallas kernels: none -> 11.4 us  [the longest x3 9.82 us: body(): call(functools.partial(relation_kernel, rel * REL, recv_at), [shape(HALO,...]
    reduce_sum x52 -> x1, other arithmetic: 8.56 us -> 0.17 us  [body(): jnp.sum(docs[:, None] < docs[None, FIRST_QUERY:], axis=0, dtype=jnp.int32)]
    unnamed x28 -> x16, local copies, waits for them, and re-layouts: 7.3 us -> 5.59 us
  transfers between devices with their start and end apart: 6 -> 11, of which waited for: 3 -> 1; matrix products, arithmetic and copies ran while one was open for 2% -> 1% of each run, Pallas kernels for 0% -> 7%
where the time goes in v1:
time: 98.7 us; the launch traced here: 98 us
  starting transfers between devices  49.4 us (50%)
  blocking collectives  28.7 us (29%)
  Pallas kernels  11.4 us (12%)
  local copies, waits for them, and re-layouts  5.79 us (6%)
  waiting for transfers between devices  1.47 us (1%)
    ppermute x8, starting transfers between devices, next_chip(): lax.ppermute(value, tok, [(i, (i + step) % count) for i in range(count)])  36 us
    all_to_all x2, blocking collectives, exchange(): return lax.all_to_all(value, axes, 0, 0, tiled=True)  28.7 us
    ppermute x3, starting transfers between devices, other_core(): return lax.ppermute(value, 'core', [(0, 1), (1, 0)])  13.4 us
    pallas_call x3, Pallas kernels, body(): call(functools.partial(relation_kernel, rel * REL, recv_at), [shape(HALO,...  9.82 us
    unnamed x16, local copies, waits for them, and re-layouts  5.59 us
  transfers between devices with their start and end apart: 11, of which 1 were waited for; matrix products, arithmetic and copies ran while one was open for 1% of the time, Pallas kernels for 7%

profile of v1, /device:TPU:1, one launch (start us, length us, event | category | flops | bytes accessed | tf_op | source)
XLA Modules:
  0.0 98.0 jit_solution(847699504611844722)
XLA Ops:
  0.6 1.0 copy-done
  1.6 1.0 copy-done.1
  2.6 1.0 copy-done.2
  3.6 0.9 copy-done.3
  4.5 0.9 copy-done.4
  5.3 0.9 copy-done.5
  6.2 0.2 shard_map.111
  6.4 8.8 %collective-permute-start.3 = (bf16[128,1792]{1,0:T(8,128)(2,1)S(1)}, bf16[128,1792]{1,0:T(8,128)(2,1)S(1)}, u32[]{:S(2)}, u32[]{:S(2)}) collective-permute-start(bf16[128,1792]{1,0:T(8,128)(2,1)S(1)} %get-tuple-element.44), channel_id=1, source_target_pairs={{0,4},{4,0},{1,5},{5,1},{2,6},{6,2},{3,7},{7,3},{8,12},{12,8},{9,1... | collective-permute-start | bytes 1376264 | tf_op jit(solution)/shard_map/ppermute | solution.py:249
  15.2 1.9 %collective-permute-start = (bf16[128,896]{1,0:T(8,128)(2,1)S(1)}, bf16[128,896]{1,0:T(8,128)(2,1)S(1)}, u32[]{:S(2)}, u32[]{:S(2)}) collective-permute-start(bf16[128,896]{1,0:T(8,128)(2,1)S(1)} %get-tuple-element.38), channel_id=1, source_target_pairs={{0,4},{4,0},{1,5},{5,1},{2,6},{6,2},{3,7},{7,3},{8,12},{12,8},{9,1... | collective-permute-start | bytes 688136 | tf_op jit(solution)/shard_map/ppermute | solution.py:249
  17.2 1.4 %collective-permute-done.recv = bf16[128,896]{1,0:T(8,128)(2,1)S(1)} collective-permute-done((bf16[128,896]{1,0:T(8,128)(2,1)S(1)}, bf16[128,896]{1,0:T(8,128)(2,1)S(1)}, u32[]{:S(2)}, u32[]{:S(2)}) %collective-permute-start) | collective-permute-done | bytes 229408 | tf_op jit(solution)/shard_map/ppermute | solution.py:249
  18.7 1.9 %collective-permute-start.1 = (bf16[192,896]{1,0:T(8,128)(2,1)S(1)}, bf16[192,896]{1,0:T(8,128)(2,1)S(1)}, u32[]{:S(2)}, u32[]{:S(2)}) collective-permute-start(bf16[192,896]{1,0:T(8,128)(2,1)S(1)} %get-tuple-element.39), channel_id=1, source_target_pairs={{0,8},{4,12},{8,16},{12,20},{16,24},{20,28},{24,32},{28,36},{32,40... | collective-permute-start | bytes 1032200 | tf_op jit(solution)/shard_map/ppermute | solution.py:253
  20.6 8.2 %collective-permute-start.2 = (bf16[192,896]{1,0:T(8,128)(2,1)S(1)}, bf16[192,896]{1,0:T(8,128)(2,1)S(1)}, u32[]{:S(2)}, u32[]{:S(2)}) collective-permute-start(bf16[192,896]{1,0:T(8,128)(2,1)S(1)} %get-tuple-element.42), channel_id=1, source_target_pairs={{0,504},{4,508},{8,0},{12,4},{16,8},{20,12},{24,16},{28,20},{32,24... | collective-permute-start | bytes 1032200 | tf_op jit(solution)/shard_map/ppermute | solution.py:253
  28.8 0.1 slice_add_fusion
  28.9 0.1 concatenate.6
  29.0 0.1 dynamic_slice.6
  29.1 0.1 shard_map.114
  29.2 1.9 %collective-permute-start.4 = (bf16[192,896]{1,0:T(8,128)(2,1)S(1)}, bf16[192,896]{1,0:T(8,128)(2,1)S(1)}, u32[]{:S(2)}, u32[]{:S(2)}) collective-permute-start(bf16[192,896]{1,0:T(8,128)(2,1)S(1)} %get-tuple-element.45), channel_id=1, source_target_pairs={{0,8},{4,12},{8,16},{12,20},{16,24},{20,28},{24,32},{28,36},{32,40... | collective-permute-start | bytes 1032200 | tf_op jit(solution)/shard_map/ppermute | solution.py:253
  31.1 6.7 %collective-permute-start.5 = (bf16[192,896]{1,0:T(8,128)(2,1)S(1)}, bf16[192,896]{1,0:T(8,128)(2,1)S(1)}, u32[]{:S(2)}, u32[]{:S(2)}) collective-permute-start(bf16[192,896]{1,0:T(8,128)(2,1)S(1)} %get-tuple-element.46), channel_id=1, source_target_pairs={{0,504},{4,508},{8,0},{12,4},{16,8},{20,12},{24,16},{28,20},{32,24... | collective-permute-start | bytes 1032200 | tf_op jit(solution)/shard_map/ppermute | solution.py:253
  37.8 0.2 convert_reduce_fusion
  38.0 1.9 %collective-permute-start.6 = (bf16[192,896]{1,0:T(8,128)(2,1)S(1)}, bf16[192,896]{1,0:T(8,128)(2,1)S(1)}, u32[]{:S(2)}, u32[]{:S(2)}) collective-permute-start(bf16[192,896]{1,0:T(8,128)(2,1)S(1)} %get-tuple-element.48), channel_id=1, source_target_pairs={{0,8},{4,12},{8,16},{12,20},{16,24},{20,28},{24,32},{28,36},{32,40... | collective-permute-start | bytes 1032200 | tf_op jit(solution)/shard_map/ppermute | solution.py:253
  40.0 6.7 %collective-permute-start.7 = (bf16[192,896]{1,0:T(8,128)(2,1)S(1)}, bf16[192,896]{1,0:T(8,128)(2,1)S(1)}, u32[]{:S(2)}, u32[]{:S(2)}) collective-permute-start(bf16[192,896]{1,0:T(8,128)(2,1)S(1)} %get-tuple-element.49), channel_id=1, source_target_pairs={{0,504},{4,508},{8,0},{12,4},{16,8},{20,12},{24,16},{28,20},{32,24... | collective-permute-start | bytes 1032200 | tf_op jit(solution)/shard_map/ppermute | solution.py:253
  46.7 0.1 fusion
  46.8 3.3 %shard_map.113 = (bf16[192,256]{1,0:T(8,128)(2,1)S(1)}, f32[256,256]{1,0:T(8,128)S(1)}, bf16[192,256]{1,0:T(8,128)(2,1)S(1)}, f32[1,128]{1,0:T(1,128)S(1)}) custom-call(s32[1]{0:T(128)} %bitcast.core, s32[1,256]{1,0:T(1,128)S(1)} %bitcast.19, f32[1,256]{1,0:T(1,128)S(1)} %bitcast.16, f32[1,128]{1,0:T(1,128)S(1)} %broadcast_in_dim.13.loss_in, ...), custom_call_target="tpu_custom_call" | custom-call | flops 1342177280 | bytes 2097152 | tf_op jit(solution)/shard_map/pallas_call | solution.py:285
  50.1 3.3 %shard_map.115 = (bf16[192,256]{1,0:T(8,128)(2,1)S(1)}, f32[256,256]{1,0:T(8,128)S(1)}, bf16[192,256]{1,0:T(8,128)(2,1)S(1)}, f32[1,128]{1,0:T(1,128)S(1)}) custom-call(s32[1]{0:T(128)} %bitcast.core, s32[1,256]{1,0:T(1,128)S(1)} %bitcast.20, f32[1,256]{1,0:T(1,128)S(1)} %bitcast.17, f32[1,128]{1,0:T(1,128)S(1)} %get-tuple-element.43.loss_in, ...), custom_call_target="tpu_custom_call" | custom-call | flops 1342177280 | bytes 2097152 | tf_op jit(solution)/shard_map/pallas_call | solution.py:285
  53.4 3.3 %shard_map.116 = (bf16[192,256]{1,0:T(8,128)(2,1)S(1)}, f32[256,256]{1,0:T(8,128)S(1)}, bf16[192,256]{1,0:T(8,128)(2,1)S(1)}, f32[1,128]{1,0:T(1,128)S(1)}) custom-call(s32[1]{0:T(128)} %bitcast.core, s32[1,256]{1,0:T(1,128)S(1)} %bitcast.21, f32[1,256]{1,0:T(1,128)S(1)} %bitcast.18, f32[1,128]{1,0:T(1,128)S(1)} %get-tuple-element.47.loss_in, ...), custom_call_target="tpu_custom_call" | custom-call | flops 1342177280 | bytes 2097152 | tf_op jit(solution)/shard_map/pallas_call | solution.py:285
  56.7 6.8 %collective-permute-start.8 = (bf16[192,768]{1,0:T(8,128)(2,1)S(1)}, bf16[192,768]{1,0:T(8,128)(2,1)S(1)}, u32[]{:S(2)}, u32[]{:S(2)}) collective-permute-start(bf16[192,768]{1,0:T(8,128)(2,1)S(1)} %get-tuple-element.61), channel_id=1, source_target_pairs={{0,504},{4,508},{8,0},{12,4},{16,8},{20,12},{24,16},{28,20},{32,24... | collective-permute-start | bytes 884744 | tf_op jit(solution)/shard_map/ppermute | solution.py:253
  63.5 1.9 %collective-permute-start.9 = (bf16[192,768]{1,0:T(8,128)(2,1)S(1)}, bf16[192,768]{1,0:T(8,128)(2,1)S(1)}, u32[]{:S(2)}, u32[]{:S(2)}) collective-permute-start(bf16[192,768]{1,0:T(8,128)(2,1)S(1)} %get-tuple-element.62), channel_id=1, source_target_pairs={{0,8},{4,12},{8,16},{12,20},{16,24},{20,28},{24,32},{28,36},{32,40... | collective-permute-start | bytes 884744 | tf_op jit(solution)/shard_map/ppermute | solution.py:253
  65.4 12.1 %all_to_all.22 = f32[16,1,128]{2,1,0:T(1,128)S(1)} all-to-all(f32[16,1,128]{2,1,0:T(1,128)S(1)} %bitcast.15), channel_id=1, replica_groups=mesh['y'=8,'z'=8,'core'=2,'head'=4] {'z','core'}, dimensions={0} | all-to-all | bytes 16384 | tf_op jit(solution)/shard_map/all_to_all | solution.py:315
  77.4 0.2 shard_map.118
  77.7 2.7 %collective-permute-start.10 = (f32[128,768]{1,0:T(8,128)S(1)}, f32[128,768]{1,0:T(8,128)S(1)}, u32[]{:S(2)}, u32[]{:S(2)}) collective-permute-start(f32[128,768]{1,0:T(8,128)S(1)} %get-tuple-element.65), channel_id=1, source_target_pairs={{0,4},{4,0},{1,5},{5,1},{2,6},{6,2},{3,7},{7,3},{8,12},{12,8},{9,1... | collective-permute-start | bytes 1179656 | tf_op jit(solution)/shard_map/ppermute | solution.py:249
  80.4 16.6 %all_to_all.23 = f32[32,1,128]{2,1,0:T(1,128)S(1)} all-to-all(f32[32,1,128]{2,1,0:T(1,128)S(1)} %bitcast.14), channel_id=1, replica_groups=mesh['y'=8,'z'=8,'core'=2,'head'=4] {'y','head'}, dimensions={0} | all-to-all | bytes 32768 | tf_op jit(solution)/shard_map/all_to_all | solution.py:315
  97.0 1.0 shard_map.119
  (26 shorter events, 0.2 us)
Async XLA Ops:
  0.6 1.0 copy-start
  1.6 1.0 copy-start.1
  2.6 1.0 copy-start.2
  3.6 0.9 copy-start.3
  4.5 0.9 copy-start.4
  5.3 0.9 copy-start.5
  6.4 22.7 %collective-permute-start.3 = (bf16[128,1792]{1,0:T(8,128)(2,1)S(1)}, bf16[128,1792]{1,0:T(8,128)(2,1)S(1)}, u32[]{:S(2)}, u32[]{:S(2)}) collective-permute-start(bf16[128,1792]{1,0:T(8,128)(2,1)S(1)} %get-tuple-element.44), channel_id=1, source_target_pairs={{0,4},{4,0},{1,5},{5,1},{2,6},{6,2},{3,7},{7,3},{8,12},{12,8},{9,1... | collective-permute-start | bytes 1376264 | tf_op jit(solution)/shard_map/ppermute | solution.py:249
  15.2 3.4 %collective-permute-start = (bf16[128,896]{1,0:T(8,128)(2,1)S(1)}, bf16[128,896]{1,0:T(8,128)(2,1)S(1)}, u32[]{:S(2)}, u32[]{:S(2)}) collective-permute-start(bf16[128,896]{1,0:T(8,128)(2,1)S(1)} %get-tuple-element.38), channel_id=1, source_target_pairs={{0,4},{4,0},{1,5},{5,1},{2,6},{6,2},{3,7},{7,3},{8,12},{12,8},{9,1... | collective-permute-start | bytes 688136 | tf_op jit(solution)/shard_map/ppermute | solution.py:249
  18.6 10.2 %copy-start.6 = (s32[16384]{0:T(1024)S(1)}, s32[16384]{0:T(1024)}, u32[]{:S(2)}) copy-start(s32[16384]{0:T(1024)} %param.14) | copy-start | bytes 196612
  18.7 28.1 %collective-permute-start.1 = (bf16[192,896]{1,0:T(8,128)(2,1)S(1)}, bf16[192,896]{1,0:T(8,128)(2,1)S(1)}, u32[]{:S(2)}, u32[]{:S(2)}) collective-permute-start(bf16[192,896]{1,0:T(8,128)(2,1)S(1)} %get-tuple-element.39), channel_id=1, source_target_pairs={{0,8},{4,12},{8,16},{12,20},{16,24},{20,28},{24,32},{28,36},{32,40... | collective-permute-start | bytes 1032200 | tf_op jit(solution)/shard_map/ppermute | solution.py:253
  20.6 19.4 %collective-permute-start.2 = (bf16[192,896]{1,0:T(8,128)(2,1)S(1)}, bf16[192,896]{1,0:T(8,128)(2,1)S(1)}, u32[]{:S(2)}, u32[]{:S(2)}) collective-permute-start(bf16[192,896]{1,0:T(8,128)(2,1)S(1)} %get-tuple-element.42), channel_id=1, source_target_pairs={{0,504},{4,508},{8,0},{12,4},{16,8},{20,12},{24,16},{28,20},{32,24... | collective-permute-start | bytes 1032200 | tf_op jit(solution)/shard_map/ppermute | solution.py:253
  29.1 17.6 %copy-start.7 = (f32[16384]{0:T(1024)S(1)}, f32[16384]{0:T(1024)}, u32[]{:S(2)}) copy-start(f32[16384]{0:T(1024)} %param.15) | copy-start | bytes 196612
  29.2 20.8 %collective-permute-start.4 = (bf16[192,896]{1,0:T(8,128)(2,1)S(1)}, bf16[192,896]{1,0:T(8,128)(2,1)S(1)}, u32[]{:S(2)}, u32[]{:S(2)}) collective-permute-start(bf16[192,896]{1,0:T(8,128)(2,1)S(1)} %get-tuple-element.45), channel_id=1, source_target_pairs={{0,8},{4,12},{8,16},{12,20},{16,24},{20,28},{24,32},{28,36},{32,40... | collective-permute-start | bytes 1032200 | tf_op jit(solution)/shard_map/ppermute | solution.py:253
  31.1 18.9 %collective-permute-start.5 = (bf16[192,896]{1,0:T(8,128)(2,1)S(1)}, bf16[192,896]{1,0:T(8,128)(2,1)S(1)}, u32[]{:S(2)}, u32[]{:S(2)}) collective-permute-start(bf16[192,896]{1,0:T(8,128)(2,1)S(1)} %get-tuple-element.46), channel_id=1, source_target_pairs={{0,504},{4,508},{8,0},{12,4},{16,8},{20,12},{24,16},{28,20},{32,24... | collective-permute-start | bytes 1032200 | tf_op jit(solution)/shard_map/ppermute | solution.py:253
  38.0 8.7 %slice-start = ((f32[16384]{0:T(1024)}), f32[192]{0:T(256)S(1)}, s32[]{:S(2)}) async-start(f32[16384]{0:T(1024)} %param.15), calls=%async_computation.2 | async-start | bytes 2048 | tf_op jit(solution)/shard_map/slice | solution.py:277
  38.0 15.3 %collective-permute-start.6 = (bf16[192,896]{1,0:T(8,128)(2,1)S(1)}, bf16[192,896]{1,0:T(8,128)(2,1)S(1)}, u32[]{:S(2)}, u32[]{:S(2)}) collective-permute-start(bf16[192,896]{1,0:T(8,128)(2,1)S(1)} %get-tuple-element.48), channel_id=1, source_target_pairs={{0,8},{4,12},{8,16},{12,20},{16,24},{20,28},{24,32},{28,36},{32,40... | collective-permute-start | bytes 1032200 | tf_op jit(solution)/shard_map/ppermute | solution.py:253
  40.0 13.4 %collective-permute-start.7 = (bf16[192,896]{1,0:T(8,128)(2,1)S(1)}, bf16[192,896]{1,0:T(8,128)(2,1)S(1)}, u32[]{:S(2)}, u32[]{:S(2)}) collective-permute-start(bf16[192,896]{1,0:T(8,128)(2,1)S(1)} %get-tuple-element.49), channel_id=1, source_target_pairs={{0,504},{4,508},{8,0},{12,4},{16,8},{20,12},{24,16},{28,20},{32,24... | collective-permute-start | bytes 1032200 | tf_op jit(solution)/shard_map/ppermute | solution.py:253
  56.7 20.8 %collective-permute-start.8 = (bf16[192,768]{1,0:T(8,128)(2,1)S(1)}, bf16[192,768]{1,0:T(8,128)(2,1)S(1)}, u32[]{:S(2)}, u32[]{:S(2)}) collective-permute-start(bf16[192,768]{1,0:T(8,128)(2,1)S(1)} %get-tuple-element.61), channel_id=1, source_target_pairs={{0,504},{4,508},{8,0},{12,4},{16,8},{20,12},{24,16},{28,20},{32,24... | collective-permute-start | bytes 884744 | tf_op jit(solution)/shard_map/ppermute | solution.py:253
  63.5 14.0 %collective-permute-start.9 = (bf16[192,768]{1,0:T(8,128)(2,1)S(1)}, bf16[192,768]{1,0:T(8,128)(2,1)S(1)}, u32[]{:S(2)}, u32[]{:S(2)}) collective-permute-start(bf16[192,768]{1,0:T(8,128)(2,1)S(1)} %get-tuple-element.62), channel_id=1, source_target_pairs={{0,8},{4,12},{8,16},{12,20},{16,24},{20,28},{24,32},{28,36},{32,40... | collective-permute-start | bytes 884744 | tf_op jit(solution)/shard_map/ppermute | solution.py:253
  77.7 19.4 %collective-permute-start.10 = (f32[128,768]{1,0:T(8,128)S(1)}, f32[128,768]{1,0:T(8,128)S(1)}, u32[]{:S(2)}, u32[]{:S(2)}) collective-permute-start(f32[128,768]{1,0:T(8,128)S(1)} %get-tuple-element.65), channel_id=1, source_target_pairs={{0,4},{4,0},{1,5},{5,1},{2,6},{6,2},{3,7},{7,3},{8,12},{12,8},{9,1... | collective-permute-start | bytes 1179656 | tf_op jit(solution)/shard_map/ppermute | solution.py:249

commit v2 on v1

v2 whole, which is shorter than its diff:
```python
import functools
import math

import jax
import jax.numpy as jnp
from jax import lax
from jax.experimental import pallas as pl
from jax.experimental.pallas import tpu as pltpu
from jax.sharding import Mesh
from jax.sharding import PartitionSpec as P

H = 32
DT = 160
DS = 48
SPAN = 384

BLOCK = 128
OWN = 2 * BLOCK
HALO = 192
WINDOW = OWN + 2 * HALO
FIRST_QUERY = WINDOW - OWN
HEADS = 4
TW = HEADS * DT
SW = HEADS * DS
SP = 256
REL = TW + SP
WIDTH_A = 2 * TW + 2 * SW
T_AT = (0, TW, 0)
S_AT = (2 * TW, 2 * TW + 128, TW)
S_OFF = (0, SW - 128, 0)
EXTRA = 16
CT = DT ** (-0.5) * math.log2(math.e)
CS = DS ** (-0.5) * math.log2(math.e)
NT = (((1,), (1,)), ((), ()))
VMEM = pl.BlockSpec(memory_space=pltpu.VMEM)
SMEM = pl.BlockSpec(memory_space=pltpu.SMEM)
HBM = pl.BlockSpec(memory_space=pltpu.HBM)
F32 = jnp.float32
BF16 = jnp.bfloat16


def call(kernel, out_shape, in_specs, scratch=(), flops=0, moved=0, exps=0, limit=40):
    return pl.pallas_call(
        kernel,
        out_shape=out_shape,
        in_specs=in_specs,
        out_specs=jax.tree.map(lambda _: VMEM, out_shape),
        scratch_shapes=list(scratch),
        compiler_params=pltpu.CompilerParams(vmem_limit_bytes=limit << 20),
        cost_estimate=pl.CostEstimate(flops=flops, bytes_accessed=moved, transcendentals=exps),
    )


def split_kernel(core, *refs):
    arrays, (send_a, keep_a, send_b, keep_b), buffers, sems = (
        refs[:6],
        refs[6:10],
        refs[10:16],
        refs[16],
    )
    me = core[0]
    copies = [
        pltpu.make_async_copy(array, buffer, sems.at[i])
        for i, (array, buffer) in enumerate(zip(arrays, buffers))
    ]
    for copy in copies:
        copy.start()
    for copy in copies:
        copy.wait()
    lane = lax.broadcasted_iota(jnp.int32, (BLOCK, SP), 1)
    mine = pl.ds(pl.multiple_of(me * TW, 128), TW)
    other = pl.ds(pl.multiple_of((1 - me) * TW, 128), TW)
    ours, theirs = [], []
    for rel in range(3):
        teacher, student = buffers[rel], buffers[3 + rel]
        keep, send, at = (keep_b, send_b, 0) if rel == 2 else (keep_a, send_a, rel * TW)
        keep[:, at : at + TW] = teacher[:, mine]
        send[:, at : at + TW] = teacher[:, other]
        low = jnp.where(lane < SW, student[:, :SP].astype(F32), 0.0)
        high = pltpu.roll(student[:, 128:].astype(F32), SP - (SW - 128), 1)
        high = jnp.where(lane < SW, high, 0.0)
        ours.append(jnp.where(me == 0, low, high))
        theirs.append(jnp.where(me == 0, high, low))
    for halves, out_a, out_b in ((ours, keep_a, keep_b), (theirs, send_a, send_b)):
        second = pltpu.roll(halves[1], S_OFF[1], 1)
        at = 2 * TW
        out_a[:, at : at + 128] = halves[0][:, :128].astype(BF16)
        out_a[:, at + 128 : at + 256] = (halves[0][:, 128:] + second[:, :128]).astype(BF16)
        out_a[:, at + 256 : at + 384] = second[:, 128:].astype(BF16)
        out_b[:, TW:] = halves[2].astype(BF16)


def edges_kernel(core, keep, recv, one, two):
    half = HALO - BLOCK

    def write(first, second, after, before):
        after[:half, :] = first[BLOCK - half :, :]
        after[half:, :] = second[...]
        before[:BLOCK, :] = first[...]
        before[BLOCK:, :] = second[:half, :]

    @pl.when(core[0] == 0)
    def _():
        write(keep, recv, one, two)

    @pl.when(core[0] != 0)
    def _():
        write(recv, keep, two, one)


def fold(value, op):
    rows, lanes = value.shape
    return op(value.reshape(rows // 8, 8, lanes), axis=0)


def relation_kernel(
    t_at,
    s_at,
    s_off,
    core,
    starts,
    weights,
    loss_in,
    keep,
    recv,
    one,
    two,
    grad_left,
    grad_own,
    grad_right,
    loss_out,
    win,
    bias,
    rt,
    rs,
    gt,
    qs,
    bt,
):
    me = core[0]
    def gather(at, rows, source):
        win[at : at + rows, :TW] = source[:, t_at : t_at + TW]
        win[at : at + rows, TW:] = source[:, s_at : s_at + SP]

    @pl.when(me == 0)
    def _():
        gather(0, HALO, one)
        gather(HALO, BLOCK, keep)
        gather(HALO + BLOCK, BLOCK, recv)
        gather(HALO + OWN, HALO, two)

    @pl.when(me != 0)
    def _():
        gather(0, HALO, two)
        gather(HALO, BLOCK, recv)
        gather(HALO + BLOCK, BLOCK, keep)
        gather(HALO + OWN, HALO, one)

    key = lax.broadcasted_iota(jnp.int32, (WINDOW, OWN), 0)
    query = lax.broadcasted_iota(jnp.int32, (WINDOW, OWN), 1) + FIRST_QUERY
    bias[...] = jnp.where((key >= starts[...]) & (key <= query), 0.0, -1e30)

    lane = lax.broadcasted_iota(jnp.int32, (OWN, SP), 1)
    student = slice(TW, REL)
    row = lax.broadcasted_iota(jnp.int32, (SP, SP), 0)
    col = lax.broadcasted_iota(jnp.int32, (SP, SP), 1)
    unit = jnp.where(row == col, 1.0, 0.0).astype(BF16)
    bt[...] = lax.dot_general(unit, win[:, student], NT, preferred_element_type=F32).astype(BF16)

    gt[:BLOCK, :] = jnp.zeros((BLOCK, HEADS * OWN), BF16)
    gt[WINDOW - BLOCK :, :] = jnp.zeros((BLOCK, HEADS * OWN), BF16)
    total = jnp.zeros((1, BLOCK), F32)
    step = 64
    for head in range(HEADS):
        start = head * DT // 128 * 128
        inside = (lane >= head * DT - start) & (lane < (head + 1) * DT - start)
        t_cols = slice(start, start + 256)
        t_query = win[FIRST_QUERY:, t_cols] * jnp.where(inside, 1.0, 0.0).astype(BF16)
        s_start = s_off + head * DS
        inside = (lane >= s_start) & (lane < s_start + DS)
        s_query = win[FIRST_QUERY:, student] * jnp.where(inside, 1.0, 0.0).astype(BF16)
        qs[head * OWN : (head + 1) * OWN, :] = s_query
        rt[...] = (
            lax.dot_general(win[:, t_cols], t_query, NT, preferred_element_type=F32) + bias[...]
        )
        rs[...] = (
            lax.dot_general(win[:, student], s_query, NT, preferred_element_type=F32) + bias[...]
        )
        for tile in range(2):
            first = tile * BLOCK
            lanes = slice(tile * BLOCK, (tile + 1) * BLOCK)
            parts = [slice(first + at, first + at + step) for at in range(0, SPAN + BLOCK, step)]
            top_t = fold(rt[parts[0], lanes], jnp.max)
            top_s = fold(rs[parts[0], lanes], jnp.max)
            for part in parts[1:]:
                top_t = jnp.maximum(top_t, fold(rt[part, lanes], jnp.max))
                top_s = jnp.maximum(top_s, fold(rs[part, lanes], jnp.max))
            top_t = jnp.max(top_t, axis=0, keepdims=True) * CT
            top_s = jnp.max(top_s, axis=0, keepdims=True) * CS
            sum_t = jnp.zeros((8, BLOCK), F32)
            sum_s = jnp.zeros((8, BLOCK), F32)
            cross = jnp.zeros((8, BLOCK), F32)
            for part in parts:
                ut = rt[part, lanes] * CT - top_t
                us = rs[part, lanes] * CS - top_s
                et = jnp.exp2(ut)
                es = jnp.exp2(us)
                sum_t = sum_t + fold(et, jnp.sum)
                sum_s = sum_s + fold(es, jnp.sum)
                cross = cross + fold(et * (ut - us), jnp.sum)
                rt[part, lanes] = et
                rs[part, lanes] = es
            sum_t = jnp.sum(sum_t, axis=0, keepdims=True)
            sum_s = jnp.sum(sum_s, axis=0, keepdims=True)
            cross = jnp.sum(cross, axis=0, keepdims=True)
            weight = weights[:, lanes]
            total = total + weight * (cross / sum_t - jnp.log2(sum_t) + jnp.log2(sum_s))
            scale_t = weight * DS ** (-0.5) / sum_t
            scale_s = weight * DS ** (-0.5) / sum_s
            g_cols = slice(head * OWN + tile * BLOCK, head * OWN + (tile + 1) * BLOCK)
            for part in parts:
                gt[part, g_cols] = (rs[part, lanes] * scale_s - rt[part, lanes] * scale_t).astype(
                    BF16
                )

    loss_out[...] = loss_in[...] + total * math.log(2.0)
    key_grad = jnp.dot(gt[...], qs[...], preferred_element_type=F32)
    row_grads = [
        jnp.dot(
            bt[s_off + head * DS : s_off + (head + 1) * DS, :],
            gt[:, head * OWN : (head + 1) * OWN],
            preferred_element_type=F32,
        )
        for head in range(HEADS)
    ]
    row_grads.insert(HEADS if s_off == 0 else 0, jnp.zeros((SP - SW, OWN), F32))
    row_grad = jnp.concatenate(row_grads, axis=0).T
    late = HALO + OWN - FIRST_QUERY
    grad_left[...] = key_grad[:HALO].astype(BF16)
    grad_own[: OWN - late, :] = key_grad[HALO:FIRST_QUERY]
    grad_own[OWN - late :, :] = key_grad[FIRST_QUERY : HALO + OWN] + row_grad[:late]
    grad_right[...] = (key_grad[HALO + OWN :] + row_grad[late:]).astype(BF16)


def join_kernel(core, loss, l0, l1, l2, r0, r1, r2, one, two):
    def write(after, before):
        for rel, (left, right) in enumerate(((l0, r0), (l1, r1), (l2, r2))):
            before[:HALO, rel * SP : (rel + 1) * SP] = left[...]
            after[:HALO, rel * SP : (rel + 1) * SP] = right[...]

    @pl.when(core[0] == 0)
    def _():
        write(one, two)

    @pl.when(core[0] != 0)
    def _():
        write(two, one)

    row = lax.broadcasted_iota(jnp.int32, (EXTRA, BLOCK), 0)
    high = loss[...].astype(BF16).astype(F32)
    middle = (loss[...] - high).astype(BF16).astype(F32)
    low = loss[...] - high - middle
    pieces = jnp.where(row == 0, high, jnp.where(row == 1, middle, jnp.where(row == 2, low, 0.0)))
    for out in (one, two):
        out[HALO:, :BLOCK] = pieces.astype(BF16)
        out[HALO:, BLOCK:] = jnp.zeros((EXTRA, 3 * SP - BLOCK), BF16)


def merge_kernel(core, loss, o0, o1, o2, one, two, keep, send, acc):
    me = core[0]
    for rel, own in enumerate((o0, o1, o2)):
        acc[:, rel * SP : (rel + 1) * SP] = own[...]

    def add(from_before, from_after):
        acc[:HALO, :] = acc[:HALO, :] + from_before[:HALO, :].astype(F32)
        acc[OWN - HALO :, :] = acc[OWN - HALO :, :] + from_after[:HALO, :].astype(F32)
        pieces = from_after[HALO:, :BLOCK].astype(F32)
        pair = loss[...] + jnp.sum(pieces, axis=0, keepdims=True)
        for out in (keep, send):
            out[BLOCK:, :BLOCK] = jnp.broadcast_to(pair, (8, BLOCK))
            out[BLOCK:, BLOCK:] = jnp.zeros((8, 3 * SP - BLOCK), F32)

    @pl.when(me == 0)
    def _():
        add(one, two)

    @pl.when(me != 0)
    def _():
        add(two, one)

    keep[:BLOCK, :] = acc[pl.ds(pl.multiple_of(me * BLOCK, 128), BLOCK), :]
    send[:BLOCK, :] = acc[pl.ds(pl.multiple_of((1 - me) * BLOCK, 128), BLOCK), :]


def place_kernel(core, keep, recv, oq, ok, ov, copies):
    me = core[0]
    pair = keep[BLOCK : BLOCK + 1, :BLOCK] + recv[BLOCK : BLOCK + 1, :BLOCK]
    copies[...] = jnp.broadcast_to(pair, copies.shape)
    empty = jnp.zeros((BLOCK, 2 * SW - SP), F32)
    for rel, out in enumerate((oq, ok, ov)):
        ours = jnp.concatenate([keep[:BLOCK, rel * SP : (rel + 1) * SP], empty], axis=1)
        theirs = jnp.concatenate([recv[:BLOCK, rel * SP : (rel + 1) * SP], empty], axis=1)
        low = jnp.where(me == 0, ours, theirs)
        high = jnp.where(me == 0, theirs, ours)
        off = S_OFF[rel]
        if off:
            low = pltpu.roll(low, 2 * SW - off, 1)
        out[...] = low + pltpu.roll(high, SW - off, 1)


def loss_kernel(tokens, parts, loss):
    total = jnp.sum(jnp.sum(parts[...], axis=0, keepdims=True), axis=1, keepdims=True)
    loss[...] = total * (1.0 / (3 * H * tokens))


def shape(rows, cols, dtype):
    return jax.ShapeDtypeStruct((rows, cols), dtype)


def body(teacher_q, teacher_k, teacher_v, student_q, student_k, student_v, doc_ids, row_weight):
    tok = ("y", "z", "parity", "core")
    count = lax.axis_size(tok)
    core = lax.axis_index("core").astype(jnp.int32).reshape(1)
    chip = lax.axis_index(("y", "z", "parity"))

    def other_core(value):
        return lax.ppermute(value, "core", [(0, 1), (1, 0)])

    def neighbours(value, way):
        step = (2 * way, -2 * way)
        pairs = [(i, (i + step[i % 2]) % count) for i in range(count)]
        return lax.ppermute(value, tok, pairs)

    arrays = (teacher_q, teacher_k, teacher_v, student_q, student_k, student_v)
    send_a, keep_a, send_b, keep_b = call(
        split_kernel,
        [shape(BLOCK, WIDTH_A, BF16)] * 2 + [shape(BLOCK, REL, BF16)] * 2,
        [SMEM] + [HBM] * 6,
        scratch=[pltpu.VMEM(a.shape, BF16) for a in arrays] + [pltpu.SemaphoreType.DMA((6,))],
        moved=4 << 20,
        limit=56,
    )(core, *arrays)
    recv_a = other_core(send_a)
    recv_b = other_core(send_b)
    edges_a = call(edges_kernel, [shape(HALO, WIDTH_A, BF16)] * 2, [SMEM] + [VMEM] * 2, moved=2 << 20)(
        core, keep_a, recv_a
    )
    halo_a = [neighbours(edges_a[0], 1), neighbours(edges_a[1], -1)]
    edges_b = call(edges_kernel, [shape(HALO, REL, BF16)] * 2, [SMEM] + [VMEM] * 2, moved=1 << 20)(
        core, keep_b, recv_b
    )
    halo_b = [neighbours(edges_b[0], 1), neighbours(edges_b[1], -1)]

    doc_ids, row_weight, _ = lax.optimization_barrier((doc_ids, row_weight, edges_b[0]))
    far = 1 << 20
    docs = jnp.concatenate([doc_ids[-HALO:] - far, doc_ids, doc_ids[:HALO] + far])
    docs = lax.dynamic_slice_in_dim(docs, chip * OWN, WINDOW)
    weight = jnp.concatenate([row_weight, row_weight[:HALO]])
    weight = lax.dynamic_slice_in_dim(weight, chip * OWN + HALO, OWN)[None, :]
    starts = jnp.sum(docs[:, None] < docs[None, FIRST_QUERY:], axis=0, dtype=jnp.int32)[None, :]

    loss = jnp.zeros((1, BLOCK), F32)
    grads = []
    for rel in range(3):
        chunk = (keep_b, recv_b, *halo_b) if rel == 2 else (keep_a, recv_a, *halo_a)
        *grad, loss = call(
            functools.partial(relation_kernel, T_AT[rel], S_AT[rel], S_OFF[rel]),
            [
                shape(HALO, SP, BF16),
                shape(OWN, SP, F32),
                shape(HALO, SP, BF16),
                shape(1, BLOCK, F32),
            ],
            [SMEM] + [VMEM] * 7,
            scratch=[
                pltpu.VMEM((WINDOW, REL), BF16),
                pltpu.VMEM((WINDOW, OWN), F32),
                pltpu.VMEM((WINDOW, OWN), F32),
                pltpu.VMEM((WINDOW, OWN), F32),
                pltpu.VMEM((WINDOW, HEADS * OWN), BF16),
                pltpu.VMEM((HEADS * OWN, SP), BF16),
                pltpu.VMEM((SP, WINDOW), BF16),
            ],
            flops=2 * 16 * WINDOW * OWN * 256,
            moved=2 << 20,
            exps=2 * HEADS * WINDOW * OWN,
        )(core, starts, weight, loss, *chunk)
        grads.append(grad)

    one, two = call(
        join_kernel, [shape(HALO + EXTRA, 3 * SP, BF16)] * 2, [SMEM] + [VMEM] * 7, moved=1 << 20
    )(core, loss, *(g[0] for g in grads), *(g[2] for g in grads))
    one = neighbours(one, 1)
    two = neighbours(two, -1)
    kept, sent = call(
        merge_kernel,
        [shape(BLOCK + 8, 3 * SP, F32)] * 2,
        [SMEM] + [VMEM] * 6,
        scratch=[pltpu.VMEM((OWN, 3 * SP), F32)],
        moved=2 << 20,
    )(core, loss, *(g[1] for g in grads), one, two)
    received = other_core(sent)
    group = ("y", "z", "head")
    grad_q, grad_k, grad_v, parts = call(
        place_kernel,
        [shape(BLOCK, 2 * SW, F32)] * 3 + [shape(lax.axis_size(group), BLOCK, F32)],
        [SMEM] + [VMEM] * 2,
        moved=1 << 20,
    )(core, kept, received)
    parts = lax.all_to_all(parts, group, 0, 0, tiled=True)
    loss = call(
        functools.partial(loss_kernel, doc_ids.shape[0]), shape(1, 1, F32), [VMEM], moved=1 << 16
    )(parts)
    return grad_q, grad_k, grad_v, loss[0, 0]


def solution(mesh):
    tok, head = mesh.devices.shape
    z = 4 if tok == 128 else 1
    axes = ("y", "z", "parity", "core", "head")
    fine = Mesh(mesh.devices.reshape(tok // (4 * z), z, 2, 2, head), axes)
    rows = axes[:4]
    placed = (P(rows, "head"),) * 6 + (P(), P())
    return jax.shard_map(
        body,
        mesh=fine,
        in_specs=placed,
        out_specs=(P(rows, "head"),) * 3 + (P(),),
        check_vma=False,
    )
```

time: 98.7 us -> 96.3 us (0.976)
  waiting for transfers between devices: 1.47 us -> 16.6 us
  starting transfers between devices: 49.4 us -> 36.9 us
  blocking collectives: 28.7 us -> 22 us
  Pallas kernels: 11.4 us -> 16.9 us
  local copies, waits for them, and re-layouts: 5.79 us -> 1.93 us
    ppermute x8 -> x6, waiting for transfers between devices: 0.02 us -> 14.9 us  [neighbours(): return lax.ppermute(value, tok, pairs)]
    ppermute x8 -> x6, starting transfers between devices: 36 us -> 24.2 us  [neighbours(): return lax.ppermute(value, tok, pairs)]
    all_to_all x2 -> x1, blocking collectives: 28.7 us -> 22 us  [body(): parts = lax.all_to_all(parts, group, 0, 0, tiled=True)]
    pallas_call x9 -> x10, Pallas kernels: 11.4 us -> 16.9 us  [the longest x3 10.7 us: body(): call(functools.partial(relation_kernel, T_AT[rel], S_AT[rel], S_OFF[rel])...]
    unnamed x16 -> x12, local copies, waits for them, and re-layouts: 5.59 us -> 1.74 us
  transfers between devices with their start and end apart: 11 -> 9, of which waited for: 1 -> 4; matrix products, arithmetic and copies ran while one was open for 1% -> 1% of each run, Pallas kernels for 7% -> 9%
where the time goes in v2:
time: 96.3 us; the launch traced here: 95.6 us
  starting transfers between devices  36.9 us (38%)
  blocking collectives  22 us (23%)
  Pallas kernels  16.9 us (18%)
  waiting for transfers between devices  16.6 us (17%)
  local copies, waits for them, and re-layouts  1.93 us (2%)
    ppermute x6, starting transfers between devices, neighbours(): return lax.ppermute(value, tok, pairs)  24.2 us
    all_to_all x1, blocking collectives, body(): parts = lax.all_to_all(parts, group, 0, 0, tiled=True)  22 us
    ppermute x6, waiting for transfers between devices, neighbours(): return lax.ppermute(value, tok, pairs)  14.9 us
    ppermute x3, starting transfers between devices, other_core(): return lax.ppermute(value, 'core', [(0, 1), (1, 0)])  12.6 us
    pallas_call x3, Pallas kernels, body(): call(functools.partial(relation_kernel, T_AT[rel], S_AT[rel], S_OFF[rel])...  10.7 us
    pallas_call x1, Pallas kernels, body(): call(split_kernel, [shape(BLOCK, WIDTH_A, BF16)] * 2 + [shape(BLOCK, REL,...  2.59 us
  transfers between devices with their start and end apart: 9, of which 4 were waited for; matrix products, arithmetic and copies ran while one was open for 1% of the time, Pallas kernels for 9%

profile of v2, /device:TPU:1, one launch (start us, length us, event | category | flops | bytes accessed | tf_op | source)
XLA Modules:
  0.0 95.6 jit_solution(1895206423033719063)
XLA Ops:
  0.6 2.6 %shard_map.111 = (bf16[128,1664]{1,0:T(8,128)(2,1)}, bf16[128,1664]{1,0:T(8,128)(2,1)}, bf16[128,896]{1,0:T(8,128)(2,1)}, bf16[128,896]{1,0:T(8,128)(2,1)}) custom-call(s32[1]{0:T(128)} %bitcast.core, bf16[128,1280]{1,0:T(8,128)(2,1)} %refs_0_.1, bf16[128,1280]{1,0:T(8,128)(2,1)} %refs_1_.1, bf16[128,1280]{1,0:T(8,128)(2,1)} %refs_2_.1, ...), custom_call_target="tpu_custom_call" | custom-call | bytes 4194304 | tf_op jit(solution)/shard_map/pallas_call | solution.py:335
  3.2 8.8 %collective-permute-start.1 = (bf16[128,1664]{1,0:T(8,128)(2,1)}, bf16[128,1664]{1,0:T(8,128)(2,1)S(1)}, u32[]{:S(2)}, u32[]{:S(2)}) collective-permute-start(bf16[128,1664]{1,0:T(8,128)(2,1)} %get-tuple-element.40), channel_id=1, source_target_pairs={{0,4},{4,0},{1,5},{5,1},{2,6},{6,2},{3,7},{7,3},{8,12},{12,8},{9,1... | collective-permute-start | bytes 1277960 | tf_op jit(solution)/shard_map/ppermute | solution.py:327
  12.0 1.9 %collective-permute-start = (bf16[128,896]{1,0:T(8,128)(2,1)}, bf16[128,896]{1,0:T(8,128)(2,1)S(1)}, u32[]{:S(2)}, u32[]{:S(2)}) collective-permute-start(bf16[128,896]{1,0:T(8,128)(2,1)} %get-tuple-element.35), channel_id=1, source_target_pairs={{0,4},{4,0},{1,5},{5,1},{2,6},{6,2},{3,7},{7,3},{8,12},{12,8},{9,1... | collective-permute-start | bytes 688136 | tf_op jit(solution)/shard_map/ppermute | solution.py:327
  14.0 1.0 %copy-done = bf16[128,1664]{1,0:T(8,128)(2,1)S(1)} copy-done((bf16[128,1664]{1,0:T(8,128)(2,1)S(1)}, bf16[128,1664]{1,0:T(8,128)(2,1)}, u32[]{:S(2)}) %copy-start) | copy-done | bytes 426008
  15.0 1.0 shard_map.113
  15.9 8.3 %collective-permute-start.2 = (bf16[192,1664]{1,0:T(8,128)(2,1)}, bf16[192,1664]{1,0:T(8,128)(2,1)S(1)}, u32[]{:S(2)}, u32[]{:S(2)}) collective-permute-start(bf16[192,1664]{1,0:T(8,128)(2,1)} %get-tuple-element.41), channel_id=1, source_target_pairs={{0,8},{4,508},{8,16},{12,4},{16,24},{20,12},{24,32},{28,20},{32,40... | collective-permute-start | bytes 1916936 | tf_op jit(solution)/shard_map/ppermute | solution.py:332
  24.3 1.9 %collective-permute-start.3 = (bf16[192,1664]{1,0:T(8,128)(2,1)S(1)}, bf16[192,1664]{1,0:T(8,128)(2,1)S(1)}, u32[]{:S(2)}, u32[]{:S(2)}) collective-permute-start(bf16[192,1664]{1,0:T(8,128)(2,1)S(1)} %get-tuple-element.42), channel_id=1, source_target_pairs={{0,504},{4,12},{8,0},{12,20},{16,8},{20,28},{24,16},{28,36},{32,24... | collective-permute-start | bytes 1916936 | tf_op jit(solution)/shard_map/ppermute | solution.py:332
  26.2 0.0 copy-start.4
  26.2 0.8 shard_map.112
  27.1 0.7 copy-done.3
  27.8 6.7 %collective-permute-start.4 = (bf16[192,896]{1,0:T(8,128)(2,1)}, bf16[192,896]{1,0:T(8,128)(2,1)}, u32[]{:S(2)}, u32[]{:S(2)}) collective-permute-start(bf16[192,896]{1,0:T(8,128)(2,1)} %get-tuple-element.36), channel_id=1, source_target_pairs={{0,8},{4,508},{8,16},{12,4},{16,24},{20,12},{24,32},{28,20},{32,40... | collective-permute-start | bytes 1032200 | tf_op jit(solution)/shard_map/ppermute | solution.py:332
  34.5 0.1 slice_add_fusion
  34.5 0.1 concatenate.6
  34.6 0.1 dynamic_slice.6
  34.7 2.0 %collective-permute-start.5 = (bf16[192,896]{1,0:T(8,128)(2,1)}, bf16[192,896]{1,0:T(8,128)(2,1)S(1)}, u32[]{:S(2)}, u32[]{:S(2)}) collective-permute-start(bf16[192,896]{1,0:T(8,128)(2,1)} %copy-done.3), channel_id=1, source_target_pairs={{0,504},{4,12},{8,0},{12,20},{16,8},{20,28},{24,16},{28,36},{32,24... | collective-permute-start | bytes 1032200 | tf_op jit(solution)/shard_map/ppermute | solution.py:332
  36.8 0.2 convert_reduce_fusion
  37.0 0.1 fusion
  37.1 6.0 %collective-permute-done.3.two = bf16[192,1664]{1,0:T(8,128)(2,1)S(1)} collective-permute-done((bf16[192,1664]{1,0:T(8,128)(2,1)S(1)}, bf16[192,1664]{1,0:T(8,128)(2,1)S(1)}, u32[]{:S(2)}, u32[]{:S(2)}) %collective-permute-start.3) | collective-permute-done | bytes 639008 | tf_op jit(solution)/shard_map/ppermute | solution.py:332
  43.1 3.3 %shard_map.114 = (bf16[192,256]{1,0:T(8,128)(2,1)S(1)}, f32[256,256]{1,0:T(8,128)S(1)}, bf16[192,256]{1,0:T(8,128)(2,1)S(1)}, f32[1,128]{1,0:T(1,128)S(1)}) custom-call(s32[1]{0:T(128)} %bitcast.core, s32[1,256]{1,0:T(1,128)S(1)} %bitcast.13, f32[1,256]{1,0:T(1,128)S(1)} %bitcast.10, f32[1,128]{1,0:T(1,128)S(1)} %broadcast_in_dim.13.loss_in, ...), custom_call_target="tpu_custom_call" | custom-call | flops 1342177280 | bytes 2097152 | tf_op jit(solution)/shard_map/pallas_call | solution.py:366
  46.3 3.3 %shard_map.115 = (bf16[192,256]{1,0:T(8,128)(2,1)S(1)}, f32[256,256]{1,0:T(8,128)S(1)}, bf16[192,256]{1,0:T(8,128)(2,1)S(1)}, f32[1,128]{1,0:T(1,128)S(1)}) custom-call(s32[1]{0:T(128)} %bitcast.core, s32[1,256]{1,0:T(1,128)S(1)} %bitcast.14, f32[1,256]{1,0:T(1,128)S(1)} %bitcast.11, f32[1,128]{1,0:T(1,128)S(1)} %get-tuple-element.43.loss_in, ...), custom_call_target="tpu_custom_call" | custom-call | flops 1342177280 | bytes 2097152 | tf_op jit(solution)/shard_map/pallas_call | solution.py:366
  49.6 4.2 %shard_map.116 = (bf16[192,256]{1,0:T(8,128)(2,1)S(1)}, f32[256,256]{1,0:T(8,128)S(1)}, bf16[192,256]{1,0:T(8,128)(2,1)S(1)}, f32[1,128]{1,0:T(1,128)S(1)}) custom-call(s32[1]{0:T(128)} %bitcast.core, s32[1,256]{1,0:T(1,128)S(1)} %bitcast.15, f32[1,256]{1,0:T(1,128)S(1)} %bitcast.12, f32[1,128]{1,0:T(1,128)S(1)} %get-tuple-element.44.loss_in, ...), custom_call_target="tpu_custom_call" | custom-call | flops 1342177280 | bytes 2097152 | tf_op jit(solution)/shard_map/pallas_call | solution.py:366
  53.9 0.1 shard_map.117
  53.9 1.9 %collective-permute-start.6 = (bf16[208,768]{1,0:T(8,128)(2,1)S(1)}, bf16[208,768]{1,0:T(8,128)(2,1)S(1)}, u32[]{:S(2)}, u32[]{:S(2)}) collective-permute-start(bf16[208,768]{1,0:T(8,128)(2,1)S(1)} %get-tuple-element.56), channel_id=1, source_target_pairs={{0,8},{4,508},{8,16},{12,4},{16,24},{20,12},{24,32},{28,20},{32,40... | collective-permute-start | bytes 958472 | tf_op jit(solution)/shard_map/ppermute | solution.py:332
  55.8 3.4 %collective-permute-start.7 = (bf16[208,768]{1,0:T(8,128)(2,1)S(1)}, bf16[208,768]{1,0:T(8,128)(2,1)S(1)}, u32[]{:S(2)}, u32[]{:S(2)}) collective-permute-start(bf16[208,768]{1,0:T(8,128)(2,1)S(1)} %get-tuple-element.57), channel_id=1, source_target_pairs={{0,504},{4,12},{8,0},{12,20},{16,8},{20,28},{24,16},{28,36},{32,24... | collective-permute-start | bytes 958472 | tf_op jit(solution)/shard_map/ppermute | solution.py:332
  59.2 5.0 %collective-permute-done.6.one = bf16[208,768]{1,0:T(8,128)(2,1)S(1)} collective-permute-done((bf16[208,768]{1,0:T(8,128)(2,1)S(1)}, bf16[208,768]{1,0:T(8,128)(2,1)S(1)}, u32[]{:S(2)}, u32[]{:S(2)}) %collective-permute-start.6) | collective-permute-done | bytes 319520 | tf_op jit(solution)/shard_map/ppermute | solution.py:332
  64.2 3.9 %collective-permute-done.7.two = bf16[208,768]{1,0:T(8,128)(2,1)S(1)} collective-permute-done((bf16[208,768]{1,0:T(8,128)(2,1)S(1)}, bf16[208,768]{1,0:T(8,128)(2,1)S(1)}, u32[]{:S(2)}, u32[]{:S(2)}) %collective-permute-start.7) | collective-permute-done | bytes 319520 | tf_op jit(solution)/shard_map/ppermute | solution.py:332
  68.1 0.2 shard_map.118
  68.3 1.9 %collective-permute-start.8 = (f32[136,768]{1,0:T(8,128)S(1)}, f32[136,768]{1,0:T(8,128)S(1)}, u32[]{:S(2)}, u32[]{:S(2)}) collective-permute-start(f32[136,768]{1,0:T(8,128)S(1)} %get-tuple-element.59), channel_id=1, source_target_pairs={{0,4},{4,0},{1,5},{5,1},{2,6},{6,2},{3,7},{7,3},{8,12},{12,8},{9,1... | collective-permute-start | bytes 1253384 | tf_op jit(solution)/shard_map/ppermute | solution.py:327
  70.2 1.7 %collective-permute-done.8.recv = f32[136,768]{1,0:T(8,128)S(1)} collective-permute-done((f32[136,768]{1,0:T(8,128)S(1)}, f32[136,768]{1,0:T(8,128)S(1)}, u32[]{:S(2)}, u32[]{:S(2)}) %collective-permute-start.8) | collective-permute-done | bytes 417824 | tf_op jit(solution)/shard_map/ppermute | solution.py:327
  72.0 0.9 shard_map.119
  72.9 22.0 %all_to_all.11 = f32[128,1,128]{2,1,0:T(1,128)S(1)} all-to-all(f32[128,1,128]{2,1,0:T(1,128)S(1)} %bitcast.9), channel_id=1, replica_groups=mesh['y'=8,'z'=4,'parity'=2,'core'=2,'head'=4] {'y','z','head'}, dimensions={0} | all-to-all | bytes 131072 | tf_op jit(solution)/shard_map/all_to_all | solution.py:410
  94.9 0.6 shard_map.120
  (18 shorter events, 0.0 us)
Async XLA Ops:
  3.2 10.7 %collective-permute-start.1 = (bf16[128,1664]{1,0:T(8,128)(2,1)}, bf16[128,1664]{1,0:T(8,128)(2,1)S(1)}, u32[]{:S(2)}, u32[]{:S(2)}) collective-permute-start(bf16[128,1664]{1,0:T(8,128)(2,1)} %get-tuple-element.40), channel_id=1, source_target_pairs={{0,4},{4,0},{1,5},{5,1},{2,6},{6,2},{3,7},{7,3},{8,12},{12,8},{9,1... | collective-permute-start | bytes 1277960 | tf_op jit(solution)/shard_map/ppermute | solution.py:327
  12.0 14.2 %collective-permute-start = (bf16[128,896]{1,0:T(8,128)(2,1)}, bf16[128,896]{1,0:T(8,128)(2,1)S(1)}, u32[]{:S(2)}, u32[]{:S(2)}) collective-permute-start(bf16[128,896]{1,0:T(8,128)(2,1)} %get-tuple-element.35), channel_id=1, source_target_pairs={{0,4},{4,0},{1,5},{5,1},{2,6},{6,2},{3,7},{7,3},{8,12},{12,8},{9,1... | collective-permute-start | bytes 688136 | tf_op jit(solution)/shard_map/ppermute | solution.py:327
  14.0 1.0 %copy-start = (bf16[128,1664]{1,0:T(8,128)(2,1)S(1)}, bf16[128,1664]{1,0:T(8,128)(2,1)}, u32[]{:S(2)}) copy-start(bf16[128,1664]{1,0:T(8,128)(2,1)} %get-tuple-element.39.keep) | copy-start | bytes 1277956
  15.0 11.2 %copy-start.2 = (bf16[128,896]{1,0:T(8,128)(2,1)S(1)}, bf16[128,896]{1,0:T(8,128)(2,1)}, u32[]{:S(2)}) copy-start(bf16[128,896]{1,0:T(8,128)(2,1)} %get-tuple-element.34.keep) | copy-start | bytes 688132
  15.9 27.1 %copy-start.1 = (bf16[128,1664]{1,0:T(8,128)(2,1)S(1)}, bf16[128,1664]{1,0:T(8,128)(2,1)}, u32[]{:S(2)}) copy-start(bf16[128,1664]{1,0:T(8,128)(2,1)} %get-tuple-element.39.keep) | copy-start | bytes 1277956
  15.9 21.1 %collective-permute-start.2 = (bf16[192,1664]{1,0:T(8,128)(2,1)}, bf16[192,1664]{1,0:T(8,128)(2,1)S(1)}, u32[]{:S(2)}, u32[]{:S(2)}) collective-permute-start(bf16[192,1664]{1,0:T(8,128)(2,1)} %get-tuple-element.41), channel_id=1, source_target_pairs={{0,8},{4,508},{8,16},{12,4},{16,24},{20,12},{24,32},{28,20},{32,40... | collective-permute-start | bytes 1916936 | tf_op jit(solution)/shard_map/ppermute | solution.py:332
  24.3 18.8 %collective-permute-start.3 = (bf16[192,1664]{1,0:T(8,128)(2,1)S(1)}, bf16[192,1664]{1,0:T(8,128)(2,1)S(1)}, u32[]{:S(2)}, u32[]{:S(2)}) collective-permute-start(bf16[192,1664]{1,0:T(8,128)(2,1)S(1)} %get-tuple-element.42), channel_id=1, source_target_pairs={{0,504},{4,12},{8,0},{12,20},{16,8},{20,28},{24,16},{28,36},{32,24... | collective-permute-start | bytes 1916936 | tf_op jit(solution)/shard_map/ppermute | solution.py:332
  26.2 8.2 %copy-start.4 = (s32[16384]{0:T(1024)S(1)}, s32[16384]{0:T(1024)}, u32[]{:S(2)}) copy-start(s32[16384]{0:T(1024)} %param.14) | copy-start | bytes 196612
  27.1 0.7 copy-start.3
  27.8 21.8 %collective-permute-start.4 = (bf16[192,896]{1,0:T(8,128)(2,1)}, bf16[192,896]{1,0:T(8,128)(2,1)}, u32[]{:S(2)}, u32[]{:S(2)}) collective-permute-start(bf16[192,896]{1,0:T(8,128)(2,1)} %get-tuple-element.36), channel_id=1, source_target_pairs={{0,8},{4,508},{8,16},{12,4},{16,24},{20,12},{24,32},{28,20},{32,40... | collective-permute-start | bytes 1032200 | tf_op jit(solution)/shard_map/ppermute | solution.py:332
  34.5 2.4 %copy-start.5 = (f32[16384]{0:T(1024)S(1)}, f32[16384]{0:T(1024)}, u32[]{:S(2)}) copy-start(f32[16384]{0:T(1024)} %param.15) | copy-start | bytes 196612
  34.7 2.2 %slice-start = ((f32[16384]{0:T(1024)}), f32[192]{0:T(256)S(1)}, s32[]{:S(2)}) async-start(f32[16384]{0:T(1024)} %param.15), calls=%async_computation.1 | async-start | bytes 2048 | tf_op jit(solution)/shard_map/slice | solution.py:358
  34.7 14.9 %collective-permute-start.5 = (bf16[192,896]{1,0:T(8,128)(2,1)}, bf16[192,896]{1,0:T(8,128)(2,1)S(1)}, u32[]{:S(2)}, u32[]{:S(2)}) collective-permute-start(bf16[192,896]{1,0:T(8,128)(2,1)} %copy-done.3), channel_id=1, source_target_pairs={{0,504},{4,12},{8,0},{12,20},{16,8},{20,28},{24,16},{28,36},{32,24... | collective-permute-start | bytes 1032200 | tf_op jit(solution)/shard_map/ppermute | solution.py:332
  53.9 10.3 %collective-permute-start.6 = (bf16[208,768]{1,0:T(8,128)(2,1)S(1)}, bf16[208,768]{1,0:T(8,128)(2,1)S(1)}, u32[]{:S(2)}, u32[]{:S(2)}) collective-permute-start(bf16[208,768]{1,0:T(8,128)(2,1)S(1)} %get-tuple-element.56), channel_id=1, source_target_pairs={{0,8},{4,508},{8,16},{12,4},{16,24},{20,12},{24,32},{28,20},{32,40... | collective-permute-start | bytes 958472 | tf_op jit(solution)/shard_map/ppermute | solution.py:332
  55.8 12.2 %collective-permute-start.7 = (bf16[208,768]{1,0:T(8,128)(2,1)S(1)}, bf16[208,768]{1,0:T(8,128)(2,1)S(1)}, u32[]{:S(2)}, u32[]{:S(2)}) collective-permute-start(bf16[208,768]{1,0:T(8,128)(2,1)S(1)} %get-tuple-element.57), channel_id=1, source_target_pairs={{0,504},{4,12},{8,0},{12,20},{16,8},{20,28},{24,16},{28,36},{32,24... | collective-permute-start | bytes 958472 | tf_op jit(solution)/shard_map/ppermute | solution.py:332
  68.3 3.7 %collective-permute-start.8 = (f32[136,768]{1,0:T(8,128)S(1)}, f32[136,768]{1,0:T(8,128)S(1)}, u32[]{:S(2)}, u32[]{:S(2)}) collective-permute-start(f32[136,768]{1,0:T(8,128)S(1)} %get-tuple-element.59), channel_id=1, source_target_pairs={{0,4},{4,0},{1,5},{5,1},{2,6},{6,2},{3,7},{7,3},{8,12},{12,8},{9,1... | collective-permute-start | bytes 1253384 | tf_op jit(solution)/shard_map/ppermute | solution.py:327

commit v3 on v2

v3 whole, which is shorter than its diff:
```python
import functools
import math

import jax
import jax.numpy as jnp
from jax import lax
from jax.experimental import pallas as pl
from jax.experimental.pallas import tpu as pltpu
from jax.sharding import Mesh
from jax.sharding import PartitionSpec as P

H = 32
DT = 160
DS = 48
SPAN = 384

BLOCK = 128
OWN = 2 * BLOCK
HALO = 192
WINDOW = OWN + 2 * HALO
FIRST_QUERY = WINDOW - OWN
HEADS = 4
TW = HEADS * DT
SW = HEADS * DS
SP = 256
REL = TW + SP
WIDTH_A = 2 * TW + 2 * SW
T_AT = (0, TW, 0)
S_AT = (2 * TW, 2 * TW + 128, TW)
S_OFF = (0, SW - 128, 0)
CT = DT ** (-0.5) * math.log2(math.e)
CS = DS ** (-0.5) * math.log2(math.e)
NT = (((1,), (1,)), ((), ()))
FAR = 4096
VMEM = pl.BlockSpec(memory_space=pltpu.VMEM)
SMEM = pl.BlockSpec(memory_space=pltpu.SMEM)
F32 = jnp.float32
BF16 = jnp.bfloat16


def call(kernel, out_shape, in_specs, scratch=(), flops=0, moved=0, exps=0, limit=8):
    return pl.pallas_call(
        kernel,
        out_shape=out_shape,
        in_specs=in_specs,
        out_specs=jax.tree.map(lambda _: VMEM, out_shape),
        scratch_shapes=list(scratch),
        compiler_params=pltpu.CompilerParams(vmem_limit_bytes=limit << 20),
        cost_estimate=pl.CostEstimate(flops=flops, bytes_accessed=moved, transcendentals=exps),
    )


def zero_kernel(loss):
    loss[...] = jnp.zeros_like(loss)


def split_kernel(core, _, tq, tk, tv, sq, sk, sv, send_a, keep_a, send_b, keep_b):
    me = core[0]
    buffers = (tq, tk, tv, sq, sk, sv)
    lane = lax.broadcasted_iota(jnp.int32, (BLOCK, SP), 1)
    mine = pl.ds(pl.multiple_of(me * TW, 128), TW)
    other = pl.ds(pl.multiple_of((1 - me) * TW, 128), TW)
    ours, theirs = [], []
    for rel in range(3):
        teacher, student = buffers[rel], buffers[3 + rel]
        keep, send, at = (keep_b, send_b, 0) if rel == 2 else (keep_a, send_a, rel * TW)
        keep[:, at : at + TW] = teacher[:, mine]
        send[:, at : at + TW] = teacher[:, other]
        low = jnp.where(lane < SW, student[:, :SP].astype(F32), 0.0)
        high = pltpu.roll(student[:, 128:].astype(F32), SP - (SW - 128), 1)
        high = jnp.where(lane < SW, high, 0.0)
        ours.append(jnp.where(me == 0, low, high))
        theirs.append(jnp.where(me == 0, high, low))
    for halves, out_a, out_b in ((ours, keep_a, keep_b), (theirs, send_a, send_b)):
        second = pltpu.roll(halves[1], S_OFF[1], 1)
        at = 2 * TW
        out_a[:, at : at + 128] = halves[0][:, :128].astype(BF16)
        out_a[:, at + 128 : at + 256] = (halves[0][:, 128:] + second[:, :128]).astype(BF16)
        out_a[:, at + 256 : at + 384] = second[:, 128:].astype(BF16)
        out_b[:, TW:] = halves[2].astype(BF16)


def mask_kernel(chip, docs, rows, starts, weights):
    count = docs.shape[0]
    first = 2 * chip[0] - 2

    def row_of(ref, r):
        at = first + r
        return ref[pl.ds(lax.rem(at + count, count), 1), :]

    lines = []
    for r in range(6):
        at = first + r
        shift = jnp.where(at < 0, -FAR, jnp.where(at >= count, FAR, 0))
        lines.append((row_of(docs, r) + shift).astype(F32))

    def queries(parts):
        joined = jnp.broadcast_to(jnp.concatenate(parts, axis=1), (8, 3 * BLOCK))
        return pltpu.roll(joined, 2 * BLOCK + 64, 1)[:1, :OWN]

    query = queries(lines[3:])
    before = jnp.zeros((1, OWN), F32)
    for line in lines:
        keys = jnp.broadcast_to(line, (BLOCK, BLOCK)).T
        keys = jnp.concatenate([keys, keys], axis=1)
        before = before + jnp.sum(jnp.where(keys < query, 1.0, 0.0), axis=0, keepdims=True)
    starts[...] = before.astype(jnp.int32) - 64
    weights[...] = queries([row_of(rows, r) for r in range(3, 6)])


def edges_kernel(core, keep, recv, one, two):
    half = HALO - BLOCK

    def write(first, second, after, before):
        after[:half, :] = first[BLOCK - half :, :]
        after[half:, :] = second[...]
        before[:BLOCK, :] = first[...]
        before[BLOCK:, :] = second[:half, :]

    @pl.when(core[0] == 0)
    def _():
        write(keep, recv, one, two)

    @pl.when(core[0] != 0)
    def _():
        write(recv, keep, two, one)


def fold(value, op):
    rows, lanes = value.shape
    return op(value.reshape(rows // 8, 8, lanes), axis=0)


def relation_kernel(
    t_at,
    s_at,
    s_off,
    core,
    starts,
    weights,
    loss_in,
    keep,
    recv,
    one,
    two,
    grad_left,
    grad_own,
    grad_right,
    loss_out,
    win,
    bias,
    rt,
    rs,
    gt,
    qs,
    bt,
    kg,
):
    me = core[0]
    def gather(at, rows, source):
        win[at : at + rows, :TW] = source[:, t_at : t_at + TW]
        win[at : at + rows, TW:] = source[:, s_at : s_at + SP]

    @pl.when(me == 0)
    def _():
        gather(0, HALO, one)
        gather(HALO, BLOCK, keep)
        gather(HALO + BLOCK, BLOCK, recv)
        gather(HALO + OWN, HALO, two)

    @pl.when(me != 0)
    def _():
        gather(0, HALO, two)
        gather(HALO, BLOCK, recv)
        gather(HALO + BLOCK, BLOCK, keep)
        gather(HALO + OWN, HALO, one)

    key = lax.broadcasted_iota(jnp.int32, (WINDOW, OWN), 0)
    query = lax.broadcasted_iota(jnp.int32, (WINDOW, OWN), 1) + FIRST_QUERY
    bias[...] = jnp.where((key >= starts[...]) & (key <= query), 0.0, -1e30)

    lane = lax.broadcasted_iota(jnp.int32, (OWN, SP), 1)
    student = slice(TW, REL)
    row = lax.broadcasted_iota(jnp.int32, (SP, SP), 0)
    col = lax.broadcasted_iota(jnp.int32, (SP, SP), 1)
    unit = jnp.where(row == col, 1.0, 0.0).astype(BF16)
    bt[...] = lax.dot_general(unit, win[:, student], NT, preferred_element_type=F32).astype(BF16)

    gt[:BLOCK, :] = jnp.zeros((BLOCK, HEADS * OWN), BF16)
    gt[WINDOW - BLOCK :, :] = jnp.zeros((BLOCK, HEADS * OWN), BF16)
    step = 64
    tiles = [
        (
            slice(tile * BLOCK, (tile + 1) * BLOCK),
            [slice(at, at + step) for at in range(tile * BLOCK, SPAN + (tile + 1) * BLOCK, step)],
        )
        for tile in range(2)
    ]
    tops, sums = {}, {}
    totals = []

    def scores(head):
        start = head * DT // 128 * 128
        inside = (lane >= head * DT - start) & (lane < (head + 1) * DT - start)
        t_cols = slice(start, start + 256)
        t_query = win[FIRST_QUERY:, t_cols] * jnp.where(inside, 1.0, 0.0).astype(BF16)
        s_start = s_off + head * DS
        inside = (lane >= s_start) & (lane < s_start + DS)
        s_query = win[FIRST_QUERY:, student] * jnp.where(inside, 1.0, 0.0).astype(BF16)
        qs[head * OWN : (head + 1) * OWN, :] = s_query
        rt[head] = (
            lax.dot_general(win[:, t_cols], t_query, NT, preferred_element_type=F32) + bias[...]
        )
        rs[head] = (
            lax.dot_general(win[:, student], s_query, NT, preferred_element_type=F32) + bias[...]
        )

    def maxima(head):
        for tile, (lanes, parts) in enumerate(tiles):
            for z, r, scale in ((0, rt, CT), (1, rs, CS)):
                top = fold(r[head, parts[0], lanes], jnp.max)
                for part in parts[1:]:
                    top = jnp.maximum(top, fold(r[head, part, lanes], jnp.max))
                tops[head, tile, z] = jnp.max(top, axis=0, keepdims=True) * scale

    def exponentials(head):
        for tile, (lanes, parts) in enumerate(tiles):
            top_t, top_s = tops[head, tile, 0], tops[head, tile, 1]
            sum_t = jnp.zeros((8, BLOCK), F32)
            sum_s = jnp.zeros((8, BLOCK), F32)
            cross = jnp.zeros((8, BLOCK), F32)
            for part in parts:
                ut = rt[head, part, lanes] * CT - top_t
                us = rs[head, part, lanes] * CS - top_s
                et = jnp.exp2(ut)
                es = jnp.exp2(us)
                sum_t = sum_t + fold(et, jnp.sum)
                sum_s = sum_s + fold(es, jnp.sum)
                cross = cross + fold(et * (ut - us), jnp.sum)
                rt[head, part, lanes] = et
                rs[head, part, lanes] = es
            sum_t = jnp.sum(sum_t, axis=0, keepdims=True)
            sum_s = jnp.sum(sum_s, axis=0, keepdims=True)
            cross = jnp.sum(cross, axis=0, keepdims=True)
            weight = weights[:, lanes]
            totals.append(weight * (cross / sum_t - jnp.log2(sum_t) + jnp.log2(sum_s)))
            sums[head, tile] = weight * DS ** (-0.5) / sum_t, weight * DS ** (-0.5) / sum_s

    def gradients(head):
        for tile, (lanes, parts) in enumerate(tiles):
            scale_t, scale_s = sums[head, tile]
            g_cols = slice(head * OWN + tile * BLOCK, head * OWN + (tile + 1) * BLOCK)
            for part in parts:
                gt[part, g_cols] = (
                    rs[head, part, lanes] * scale_s - rt[head, part, lanes] * scale_t
                ).astype(BF16)

    row_grads = []

    def products(head):
        row_grads.append(
            jnp.dot(
                bt[s_off + head * DS : s_off + (head + 1) * DS, :],
                gt[:, head * OWN : (head + 1) * OWN],
                preferred_element_type=F32,
            )
        )

    def key_product(first, last):
        return jnp.dot(
            gt[:, first * OWN : last * OWN],
            qs[first * OWN : last * OWN, :],
            preferred_element_type=F32,
        )

    scores(0)
    scores(1)
    maxima(0)
    exponentials(0)
    scores(2)
    maxima(1)
    gradients(0)
    exponentials(1)
    products(0)
    scores(3)
    maxima(2)
    gradients(1)
    exponentials(2)
    products(1)
    kg[...] = key_product(0, 2)
    maxima(3)
    gradients(2)
    exponentials(3)
    products(2)
    gradients(3)
    products(3)
    key_grad = kg[...] + key_product(2, 4)
    loss_out[...] = loss_in[...] + functools.reduce(jnp.add, totals) * math.log(2.0)
    row_grads.insert(HEADS if s_off == 0 else 0, jnp.zeros((SP - SW, OWN), F32))
    row_grad = jnp.concatenate(row_grads, axis=0).T
    late = HALO + OWN - FIRST_QUERY
    grad_left[...] = key_grad[:HALO].astype(BF16)
    grad_own[: OWN - late, :] = key_grad[HALO:FIRST_QUERY]
    grad_own[OWN - late :, :] = key_grad[FIRST_QUERY : HALO + OWN] + row_grad[:late]
    grad_right[...] = (key_grad[HALO + OWN :] + row_grad[late:]).astype(BF16)


def join_kernel(core, loss, l0, l1, l2, r0, r1, r2, one, two, copies):
    copies[...] = jnp.broadcast_to(loss[...], copies.shape)

    def write(after, before):
        for rel, (left, right) in enumerate(((l0, r0), (l1, r1), (l2, r2))):
            before[:, rel * SP : (rel + 1) * SP] = left[...]
            after[:, rel * SP : (rel + 1) * SP] = right[...]

    @pl.when(core[0] == 0)
    def _():
        write(one, two)

    @pl.when(core[0] != 0)
    def _():
        write(two, one)


def merge_kernel(core, parts, o0, o1, o2, one, two, keep, send, copies, acc):
    me = core[0]
    copies[...] = jnp.broadcast_to(jnp.sum(parts[...], axis=0, keepdims=True), copies.shape)
    for rel, own in enumerate((o0, o1, o2)):
        acc[:, rel * SP : (rel + 1) * SP] = own[...]

    def add(from_before, from_after):
        acc[:HALO, :] = acc[:HALO, :] + from_before[...].astype(F32)
        acc[OWN - HALO :, :] = acc[OWN - HALO :, :] + from_after[...].astype(F32)

    @pl.when(me == 0)
    def _():
        add(one, two)

    @pl.when(me != 0)
    def _():
        add(two, one)

    keep[...] = acc[pl.ds(pl.multiple_of(me * BLOCK, 128), BLOCK), :]
    send[...] = acc[pl.ds(pl.multiple_of((1 - me) * BLOCK, 128), BLOCK), :]


def place_kernel(tokens, core, parts, keep, recv, oq, ok, ov, loss):
    me = core[0]
    total = jnp.sum(jnp.sum(parts[...], axis=0, keepdims=True), axis=1, keepdims=True)
    loss[...] = total * (1.0 / (3 * H * tokens))
    empty = jnp.zeros((BLOCK, 2 * SW - SP), F32)
    for rel, out in enumerate((oq, ok, ov)):
        ours = jnp.concatenate([keep[:, rel * SP : (rel + 1) * SP], empty], axis=1)
        theirs = jnp.concatenate([recv[:, rel * SP : (rel + 1) * SP], empty], axis=1)
        low = jnp.where(me == 0, ours, theirs)
        high = jnp.where(me == 0, theirs, ours)
        off = S_OFF[rel]
        if off:
            low = pltpu.roll(low, 2 * SW - off, 1)
        out[...] = low + pltpu.roll(high, SW - off, 1)


def shape(rows, cols, dtype):
    return jax.ShapeDtypeStruct((rows, cols), dtype)


def call_relation(rel, core, starts, weight, loss, chunk):
    return call(
        functools.partial(relation_kernel, T_AT[rel], S_AT[rel], S_OFF[rel]),
        [
            shape(HALO, SP, BF16),
            shape(OWN, SP, F32),
            shape(HALO, SP, BF16),
            shape(1, BLOCK, F32),
        ],
        [SMEM] + [VMEM] * 7,
        scratch=[
            pltpu.VMEM((WINDOW, REL), BF16),
            pltpu.VMEM((WINDOW, OWN), F32),
            pltpu.VMEM((HEADS, WINDOW, OWN), F32),
            pltpu.VMEM((HEADS, WINDOW, OWN), F32),
            pltpu.VMEM((WINDOW, HEADS * OWN), BF16),
            pltpu.VMEM((HEADS * OWN, SP), BF16),
            pltpu.VMEM((SP, WINDOW), BF16),
            pltpu.VMEM((WINDOW, SP), F32),
        ],
        flops=2 * 16 * WINDOW * OWN * 256,
        moved=2 << 20,
        exps=2 * HEADS * WINDOW * OWN,
        limit=20,
    )(core, starts, weight, loss, *chunk)


def body(teacher_q, teacher_k, teacher_v, student_q, student_k, student_v, doc_ids, row_weight):
    tok = ("y", "z", "parity", "core")
    count = lax.axis_size(tok)
    core = lax.axis_index("core").astype(jnp.int32).reshape(1)
    chip = lax.axis_index(("y", "z", "parity"))

    def other_core(value):
        return lax.ppermute(value, "core", [(0, 1), (1, 0)])

    def neighbours(value, way):
        step = (2 * way, -2 * way)
        pairs = [(i, (i + step[i % 2]) % count) for i in range(count)]
        return lax.ppermute(value, tok, pairs)

    loss = call(zero_kernel, shape(1, BLOCK, F32), [], moved=32 << 20)()
    send_a, keep_a, send_b, keep_b = call(
        split_kernel,
        [shape(BLOCK, WIDTH_A, BF16)] * 2 + [shape(BLOCK, REL, BF16)] * 2,
        [SMEM] + [VMEM] * 7,
        moved=4 << 20,
    )(core, loss, teacher_q, teacher_k, teacher_v, student_q, student_k, student_v)
    recv_a = other_core(send_a)
    recv_b = other_core(send_b)
    edges_a = call(edges_kernel, [shape(HALO, WIDTH_A, BF16)] * 2, [SMEM] + [VMEM] * 2, moved=2 << 20)(
        core, keep_a, recv_a
    )
    halo_a = [neighbours(edges_a[0], 1), neighbours(edges_a[1], -1)]
    keep_b, recv_b, _ = lax.optimization_barrier((keep_b, recv_b, halo_a[0]))
    edges_b = call(edges_kernel, [shape(HALO, REL, BF16)] * 2, [SMEM] + [VMEM] * 2, moved=1 << 20)(
        core, keep_b, recv_b
    )
    halo_b = [neighbours(edges_b[0], 1), neighbours(edges_b[1], -1)]

    doc_ids, row_weight, _ = lax.optimization_barrier((doc_ids, row_weight, edges_a[0]))
    starts, weight = call(
        mask_kernel,
        [shape(1, OWN, jnp.int32), shape(1, OWN, F32)],
        [SMEM] + [VMEM] * 2,
        moved=1 << 17,
    )(
        chip.astype(jnp.int32).reshape(1),
        doc_ids.reshape(-1, BLOCK),
        row_weight.reshape(-1, BLOCK),
    )
    grads = []
    for rel in range(3):
        chunk = (keep_b, recv_b, *halo_b) if rel == 2 else (keep_a, recv_a, *halo_a)
        *grad, loss = call_relation(rel, core, starts, weight, loss, chunk)
        grads.append(grad)

    stages = (("z", "parity", "core"), ("y", "head"))
    copies = [shape(lax.axis_size(axes), BLOCK, F32) for axes in stages]

    def exchange(value, axes):
        return lax.all_to_all(value, axes, 0, 0, tiled=True)

    one, two, parts = call(
        join_kernel,
        [shape(HALO, 3 * SP, BF16)] * 2 + [copies[0]],
        [SMEM] + [VMEM] * 7,
        moved=1 << 20,
    )(core, loss, *(g[0] for g in grads), *(g[2] for g in grads))
    one = neighbours(one, 1)
    two = neighbours(two, -1)
    parts = exchange(parts, stages[0])
    kept, sent, parts = call(
        merge_kernel,
        [shape(BLOCK, 3 * SP, F32)] * 2 + [copies[1]],
        [SMEM] + [VMEM] * 6,
        scratch=[pltpu.VMEM((OWN, 3 * SP), F32)],
        moved=2 << 20,
    )(core, parts, *(g[1] for g in grads), one, two)
    received = other_core(sent)
    parts = exchange(parts, stages[1])
    grad_q, grad_k, grad_v, loss = call(
        functools.partial(place_kernel, doc_ids.shape[0]),
        [shape(BLOCK, 2 * SW, F32)] * 3 + [shape(1, 1, F32)],
        [SMEM] + [VMEM] * 3,
        moved=1 << 20,
    )(core, parts, kept, received)
    return grad_q, grad_k, grad_v, loss[0, 0]


def solution(mesh):
    tok, head = mesh.devices.shape
    z = 4 if tok == 128 else 1
    axes = ("y", "z", "parity", "core", "head")
    fine = Mesh(mesh.devices.reshape(tok // (4 * z), z, 2, 2, head), axes)
    rows = axes[:4]
    placed = (P(rows, "head"),) * 6 + (P(), P())
    return jax.shard_map(
        body,
        mesh=fine,
        in_specs=placed,
        out_specs=(P(rows, "head"),) * 3 + (P(),),
        check_vma=False,
    )
```

time: 96.3 us -> 96.4 us (level)
  waiting for transfers between devices: 16.6 us -> 11.6 us
  blocking collectives: 22 us -> 26.2 us
  Pallas kernels: 16.9 us -> 12.9 us
  local copies, waits for them, and re-layouts: 1.93 us -> 5.6 us
  starting transfers between devices: 36.9 us -> 38.7 us
    ppermute x6, waiting for transfers between devices: 14.9 us -> 9.1 us  [neighbours(): return lax.ppermute(value, tok, pairs)]
    all_to_all x1 -> x2, blocking collectives: 22 us -> 26.2 us  [exchange(): return lax.all_to_all(value, axes, 0, 0, tiled=True)]
    unnamed x12 -> x16, local copies, waits for them, and re-layouts: 1.74 us -> 5.6 us
    pallas_call x1, Pallas kernels: 2.59 us -> 0.26 us  [body(): call(split_kernel, [shape(BLOCK, WIDTH_A, BF16)] * 2 + [shape(BLOCK, REL,...]
    ppermute x3, starting transfers between devices: 12.6 us -> 13.9 us  [other_core(): return lax.ppermute(value, 'core', [(0, 1), (1, 0)])]
    pallas_call x7 -> x8, Pallas kernels: 12.6 us -> 11.7 us  [the longest x3 10.2 us: call_relation(): call(functools.partial(relation_kernel, T_AT[rel], S_AT[rel], S_OFF[rel])...]
  transfers between devices with their start and end apart: 9 -> 9, of which waited for: 4 -> 4; matrix products, arithmetic and copies ran while one was open for 1% -> 0% of each run, Pallas kernels for 9% -> 8%
where the time goes in v3:
time: 96.4 us; the launch traced here: 95.8 us
  starting transfers between devices  38.7 us (40%)
  blocking collectives  26.2 us (27%)
  Pallas kernels  12.9 us (13%)
  waiting for transfers between devices  11.6 us (12%)
  local copies, waits for them, and re-layouts  5.6 us (6%)
    all_to_all x2, blocking collectives, exchange(): return lax.all_to_all(value, axes, 0, 0, tiled=True)  26.2 us
    ppermute x6, starting transfers between devices, neighbours(): return lax.ppermute(value, tok, pairs)  24.7 us
    ppermute x3, starting transfers between devices, other_core(): return lax.ppermute(value, 'core', [(0, 1), (1, 0)])  13.9 us
    pallas_call x3, Pallas kernels, call_relation(): call(functools.partial(relation_kernel, T_AT[rel], S_AT[rel], S_OFF[rel])...  10.2 us
    ppermute x6, waiting for transfers between devices, neighbours(): return lax.ppermute(value, tok, pairs)  9.1 us
    unnamed x16, local copies, waits for them, and re-layouts  5.6 us
    ppermute x3, waiting for transfers between devices, other_core(): return lax.ppermute(value, 'core', [(0, 1), (1, 0)])  2.47 us
  transfers between devices with their start and end apart: 9, of which 4 were waited for; matrix products, arithmetic and copies ran while one was open for 0% of the time, Pallas kernels for 8%

profile of v3, /device:TPU:1, one launch (start us, length us, event | category | flops | bytes accessed | tf_op | source)
XLA Modules:
  0.0 95.8 jit_solution(17727929875314447835)
XLA Ops:
  0.6 0.0 copy-start
  0.7 1.0 %copy-done = bf16[128,1280]{1,0:T(8,128)(2,1)S(1)} copy-done((bf16[128,1280]{1,0:T(8,128)(2,1)S(1)}, bf16[128,1280]{1,0:T(8,128)(2,1)}, u32[]{:S(2)}) %copy-start) | copy-done | bytes 327704
  1.6 1.0 %copy-done.1 = bf16[128,1280]{1,0:T(8,128)(2,1)S(1)} copy-done((bf16[128,1280]{1,0:T(8,128)(2,1)S(1)}, bf16[128,1280]{1,0:T(8,128)(2,1)}, u32[]{:S(2)}) %copy-start.1) | copy-done | bytes 327704
  2.6 1.0 %copy-done.2 = bf16[128,1280]{1,0:T(8,128)(2,1)S(1)} copy-done((bf16[128,1280]{1,0:T(8,128)(2,1)S(1)}, bf16[128,1280]{1,0:T(8,128)(2,1)}, u32[]{:S(2)}) %copy-start.2) | copy-done | bytes 327704
  3.6 0.9 copy-done.3
  4.5 0.9 copy-done.4
  5.4 0.9 copy-done.5
  6.2 0.3 shard_map.112
  6.5 8.8 %collective-permute-start = (bf16[128,1664]{1,0:T(8,128)(2,1)S(1)}, bf16[128,1664]{1,0:T(8,128)(2,1)S(1)}, u32[]{:S(2)}, u32[]{:S(2)}) collective-permute-start(bf16[128,1664]{1,0:T(8,128)(2,1)S(1)} %get-tuple-element.41), channel_id=1, source_target_pairs={{0,4},{4,0},{1,5},{5,1},{2,6},{6,2},{3,7},{7,3},{8,12},{12,8},{9,1... | collective-permute-start | bytes 1277960 | tf_op jit(solution)/shard_map/ppermute | solution.py:401
  15.3 1.4 %collective-permute-done.recv = bf16[128,1664]{1,0:T(8,128)(2,1)S(1)} collective-permute-done((bf16[128,1664]{1,0:T(8,128)(2,1)S(1)}, bf16[128,1664]{1,0:T(8,128)(2,1)S(1)}, u32[]{:S(2)}, u32[]{:S(2)}) %collective-permute-start) | collective-permute-done | bytes 426016 | tf_op jit(solution)/shard_map/ppermute | solution.py:401
  16.7 0.1 shard_map.113
  16.8 8.2 %collective-permute-start.1 = (bf16[192,1664]{1,0:T(8,128)(2,1)S(1)}, bf16[192,1664]{1,0:T(8,128)(2,1)S(1)}, u32[]{:S(2)}, u32[]{:S(2)}) collective-permute-start(bf16[192,1664]{1,0:T(8,128)(2,1)S(1)} %get-tuple-element.42), channel_id=1, source_target_pairs={{0,8},{4,508},{8,16},{12,4},{16,24},{20,12},{24,32},{28,20},{32,40... | collective-permute-start | bytes 1916936 | tf_op jit(solution)/shard_map/ppermute | solution.py:406
  25.0 1.9 %collective-permute-start.2 = (bf16[192,1664]{1,0:T(8,128)(2,1)S(1)}, bf16[192,1664]{1,0:T(8,128)(2,1)S(1)}, u32[]{:S(2)}, u32[]{:S(2)}) collective-permute-start(bf16[192,1664]{1,0:T(8,128)(2,1)S(1)} %get-tuple-element.47), channel_id=1, source_target_pairs={{0,504},{4,12},{8,0},{12,20},{16,8},{20,28},{24,16},{28,36},{32,24... | collective-permute-start | bytes 1916936 | tf_op jit(solution)/shard_map/ppermute | solution.py:406
  26.9 2.6 %collective-permute-start.3 = (bf16[128,896]{1,0:T(8,128)(2,1)S(1)}, bf16[128,896]{1,0:T(8,128)(2,1)S(1)}, u32[]{:S(2)}, u32[]{:S(2)}) collective-permute-start(bf16[128,896]{1,0:T(8,128)(2,1)S(1)} %get-tuple-element.51), channel_id=1, source_target_pairs={{0,4},{4,0},{1,5},{5,1},{2,6},{6,2},{3,7},{7,3},{8,12},{12,8},{9,1... | collective-permute-start | bytes 688136 | tf_op jit(solution)/shard_map/ppermute | solution.py:401
  29.5 1.1 %collective-permute-done.3.recv = bf16[128,896]{1,0:T(8,128)(2,1)S(1)} collective-permute-done((bf16[128,896]{1,0:T(8,128)(2,1)S(1)}, bf16[128,896]{1,0:T(8,128)(2,1)S(1)}, u32[]{:S(2)}, u32[]{:S(2)}) %collective-permute-start.3) | collective-permute-done | bytes 229408 | tf_op jit(solution)/shard_map/ppermute | solution.py:401
  30.6 5.7 %collective-permute-done.1.one = bf16[192,1664]{1,0:T(8,128)(2,1)S(1)} collective-permute-done((bf16[192,1664]{1,0:T(8,128)(2,1)S(1)}, bf16[192,1664]{1,0:T(8,128)(2,1)S(1)}, u32[]{:S(2)}, u32[]{:S(2)}) %collective-permute-start.1) | collective-permute-done | bytes 639008 | tf_op jit(solution)/shard_map/ppermute | solution.py:406
  36.3 0.9 shard_map.117
  37.2 7.4 %collective-permute-start.4 = (bf16[192,896]{1,0:T(8,128)(2,1)}, bf16[192,896]{1,0:T(8,128)(2,1)}, u32[]{:S(2)}, u32[]{:S(2)}) collective-permute-start(bf16[192,896]{1,0:T(8,128)(2,1)} %get-tuple-element.54), channel_id=1, source_target_pairs={{0,8},{4,508},{8,16},{12,4},{16,24},{20,12},{24,32},{28,20},{32,40... | collective-permute-start | bytes 1032200 | tf_op jit(solution)/shard_map/ppermute | solution.py:406
  44.7 1.9 %collective-permute-start.5 = (bf16[192,896]{1,0:T(8,128)(2,1)}, bf16[192,896]{1,0:T(8,128)(2,1)}, u32[]{:S(2)}, u32[]{:S(2)}) collective-permute-start(bf16[192,896]{1,0:T(8,128)(2,1)} %get-tuple-element.55), channel_id=1, source_target_pairs={{0,504},{4,12},{8,0},{12,20},{16,8},{20,28},{24,16},{28,36},{32,24... | collective-permute-start | bytes 1032200 | tf_op jit(solution)/shard_map/ppermute | solution.py:406
  46.6 0.2 shard_map.114
  46.9 3.0 %shard_map.115 = (bf16[192,256]{1,0:T(8,128)(2,1)S(1)}, f32[256,256]{1,0:T(8,128)S(1)}, bf16[192,256]{1,0:T(8,128)(2,1)S(1)}, f32[1,128]{1,0:T(1,128)S(1)}) custom-call(s32[1]{0:T(128)} %bitcast.core, s32[1,256]{1,0:T(1,128)S(1)} %get-tuple-element.45.starts, f32[1,256]{1,0:T(1,128)S(1)} %get-tuple-element.46.weights, f32[1,128]{1,0:T(1,128)S(1)} %shard_map.111._.loss_in, ...), custom_call_target="tpu_custom_call" | custom-call | flops 1342177280 | bytes 2097152 | tf_op jit(solution)/shard_map/pallas_call | solution.py:368
  49.9 3.0 %shard_map.116 = (bf16[192,256]{1,0:T(8,128)(2,1)S(1)}, f32[256,256]{1,0:T(8,128)S(1)}, bf16[192,256]{1,0:T(8,128)(2,1)S(1)}, f32[1,128]{1,0:T(1,128)S(1)}) custom-call(s32[1]{0:T(128)} %bitcast.core, s32[1,256]{1,0:T(1,128)S(1)} %get-tuple-element.45.starts, f32[1,256]{1,0:T(1,128)S(1)} %get-tuple-element.46.weights, ...), custom_call_target="tpu_custom_call" | custom-call | flops 1342177280 | bytes 2097152 | tf_op jit(solution)/shard_map/pallas_call | solution.py:368
  53.0 3.3 %collective-permute-done.5.two = bf16[192,896]{1,0:T(8,128)(2,1)} collective-permute-done((bf16[192,896]{1,0:T(8,128)(2,1)}, bf16[192,896]{1,0:T(8,128)(2,1)}, u32[]{:S(2)}, u32[]{:S(2)}) %collective-permute-start.5) | collective-permute-done | bytes 344096 | tf_op jit(solution)/shard_map/ppermute | solution.py:406
  56.3 4.1 %shard_map.118 = (bf16[192,256]{1,0:T(8,128)(2,1)S(1)}, f32[256,256]{1,0:T(8,128)S(1)}, bf16[192,256]{1,0:T(8,128)(2,1)S(1)}, f32[1,128]{1,0:T(1,128)S(1)}) custom-call(s32[1]{0:T(128)} %bitcast.core, s32[1,256]{1,0:T(1,128)S(1)} %get-tuple-element.45.starts, f32[1,256]{1,0:T(1,128)S(1)} %get-tuple-element.46.weights, ...), custom_call_target="tpu_custom_call" | custom-call | flops 1342177280 | bytes 2097152 | tf_op jit(solution)/shard_map/pallas_call | solution.py:368
  60.4 0.1 shard_map.119
  60.5 3.4 %collective-permute-start.6 = (bf16[192,768]{1,0:T(8,128)(2,1)S(1)}, bf16[192,768]{1,0:T(8,128)(2,1)S(1)}, u32[]{:S(2)}, u32[]{:S(2)}) collective-permute-start(bf16[192,768]{1,0:T(8,128)(2,1)S(1)} %get-tuple-element.67), channel_id=1, source_target_pairs={{0,8},{4,508},{8,16},{12,4},{16,24},{20,12},{24,32},{28,20},{32,40... | collective-permute-start | bytes 884744 | tf_op jit(solution)/shard_map/ppermute | solution.py:406
  63.8 1.9 %collective-permute-start.7 = (bf16[192,768]{1,0:T(8,128)(2,1)S(1)}, bf16[192,768]{1,0:T(8,128)(2,1)S(1)}, u32[]{:S(2)}, u32[]{:S(2)}) collective-permute-start(bf16[192,768]{1,0:T(8,128)(2,1)S(1)} %get-tuple-element.68), channel_id=1, source_target_pairs={{0,504},{4,12},{8,0},{12,20},{16,8},{20,28},{24,16},{28,36},{32,24... | collective-permute-start | bytes 884744 | tf_op jit(solution)/shard_map/ppermute | solution.py:406
  65.8 10.7 %all_to_all.22 = f32[16,1,128]{2,1,0:T(1,128)S(1)} all-to-all(f32[16,1,128]{2,1,0:T(1,128)S(1)} %bitcast.18), channel_id=1, replica_groups=mesh['y'=8,'z'=4,'parity'=2,'core'=2,'head'=4] {'z','parity','core'}, dimensions={0} | all-to-all | bytes 16384 | tf_op jit(solution)/shard_map/all_to_all | solution.py:448
  76.5 0.2 shard_map.120
  76.8 2.6 %collective-permute-start.8 = (f32[128,768]{1,0:T(8,128)S(1)}, f32[128,768]{1,0:T(8,128)S(1)}, u32[]{:S(2)}, u32[]{:S(2)}) collective-permute-start(f32[128,768]{1,0:T(8,128)S(1)} %get-tuple-element.71), channel_id=1, source_target_pairs={{0,4},{4,0},{1,5},{5,1},{2,6},{6,2},{3,7},{7,3},{8,12},{12,8},{9,1... | collective-permute-start | bytes 1179656 | tf_op jit(solution)/shard_map/ppermute | solution.py:401
  79.4 15.4 %all_to_all.23 = f32[32,1,128]{2,1,0:T(1,128)S(1)} all-to-all(f32[32,1,128]{2,1,0:T(1,128)S(1)} %bitcast.17), channel_id=1, replica_groups=mesh['y'=8,'z'=4,'parity'=2,'core'=2,'head'=4] {'y','head'}, dimensions={0} | all-to-all | bytes 32768 | tf_op jit(solution)/shard_map/all_to_all | solution.py:448
  94.8 1.0 shard_map.121
  (15 shorter events, 0.0 us)
Async XLA Ops:
  0.6 1.0 %copy-start = (bf16[128,1280]{1,0:T(8,128)(2,1)S(1)}, bf16[128,1280]{1,0:T(8,128)(2,1)}, u32[]{:S(2)}) copy-start(bf16[128,1280]{1,0:T(8,128)(2,1)} %tq.1) | copy-start | bytes 983044
  1.6 1.0 %copy-start.1 = (bf16[128,1280]{1,0:T(8,128)(2,1)S(1)}, bf16[128,1280]{1,0:T(8,128)(2,1)}, u32[]{:S(2)}) copy-start(bf16[128,1280]{1,0:T(8,128)(2,1)} %tk.1) | copy-start | bytes 983044
  2.6 1.0 %copy-start.2 = (bf16[128,1280]{1,0:T(8,128)(2,1)S(1)}, bf16[128,1280]{1,0:T(8,128)(2,1)}, u32[]{:S(2)}) copy-start(bf16[128,1280]{1,0:T(8,128)(2,1)} %tv.1) | copy-start | bytes 983044
  3.6 0.9 copy-start.3
  4.5 0.9 copy-start.4
  5.4 0.9 copy-start.5
  6.5 10.2 %collective-permute-start = (bf16[128,1664]{1,0:T(8,128)(2,1)S(1)}, bf16[128,1664]{1,0:T(8,128)(2,1)S(1)}, u32[]{:S(2)}, u32[]{:S(2)}) collective-permute-start(bf16[128,1664]{1,0:T(8,128)(2,1)S(1)} %get-tuple-element.41), channel_id=1, source_target_pairs={{0,4},{4,0},{1,5},{5,1},{2,6},{6,2},{3,7},{7,3},{8,12},{12,8},{9,1... | collective-permute-start | bytes 1277960 | tf_op jit(solution)/shard_map/ppermute | solution.py:401
  16.8 19.6 %collective-permute-start.1 = (bf16[192,1664]{1,0:T(8,128)(2,1)S(1)}, bf16[192,1664]{1,0:T(8,128)(2,1)S(1)}, u32[]{:S(2)}, u32[]{:S(2)}) collective-permute-start(bf16[192,1664]{1,0:T(8,128)(2,1)S(1)} %get-tuple-element.42), channel_id=1, source_target_pairs={{0,8},{4,508},{8,16},{12,4},{16,24},{20,12},{24,32},{28,20},{32,40... | collective-permute-start | bytes 1916936 | tf_op jit(solution)/shard_map/ppermute | solution.py:406
  25.0 21.9 %collective-permute-start.2 = (bf16[192,1664]{1,0:T(8,128)(2,1)S(1)}, bf16[192,1664]{1,0:T(8,128)(2,1)S(1)}, u32[]{:S(2)}, u32[]{:S(2)}) collective-permute-start(bf16[192,1664]{1,0:T(8,128)(2,1)S(1)} %get-tuple-element.47), channel_id=1, source_target_pairs={{0,504},{4,12},{8,0},{12,20},{16,8},{20,28},{24,16},{28,36},{32,24... | collective-permute-start | bytes 1916936 | tf_op jit(solution)/shard_map/ppermute | solution.py:406
  26.9 3.7 %collective-permute-start.3 = (bf16[128,896]{1,0:T(8,128)(2,1)S(1)}, bf16[128,896]{1,0:T(8,128)(2,1)S(1)}, u32[]{:S(2)}, u32[]{:S(2)}) collective-permute-start(bf16[128,896]{1,0:T(8,128)(2,1)S(1)} %get-tuple-element.51), channel_id=1, source_target_pairs={{0,4},{4,0},{1,5},{5,1},{2,6},{6,2},{3,7},{7,3},{8,12},{12,8},{9,1... | collective-permute-start | bytes 688136 | tf_op jit(solution)/shard_map/ppermute | solution.py:401
  36.3 10.3 %copy-start.6 = (s32[16384]{0:T(1024)S(1)}, s32[16384]{0:T(1024)}, u32[]{:S(2)}) copy-start(s32[16384]{0:T(1024)} %param.14) | copy-start | bytes 196612
  36.3 10.3 %copy-start.7 = (f32[16384]{0:T(1024)S(1)}, f32[16384]{0:T(1024)}, u32[]{:S(2)}) copy-start(f32[16384]{0:T(1024)} %param.15) | copy-start | bytes 196612
  37.2 15.7 %collective-permute-start.4 = (bf16[192,896]{1,0:T(8,128)(2,1)}, bf16[192,896]{1,0:T(8,128)(2,1)}, u32[]{:S(2)}, u32[]{:S(2)}) collective-permute-start(bf16[192,896]{1,0:T(8,128)(2,1)} %get-tuple-element.54), channel_id=1, source_target_pairs={{0,8},{4,508},{8,16},{12,4},{16,24},{20,12},{24,32},{28,20},{32,40... | collective-permute-start | bytes 1032200 | tf_op jit(solution)/shard_map/ppermute | solution.py:406
  44.7 11.6 %collective-permute-start.5 = (bf16[192,896]{1,0:T(8,128)(2,1)}, bf16[192,896]{1,0:T(8,128)(2,1)}, u32[]{:S(2)}, u32[]{:S(2)}) collective-permute-start(bf16[192,896]{1,0:T(8,128)(2,1)} %get-tuple-element.55), channel_id=1, source_target_pairs={{0,504},{4,12},{8,0},{12,20},{16,8},{20,28},{24,16},{28,36},{32,24... | collective-permute-start | bytes 1032200 | tf_op jit(solution)/shard_map/ppermute | solution.py:406
  60.5 16.0 %collective-permute-start.6 = (bf16[192,768]{1,0:T(8,128)(2,1)S(1)}, bf16[192,768]{1,0:T(8,128)(2,1)S(1)}, u32[]{:S(2)}, u32[]{:S(2)}) collective-permute-start(bf16[192,768]{1,0:T(8,128)(2,1)S(1)} %get-tuple-element.67), channel_id=1, source_target_pairs={{0,8},{4,508},{8,16},{12,4},{16,24},{20,12},{24,32},{28,20},{32,40... | collective-permute-start | bytes 884744 | tf_op jit(solution)/shard_map/ppermute | solution.py:406
  63.8 12.7 %collective-permute-start.7 = (bf16[192,768]{1,0:T(8,128)(2,1)S(1)}, bf16[192,768]{1,0:T(8,128)(2,1)S(1)}, u32[]{:S(2)}, u32[]{:S(2)}) collective-permute-start(bf16[192,768]{1,0:T(8,128)(2,1)S(1)} %get-tuple-element.68), channel_id=1, source_target_pairs={{0,504},{4,12},{8,0},{12,20},{16,8},{20,28},{24,16},{28,36},{32,24... | collective-permute-start | bytes 884744 | tf_op jit(solution)/shard_map/ppermute | solution.py:406
  76.8 18.0 %collective-permute-start.8 = (f32[128,768]{1,0:T(8,128)S(1)}, f32[128,768]{1,0:T(8,128)S(1)}, u32[]{:S(2)}, u32[]{:S(2)}) collective-permute-start(f32[128,768]{1,0:T(8,128)S(1)} %get-tuple-element.71), channel_id=1, source_target_pairs={{0,4},{4,0},{1,5},{5,1},{2,6},{6,2},{3,7},{7,3},{8,12},{12,8},{9,1... | collective-permute-start | bytes 1179656 | tf_op jit(solution)/shard_map/ppermute | solution.py:401

commit v4 on v3

--- a/solution.py
+++ b/solution.py
@@ -34,6 +34,7 @@
 FAR = 4096
 VMEM = pl.BlockSpec(memory_space=pltpu.VMEM)
 SMEM = pl.BlockSpec(memory_space=pltpu.SMEM)
+HBM = pl.BlockSpec(memory_space=pltpu.HBM)
 F32 = jnp.float32
 BF16 = jnp.bfloat16
 
@@ -50,13 +51,22 @@
     )
 
 
-def zero_kernel(loss):
-    loss[...] = jnp.zeros_like(loss)
-
-
-def split_kernel(core, _, tq, tk, tv, sq, sk, sv, send_a, keep_a, send_b, keep_b):
+def split_kernel(core, *refs):
+    arrays, (send_a, keep_a, send_b, keep_b), buffers, sems = (
+        refs[:6],
+        refs[6:10],
+        refs[10:16],
+        refs[16],
+    )
     me = core[0]
-    buffers = (tq, tk, tv, sq, sk, sv)
+    copies = [
+        pltpu.make_async_copy(array, buffer, sems.at[i])
+        for i, (array, buffer) in enumerate(zip(arrays, buffers))
+    ]
+    for copy in copies:
+        copy.start()
+    for copy in copies:
+        copy.wait()
     lane = lax.broadcasted_iota(jnp.int32, (BLOCK, SP), 1)
     mine = pl.ds(pl.multiple_of(me * TW, 128), TW)
     other = pl.ds(pl.multiple_of((1 - me) * TW, 128), TW)
@@ -126,6 +136,22 @@
         write(recv, keep, two, one)
 
 
+def rest_kernel(core, keep, recv, one, two):
+    half = HALO - BLOCK
+
+    @pl.when(core[0] == 0)
+    def _():
+        one[:half, :] = keep[BLOCK - half :, :]
+        one[half:, :] = recv[...]
+        two[...] = recv[:half, :]
+
+    @pl.when(core[0] != 0)
+    def _():
+        one[:BLOCK, :] = recv[...]
+        one[BLOCK:, :] = keep[:half, :]
+        two[...] = recv[BLOCK - half :, :]
+
+
 def fold(value, op):
     rows, lanes = value.shape
     return op(value.reshape(rows // 8, 8, lanes), axis=0)
@@ -139,41 +165,35 @@
     starts,
     weights,
     loss_in,
-    keep,
-    recv,
-    one,
-    two,
-    grad_left,
-    grad_own,
-    grad_right,
-    loss_out,
-    win,
-    bias,
-    rt,
-    rs,
-    gt,
-    qs,
-    bt,
-    kg,
+    *refs,
 ):
+    keep, recv, *halo = refs[:-12]
+    grad_left, grad_own, grad_right, loss_out, win, bias, rt, rs, gt, qs, bt, kg = refs[-12:]
     me = core[0]
     def gather(at, rows, source):
         win[at : at + rows, :TW] = source[:, t_at : t_at + TW]
         win[at : at + rows, TW:] = source[:, s_at : s_at + SP]
 
+    def gather_all(*sources):
+        at = 0
+        for source in sources:
+            gather(at, source.shape[0], source)
+            at += source.shape[0]
+
+    if len(halo) == 2:
+        one, two = halo
+        order = (one, keep, recv, two), (two, recv, keep, one)
+    else:
+        own, one, two = halo
+        order = (one, keep, recv, own, two), (two, own, recv, keep, one)
+
     @pl.when(me == 0)
     def _():
-        gather(0, HALO, one)
-        gather(HALO, BLOCK, keep)
-        gather(HALO + BLOCK, BLOCK, recv)
-        gather(HALO + OWN, HALO, two)
+        gather_all(*order[0])
 
     @pl.when(me != 0)
     def _():
-        gather(0, HALO, two)
-        gather(HALO, BLOCK, recv)
-        gather(HALO + BLOCK, BLOCK, keep)
-        gather(HALO + OWN, HALO, one)
+        gather_all(*order[1])
 
     key = lax.broadcasted_iota(jnp.int32, (WINDOW, OWN), 0)
     query = lax.broadcasted_iota(jnp.int32, (WINDOW, OWN), 1) + FIRST_QUERY
@@ -373,7 +393,7 @@
             shape(HALO, SP, BF16),
             shape(1, BLOCK, F32),
         ],
-        [SMEM] + [VMEM] * 7,
+        [SMEM] + [VMEM] * (3 + len(chunk)),
         scratch=[
             pltpu.VMEM((WINDOW, REL), BF16),
             pltpu.VMEM((WINDOW, OWN), F32),
@@ -405,26 +425,33 @@
         pairs = [(i, (i + step[i % 2]) % count) for i in range(count)]
         return lax.ppermute(value, tok, pairs)
 
-    loss = call(zero_kernel, shape(1, BLOCK, F32), [], moved=32 << 20)()
+    arrays = (teacher_q, teacher_k, teacher_v, student_q, student_k, student_v)
     send_a, keep_a, send_b, keep_b = call(
         split_kernel,
         [shape(BLOCK, WIDTH_A, BF16)] * 2 + [shape(BLOCK, REL, BF16)] * 2,
-        [SMEM] + [VMEM] * 7,
+        [SMEM] + [HBM] * 6,
+        scratch=[pltpu.VMEM(a.shape, BF16) for a in arrays] + [pltpu.SemaphoreType.DMA((6,))],
         moved=4 << 20,
-    )(core, loss, teacher_q, teacher_k, teacher_v, student_q, student_k, student_v)
+        limit=56,
+    )(core, *arrays)
     recv_a = other_core(send_a)
     recv_b = other_core(send_b)
-    edges_a = call(edges_kernel, [shape(HALO, WIDTH_A, BF16)] * 2, [SMEM] + [VMEM] * 2, moved=2 << 20)(
-        core, keep_a, recv_a
-    )
-    halo_a = [neighbours(edges_a[0], 1), neighbours(edges_a[1], -1)]
-    keep_b, recv_b, _ = lax.optimization_barrier((keep_b, recv_b, halo_a[0]))
+    own_a = neighbours(keep_a, -1)
+    recv_a, recv_b, own_a = lax.optimization_barrier((recv_a, recv_b, own_a))
+    halo_a = [own_a]
+    rest_a = call(
+        rest_kernel,
+        [shape(HALO, WIDTH_A, BF16), shape(HALO - BLOCK, WIDTH_A, BF16)],
+        [SMEM] + [VMEM] * 2,
+        moved=2 << 20,
+    )(core, keep_a, recv_a)
+    halo_a += [neighbours(rest_a[0], 1), neighbours(rest_a[1], -1)]
     edges_b = call(edges_kernel, [shape(HALO, REL, BF16)] * 2, [SMEM] + [VMEM] * 2, moved=1 << 20)(
         core, keep_b, recv_b
     )
     halo_b = [neighbours(edges_b[0], 1), neighbours(edges_b[1], -1)]
 
-    doc_ids, row_weight, _ = lax.optimization_barrier((doc_ids, row_weight, edges_a[0]))
+    doc_ids, row_weight, _ = lax.optimization_barrier((doc_ids, row_weight, rest_a[0]))
     starts, weight = call(
         mask_kernel,
         [shape(1, OWN, jnp.int32), shape(1, OWN, F32)],
@@ -435,6 +462,7 @@
         doc_ids.reshape(-1, BLOCK),
         row_weight.reshape(-1, BLOCK),
     )
+    loss = jnp.zeros((1, BLOCK), F32)
     grads = []
     for rel in range(3):
         chunk = (keep_b, recv_b, *halo_b) if rel == 2 else (keep_a, recv_a, *halo_a)

time: 96.4 us -> 96.5 us (level)
  waiting for transfers between devices: 11.6 us -> 5.77 us
  Pallas kernels: 12.9 us -> 17.7 us
  local copies, waits for them, and re-layouts: 5.6 us -> 1.03 us
  blocking collectives: 26.2 us -> 30 us
  starting transfers between devices: 38.7 us -> 40.6 us
    ppermute x6 -> x7, waiting for transfers between devices: 9.1 us -> 4.1 us  [neighbours(): return lax.ppermute(value, tok, pairs)]
    unnamed x16 -> x10, local copies, waits for them, and re-layouts: 5.6 us -> 1.02 us
    all_to_all x2, blocking collectives: 26.2 us -> 30 us  [exchange(): return lax.all_to_all(value, axes, 0, 0, tiled=True)]
    ppermute x3, starting transfers between devices: 13.9 us -> 16.9 us  [other_core(): return lax.ppermute(value, 'core', [(0, 1), (1, 0)])]
    pallas_call x1, Pallas kernels: 0.26 us -> 2.6 us  [body(): call(split_kernel, [shape(BLOCK, WIDTH_A, BF16)] * 2 + [shape(BLOCK, REL,...]
    pallas_call x3, Pallas kernels: 10.2 us -> 11.9 us  [call_relation(): call(functools.partial(relation_kernel, T_AT[rel], S_AT[rel], S_OFF[rel])...]
    ppermute x6 -> x7, starting transfers between devices: 24.7 us -> 23.6 us  [neighbours(): return lax.ppermute(value, tok, pairs)]
  transfers between devices with their start and end apart: 9 -> 10, of which waited for: 4 -> 3; matrix products, arithmetic and copies ran while one was open for 0% -> 0% of each run, Pallas kernels for 8% -> 9%
where the time goes in v4:
time: 96.5 us; the launch traced here: 95.9 us
  starting transfers between devices  40.6 us (42%)
  blocking collectives  30 us (31%)
  Pallas kernels  17.7 us (18%)
  waiting for transfers between devices  5.77 us (6%)
  local copies, waits for them, and re-layouts  1.03 us (1%)
    all_to_all x2, blocking collectives, exchange(): return lax.all_to_all(value, axes, 0, 0, tiled=True)  30 us
    ppermute x7, starting transfers between devices, neighbours(): return lax.ppermute(value, tok, pairs)  23.6 us
    ppermute x3, starting transfers between devices, other_core(): return lax.ppermute(value, 'core', [(0, 1), (1, 0)])  16.9 us
    pallas_call x3, Pallas kernels, call_relation(): call(functools.partial(relation_kernel, T_AT[rel], S_AT[rel], S_OFF[rel])...  11.9 us
    ppermute x7, waiting for transfers between devices, neighbours(): return lax.ppermute(value, tok, pairs)  4.1 us
    pallas_call x1, Pallas kernels, body(): call(split_kernel, [shape(BLOCK, WIDTH_A, BF16)] * 2 + [shape(BLOCK, REL,...  2.6 us
  transfers between devices with their start and end apart: 10, of which 3 were waited for; matrix products, arithmetic and copies ran while one was open for 0% of the time, Pallas kernels for 9%

profile of v4, /device:TPU:1, one launch (start us, length us, event | category | flops | bytes accessed | tf_op | source)
XLA Modules:
  0.0 95.9 jit_solution(14472307678838219441)
XLA Ops:
  0.6 2.6 %shard_map.111 = (bf16[128,1664]{1,0:T(8,128)(2,1)}, bf16[128,1664]{1,0:T(8,128)(2,1)}, bf16[128,896]{1,0:T(8,128)(2,1)}, bf16[128,896]{1,0:T(8,128)(2,1)}) custom-call(s32[1]{0:T(128)} %bitcast.core, bf16[128,1280]{1,0:T(8,128)(2,1)} %refs_0_.1, bf16[128,1280]{1,0:T(8,128)(2,1)} %refs_1_.1, bf16[128,1280]{1,0:T(8,128)(2,1)} %refs_2_.1, ...), custom_call_target="tpu_custom_call" | custom-call | bytes 4194304 | tf_op jit(solution)/shard_map/pallas_call | solution.py:429
  3.2 4.8 %collective-permute-start.2 = (bf16[128,1664]{1,0:T(8,128)(2,1)}, bf16[128,1664]{1,0:T(8,128)(2,1)S(1)}, u32[]{:S(2)}, u32[]{:S(2)}) collective-permute-start(bf16[128,1664]{1,0:T(8,128)(2,1)} %get-tuple-element.41.keep.refs_0_), channel_id=1, source_target_pairs={{0,504},{4,12},{8,0},{12,20},{16,8},{20,28},{24,16},{28,36},{32,24... | collective-permute-start | bytes 1277960 | tf_op jit(solution)/shard_map/ppermute | solution.py:426
  8.1 12.4 %collective-permute-start = (bf16[128,1664]{1,0:T(8,128)(2,1)}, bf16[128,1664]{1,0:T(8,128)(2,1)S(1)}, u32[]{:S(2)}, u32[]{:S(2)}) collective-permute-start(bf16[128,1664]{1,0:T(8,128)(2,1)} %get-tuple-element.42), channel_id=1, source_target_pairs={{0,4},{4,0},{1,5},{5,1},{2,6},{6,2},{3,7},{7,3},{8,12},{12,8},{9,1... | collective-permute-start | bytes 1277960 | tf_op jit(solution)/shard_map/ppermute | solution.py:421
  20.5 1.9 %collective-permute-start.1 = (bf16[128,896]{1,0:T(8,128)(2,1)}, bf16[128,896]{1,0:T(8,128)(2,1)S(1)}, u32[]{:S(2)}, u32[]{:S(2)}) collective-permute-start(bf16[128,896]{1,0:T(8,128)(2,1)} %get-tuple-element.43), channel_id=1, source_target_pairs={{0,4},{4,0},{1,5},{5,1},{2,6},{6,2},{3,7},{7,3},{8,12},{12,8},{9,1... | collective-permute-start | bytes 688136 | tf_op jit(solution)/shard_map/ppermute | solution.py:421
  22.5 1.7 %collective-permute-done.1.recv.refs_1_ = bf16[128,896]{1,0:T(8,128)(2,1)S(1)} collective-permute-done((bf16[128,896]{1,0:T(8,128)(2,1)}, bf16[128,896]{1,0:T(8,128)(2,1)S(1)}, u32[]{:S(2)}, u32[]{:S(2)}) %collective-permute-start.1) | collective-permute-done | bytes 229408 | tf_op jit(solution)/shard_map/ppermute | solution.py:421
  24.1 0.0 collective-permute-done.2.refs_2_
  24.1 0.0 collective-permute-done.recv.refs_1_
  24.1 1.0 %copy-done = bf16[128,1664]{1,0:T(8,128)(2,1)S(1)} copy-done((bf16[128,1664]{1,0:T(8,128)(2,1)S(1)}, bf16[128,1664]{1,0:T(8,128)(2,1)}, u32[]{:S(2)}) %copy-start) | copy-done | bytes 426008
  25.1 0.8 shard_map.112
  25.9 3.0 %collective-permute-start.3 = (bf16[192,1664]{1,0:T(8,128)(2,1)S(1)}, bf16[192,1664]{1,0:T(8,128)(2,1)S(1)}, u32[]{:S(2)}, u32[]{:S(2)}) collective-permute-start(bf16[192,1664]{1,0:T(8,128)(2,1)S(1)} %get-tuple-element.45), channel_id=1, source_target_pairs={{0,8},{4,508},{8,16},{12,4},{16,24},{20,12},{24,32},{28,20},{32,40... | collective-permute-start | bytes 1916936 | tf_op jit(solution)/shard_map/ppermute | solution.py:426
  28.9 2.4 %collective-permute-start.4 = (bf16[64,1664]{1,0:T(8,128)(2,1)}, bf16[64,1664]{1,0:T(8,128)(2,1)}, u32[]{:S(2)}, u32[]{:S(2)}) collective-permute-start(bf16[64,1664]{1,0:T(8,128)(2,1)} %get-tuple-element.51), channel_id=1, source_target_pairs={{0,504},{4,12},{8,0},{12,20},{16,8},{20,28},{24,16},{28,36},{32,24... | collective-permute-start | bytes 638984 | tf_op jit(solution)/shard_map/ppermute | solution.py:426
  31.3 0.0 copy-start.3
  31.4 0.9 shard_map.116
  32.3 6.2 %collective-permute-start.5 = (bf16[192,896]{1,0:T(8,128)(2,1)}, bf16[192,896]{1,0:T(8,128)(2,1)S(1)}, u32[]{:S(2)}, u32[]{:S(2)}) collective-permute-start(bf16[192,896]{1,0:T(8,128)(2,1)} %get-tuple-element.56), channel_id=1, source_target_pairs={{0,8},{4,508},{8,16},{12,4},{16,24},{20,12},{24,32},{28,20},{32,40... | collective-permute-start | bytes 1032200 | tf_op jit(solution)/shard_map/ppermute | solution.py:426
  38.5 1.9 %collective-permute-start.6 = (bf16[192,896]{1,0:T(8,128)(2,1)}, bf16[192,896]{1,0:T(8,128)(2,1)}, u32[]{:S(2)}, u32[]{:S(2)}) collective-permute-start(bf16[192,896]{1,0:T(8,128)(2,1)} %get-tuple-element.57), channel_id=1, source_target_pairs={{0,504},{4,12},{8,0},{12,20},{16,8},{20,28},{24,16},{28,36},{32,24... | collective-permute-start | bytes 1032200 | tf_op jit(solution)/shard_map/ppermute | solution.py:426
  40.5 0.2 shard_map.113
  40.7 1.0 %collective-permute-done.4.refs_4_ = bf16[64,1664]{1,0:T(8,128)(2,1)} collective-permute-done((bf16[64,1664]{1,0:T(8,128)(2,1)}, bf16[64,1664]{1,0:T(8,128)(2,1)}, u32[]{:S(2)}, u32[]{:S(2)}) %collective-permute-start.4) | collective-permute-done | bytes 213024 | tf_op jit(solution)/shard_map/ppermute | solution.py:426
  41.7 0.0 collective-permute-done.3.refs_3_
  41.7 4.0 %shard_map.114 = (bf16[192,256]{1,0:T(8,128)(2,1)S(1)}, f32[256,256]{1,0:T(8,128)S(1)}, bf16[192,256]{1,0:T(8,128)(2,1)S(1)}, f32[1,128]{1,0:T(1,128)S(1)}) custom-call(s32[1]{0:T(128)} %bitcast.core, s32[1,256]{1,0:T(1,128)S(1)} %get-tuple-element.48.starts, f32[1,256]{1,0:T(1,128)S(1)} %get-tuple-element.49.weights, f32[1,128]{1,0:T(1,128)S(1)} %broadcast_in_dim.3.loss_in, ...), custom_call_target="tpu_custom_call" | custom-call | flops 1342177280 | bytes 2097152 | tf_op jit(solution)/shard_map/pallas_call | solution.py:388
  45.7 3.9 %shard_map.115 = (bf16[192,256]{1,0:T(8,128)(2,1)S(1)}, f32[256,256]{1,0:T(8,128)S(1)}, bf16[192,256]{1,0:T(8,128)(2,1)S(1)}, f32[1,128]{1,0:T(1,128)S(1)}) custom-call(s32[1]{0:T(128)} %bitcast.core, s32[1,256]{1,0:T(1,128)S(1)} %get-tuple-element.48.starts, f32[1,256]{1,0:T(1,128)S(1)} %get-tuple-element.49.weights, ...), custom_call_target="tpu_custom_call" | custom-call | flops 1342177280 | bytes 2097152 | tf_op jit(solution)/shard_map/pallas_call | solution.py:388
  49.6 0.0 collective-permute-done.5.refs_2_
  49.7 3.1 %collective-permute-done.6.refs_3_ = bf16[192,896]{1,0:T(8,128)(2,1)} collective-permute-done((bf16[192,896]{1,0:T(8,128)(2,1)}, bf16[192,896]{1,0:T(8,128)(2,1)}, u32[]{:S(2)}, u32[]{:S(2)}) %collective-permute-start.6) | collective-permute-done | bytes 344096 | tf_op jit(solution)/shard_map/ppermute | solution.py:426
  52.7 4.0 %shard_map.117 = (bf16[192,256]{1,0:T(8,128)(2,1)S(1)}, f32[256,256]{1,0:T(8,128)S(1)}, bf16[192,256]{1,0:T(8,128)(2,1)S(1)}, f32[1,128]{1,0:T(1,128)S(1)}) custom-call(s32[1]{0:T(128)} %bitcast.core, s32[1,256]{1,0:T(1,128)S(1)} %get-tuple-element.48.starts, f32[1,256]{1,0:T(1,128)S(1)} %get-tuple-element.49.weights, ...), custom_call_target="tpu_custom_call" | custom-call | flops 1342177280 | bytes 2097152 | tf_op jit(solution)/shard_map/pallas_call | solution.py:388
  56.8 0.1 shard_map.118
  56.8 2.6 %collective-permute-start.7 = (bf16[192,768]{1,0:T(8,128)(2,1)S(1)}, bf16[192,768]{1,0:T(8,128)(2,1)S(1)}, u32[]{:S(2)}, u32[]{:S(2)}) collective-permute-start(bf16[192,768]{1,0:T(8,128)(2,1)S(1)} %get-tuple-element.69), channel_id=1, source_target_pairs={{0,8},{4,508},{8,16},{12,4},{16,24},{20,12},{24,32},{28,20},{32,40... | collective-permute-start | bytes 884744 | tf_op jit(solution)/shard_map/ppermute | solution.py:426
  59.5 2.6 %collective-permute-start.8 = (bf16[192,768]{1,0:T(8,128)(2,1)S(1)}, bf16[192,768]{1,0:T(8,128)(2,1)S(1)}, u32[]{:S(2)}, u32[]{:S(2)}) collective-permute-start(bf16[192,768]{1,0:T(8,128)(2,1)S(1)} %get-tuple-element.70), channel_id=1, source_target_pairs={{0,504},{4,12},{8,0},{12,20},{16,8},{20,28},{24,16},{28,36},{32,24... | collective-permute-start | bytes 884744 | tf_op jit(solution)/shard_map/ppermute | solution.py:426
  62.1 15.0 %all_to_all.22 = f32[16,1,128]{2,1,0:T(1,128)S(1)} all-to-all(f32[16,1,128]{2,1,0:T(1,128)S(1)} %bitcast.18), channel_id=1, replica_groups=mesh['y'=8,'z'=4,'parity'=2,'core'=2,'head'=4] {'z','parity','core'}, dimensions={0} | all-to-all | bytes 16384 | tf_op jit(solution)/shard_map/all_to_all | solution.py:476
  77.1 0.2 shard_map.119
  77.4 2.6 %collective-permute-start.9 = (f32[128,768]{1,0:T(8,128)S(1)}, f32[128,768]{1,0:T(8,128)S(1)}, u32[]{:S(2)}, u32[]{:S(2)}) collective-permute-start(f32[128,768]{1,0:T(8,128)S(1)} %get-tuple-element.73), channel_id=1, source_target_pairs={{0,4},{4,0},{1,5},{5,1},{2,6},{6,2},{3,7},{7,3},{8,12},{12,8},{9,1... | collective-permute-start | bytes 1179656 | tf_op jit(solution)/shard_map/ppermute | solution.py:421
  79.9 15.0 %all_to_all.23 = f32[32,1,128]{2,1,0:T(1,128)S(1)} all-to-all(f32[32,1,128]{2,1,0:T(1,128)S(1)} %bitcast.17), channel_id=1, replica_groups=mesh['y'=8,'z'=4,'parity'=2,'core'=2,'head'=4] {'y','head'}, dimensions={0} | all-to-all | bytes 32768 | tf_op jit(solution)/shard_map/all_to_all | solution.py:476
  95.0 0.0 collective-permute-done.9.recv
  95.0 1.0 shard_map.120
  (11 shorter events, 0.0 us)
Async XLA Ops:
  3.2 20.9 %collective-permute-start.2 = (bf16[128,1664]{1,0:T(8,128)(2,1)}, bf16[128,1664]{1,0:T(8,128)(2,1)S(1)}, u32[]{:S(2)}, u32[]{:S(2)}) collective-permute-start(bf16[128,1664]{1,0:T(8,128)(2,1)} %get-tuple-element.41.keep.refs_0_), channel_id=1, source_target_pairs={{0,504},{4,12},{8,0},{12,20},{16,8},{20,28},{24,16},{28,36},{32,24... | collective-permute-start | bytes 1277960 | tf_op jit(solution)/shard_map/ppermute | solution.py:426
  8.1 16.0 %collective-permute-start = (bf16[128,1664]{1,0:T(8,128)(2,1)}, bf16[128,1664]{1,0:T(8,128)(2,1)S(1)}, u32[]{:S(2)}, u32[]{:S(2)}) collective-permute-start(bf16[128,1664]{1,0:T(8,128)(2,1)} %get-tuple-element.42), channel_id=1, source_target_pairs={{0,4},{4,0},{1,5},{5,1},{2,6},{6,2},{3,7},{7,3},{8,12},{12,8},{9,1... | collective-permute-start | bytes 1277960 | tf_op jit(solution)/shard_map/ppermute | solution.py:421
  20.5 3.6 %collective-permute-start.1 = (bf16[128,896]{1,0:T(8,128)(2,1)}, bf16[128,896]{1,0:T(8,128)(2,1)S(1)}, u32[]{:S(2)}, u32[]{:S(2)}) collective-permute-start(bf16[128,896]{1,0:T(8,128)(2,1)} %get-tuple-element.43), channel_id=1, source_target_pairs={{0,4},{4,0},{1,5},{5,1},{2,6},{6,2},{3,7},{7,3},{8,12},{12,8},{9,1... | collective-permute-start | bytes 688136 | tf_op jit(solution)/shard_map/ppermute | solution.py:421
  24.1 1.0 %copy-start = (bf16[128,1664]{1,0:T(8,128)(2,1)S(1)}, bf16[128,1664]{1,0:T(8,128)(2,1)}, u32[]{:S(2)}) copy-start(bf16[128,1664]{1,0:T(8,128)(2,1)} %get-tuple-element.41.keep.refs_0_) | copy-start | bytes 1277956
  25.1 6.2 %copy-start.2 = (bf16[128,896]{1,0:T(8,128)(2,1)S(1)}, bf16[128,896]{1,0:T(8,128)(2,1)}, u32[]{:S(2)}) copy-start(bf16[128,896]{1,0:T(8,128)(2,1)} %get-tuple-element.54.keep.refs_0_) | copy-start | bytes 688132
  25.1 15.3 %copy-start.4 = (f32[16384]{0:T(1024)S(1)}, f32[16384]{0:T(1024)}, u32[]{:S(2)}) copy-start(f32[16384]{0:T(1024)} %param.15) | copy-start | bytes 196612
  25.9 15.8 %copy-start.1 = (bf16[128,1664]{1,0:T(8,128)(2,1)S(1)}, bf16[128,1664]{1,0:T(8,128)(2,1)}, u32[]{:S(2)}) copy-start(bf16[128,1664]{1,0:T(8,128)(2,1)} %get-tuple-element.41.keep.refs_0_) | copy-start | bytes 1277956
  25.9 15.8 %collective-permute-start.3 = (bf16[192,1664]{1,0:T(8,128)(2,1)S(1)}, bf16[192,1664]{1,0:T(8,128)(2,1)S(1)}, u32[]{:S(2)}, u32[]{:S(2)}) collective-permute-start(bf16[192,1664]{1,0:T(8,128)(2,1)S(1)} %get-tuple-element.45), channel_id=1, source_target_pairs={{0,8},{4,508},{8,16},{12,4},{16,24},{20,12},{24,32},{28,20},{32,40... | collective-permute-start | bytes 1916936 | tf_op jit(solution)/shard_map/ppermute | solution.py:426
  28.9 12.8 %collective-permute-start.4 = (bf16[64,1664]{1,0:T(8,128)(2,1)}, bf16[64,1664]{1,0:T(8,128)(2,1)}, u32[]{:S(2)}, u32[]{:S(2)}) collective-permute-start(bf16[64,1664]{1,0:T(8,128)(2,1)} %get-tuple-element.51), channel_id=1, source_target_pairs={{0,504},{4,12},{8,0},{12,20},{16,8},{20,28},{24,16},{28,36},{32,24... | collective-permute-start | bytes 638984 | tf_op jit(solution)/shard_map/ppermute | solution.py:426
  31.3 9.1 %copy-start.3 = (s32[16384]{0:T(1024)S(1)}, s32[16384]{0:T(1024)}, u32[]{:S(2)}) copy-start(s32[16384]{0:T(1024)} %param.14) | copy-start | bytes 196612
  32.3 17.4 %collective-permute-start.5 = (bf16[192,896]{1,0:T(8,128)(2,1)}, bf16[192,896]{1,0:T(8,128)(2,1)S(1)}, u32[]{:S(2)}, u32[]{:S(2)}) collective-permute-start(bf16[192,896]{1,0:T(8,128)(2,1)} %get-tuple-element.56), channel_id=1, source_target_pairs={{0,8},{4,508},{8,16},{12,4},{16,24},{20,12},{24,32},{28,20},{32,40... | collective-permute-start | bytes 1032200 | tf_op jit(solution)/shard_map/ppermute | solution.py:426
  38.5 14.2 %collective-permute-start.6 = (bf16[192,896]{1,0:T(8,128)(2,1)}, bf16[192,896]{1,0:T(8,128)(2,1)}, u32[]{:S(2)}, u32[]{:S(2)}) collective-permute-start(bf16[192,896]{1,0:T(8,128)(2,1)} %get-tuple-element.57), channel_id=1, source_target_pairs={{0,504},{4,12},{8,0},{12,20},{16,8},{20,28},{24,16},{28,36},{32,24... | collective-permute-start | bytes 1032200 | tf_op jit(solution)/shard_map/ppermute | solution.py:426
  56.8 20.3 %collective-permute-start.7 = (bf16[192,768]{1,0:T(8,128)(2,1)S(1)}, bf16[192,768]{1,0:T(8,128)(2,1)S(1)}, u32[]{:S(2)}, u32[]{:S(2)}) collective-permute-start(bf16[192,768]{1,0:T(8,128)(2,1)S(1)} %get-tuple-element.69), channel_id=1, source_target_pairs={{0,8},{4,508},{8,16},{12,4},{16,24},{20,12},{24,32},{28,20},{32,40... | collective-permute-start | bytes 884744 | tf_op jit(solution)/shard_map/ppermute | solution.py:426
  59.5 17.6 %collective-permute-start.8 = (bf16[192,768]{1,0:T(8,128)(2,1)S(1)}, bf16[192,768]{1,0:T(8,128)(2,1)S(1)}, u32[]{:S(2)}, u32[]{:S(2)}) collective-permute-start(bf16[192,768]{1,0:T(8,128)(2,1)S(1)} %get-tuple-element.70), channel_id=1, source_target_pairs={{0,504},{4,12},{8,0},{12,20},{16,8},{20,28},{24,16},{28,36},{32,24... | collective-permute-start | bytes 884744 | tf_op jit(solution)/shard_map/ppermute | solution.py:426
  77.4 17.6 %collective-permute-start.9 = (f32[128,768]{1,0:T(8,128)S(1)}, f32[128,768]{1,0:T(8,128)S(1)}, u32[]{:S(2)}, u32[]{:S(2)}) collective-permute-start(f32[128,768]{1,0:T(8,128)S(1)} %get-tuple-element.73), channel_id=1, source_target_pairs={{0,4},{4,0},{1,5},{5,1},{2,6},{6,2},{3,7},{7,3},{8,12},{12,8},{9,1... | collective-permute-start | bytes 1179656 | tf_op jit(solution)/shard_map/ppermute | solution.py:421

commit v5 on v4

--- a/solution.py
+++ b/solution.py
@@ -136,20 +136,9 @@
         write(recv, keep, two, one)
 
 
-def rest_kernel(core, keep, recv, one, two):
-    half = HALO - BLOCK
-
-    @pl.when(core[0] == 0)
-    def _():
-        one[:half, :] = keep[BLOCK - half :, :]
-        one[half:, :] = recv[...]
-        two[...] = recv[:half, :]
-
-    @pl.when(core[0] != 0)
-    def _():
-        one[:BLOCK, :] = recv[...]
-        one[BLOCK:, :] = keep[:half, :]
-        two[...] = recv[BLOCK - half :, :]
+def edges(core, keep, recv):
+    out = [shape(HALO, keep.shape[1], BF16)] * 2
+    return call(edges_kernel, out, [SMEM] + [VMEM] * 2, moved=2 << 20)(core, keep, recv)
 
 
 def fold(value, op):
@@ -161,13 +150,16 @@
     t_at,
     s_at,
     s_off,
+    flipped,
     core,
     starts,
     weights,
     loss_in,
     *refs,
 ):
-    keep, recv, *halo = refs[:-12]
+    keep, recv, one, two = refs[:-12]
+    if flipped:
+        one, two = two, one
     grad_left, grad_own, grad_right, loss_out, win, bias, rt, rs, gt, qs, bt, kg = refs[-12:]
     me = core[0]
     def gather(at, rows, source):
@@ -180,20 +172,13 @@
             gather(at, source.shape[0], source)
             at += source.shape[0]
 
-    if len(halo) == 2:
-        one, two = halo
-        order = (one, keep, recv, two), (two, recv, keep, one)
-    else:
-        own, one, two = halo
-        order = (one, keep, recv, own, two), (two, own, recv, keep, one)
-
     @pl.when(me == 0)
     def _():
-        gather_all(*order[0])
+        gather_all(one, keep, recv, two)
 
     @pl.when(me != 0)
     def _():
-        gather_all(*order[1])
+        gather_all(two, recv, keep, one)
 
     key = lax.broadcasted_iota(jnp.int32, (WINDOW, OWN), 0)
     query = lax.broadcasted_iota(jnp.int32, (WINDOW, OWN), 1) + FIRST_QUERY
@@ -386,7 +371,7 @@
 
 def call_relation(rel, core, starts, weight, loss, chunk):
     return call(
-        functools.partial(relation_kernel, T_AT[rel], S_AT[rel], S_OFF[rel]),
+        functools.partial(relation_kernel, T_AT[rel], S_AT[rel], S_OFF[rel], rel == 2),
         [
             shape(HALO, SP, BF16),
             shape(OWN, SP, F32),
@@ -436,22 +421,12 @@
     )(core, *arrays)
     recv_a = other_core(send_a)
     recv_b = other_core(send_b)
-    own_a = neighbours(keep_a, -1)
-    recv_a, recv_b, own_a = lax.optimization_barrier((recv_a, recv_b, own_a))
-    halo_a = [own_a]
-    rest_a = call(
-        rest_kernel,
-        [shape(HALO, WIDTH_A, BF16), shape(HALO - BLOCK, WIDTH_A, BF16)],
-        [SMEM] + [VMEM] * 2,
-        moved=2 << 20,
-    )(core, keep_a, recv_a)
-    halo_a += [neighbours(rest_a[0], 1), neighbours(rest_a[1], -1)]
-    edges_b = call(edges_kernel, [shape(HALO, REL, BF16)] * 2, [SMEM] + [VMEM] * 2, moved=1 << 20)(
-        core, keep_b, recv_b
-    )
-    halo_b = [neighbours(edges_b[0], 1), neighbours(edges_b[1], -1)]
-
-    doc_ids, row_weight, _ = lax.optimization_barrier((doc_ids, row_weight, rest_a[0]))
+    edges_a = edges(core, keep_a, recv_a)
+    halo_a = [neighbours(edges_a[0], 1), neighbours(edges_a[1], -1)]
+    edges_b = edges(core, keep_b, recv_b)
+    halo_b = [neighbours(edges_b[1], -1), neighbours(edges_b[0], 1)]
+
+    doc_ids, row_weight, _ = lax.optimization_barrier((doc_ids, row_weight, edges_a[0]))
     starts, weight = call(
         mask_kernel,
         [shape(1, OWN, jnp.int32), shape(1, OWN, F32)],

time: 96.5 us -> 92.2 us (0.955)
  waiting for transfers between devices: 5.77 us -> 3.05 us
  Pallas kernels: 17.7 us -> 16.1 us
  blocking collectives: 30 us -> 28.8 us
  starting transfers between devices: 40.6 us -> 41.8 us
    ppermute x7 -> x6, starting transfers between devices: 23.6 us -> 27.9 us  [neighbours(): return lax.ppermute(value, tok, pairs)]
    ppermute x7 -> x6, waiting for transfers between devices: 4.1 us -> 0.37 us  [neighbours(): return lax.ppermute(value, tok, pairs)]
    ppermute x3, starting transfers between devices: 16.9 us -> 13.9 us  [other_core(): return lax.ppermute(value, 'core', [(0, 1), (1, 0)])]
    pallas_call x5, Pallas kernels: 13.6 us -> 12.1 us  [the longest x3 10.2 us: call_relation(): call(functools.partial(relation_kernel, T_AT[rel], S_AT[rel], S_OFF[rel],...]
    all_to_all x2, blocking collectives: 30 us -> 28.8 us  [exchange(): return lax.all_to_all(value, axes, 0, 0, tiled=True)]
    ppermute x3, waiting for transfers between devices: 1.67 us -> 2.68 us  [other_core(): return lax.ppermute(value, 'core', [(0, 1), (1, 0)])]
  transfers between devices with their start and end apart: 10 -> 9, of which waited for: 3 -> 3; matrix products, arithmetic and copies ran while one was open for 0% -> 0% of each run, Pallas kernels for 9% -> 8%
where the time goes in v5:
time: 92.2 us; the launch traced here: 91.7 us
  starting transfers between devices  41.8 us (45%)
  blocking collectives  28.8 us (31%)
  Pallas kernels  16.1 us (17%)
  waiting for transfers between devices  3.05 us (3%)
  local copies, waits for them, and re-layouts  1.03 us (1%)
    all_to_all x2, blocking collectives, exchange(): return lax.all_to_all(value, axes, 0, 0, tiled=True)  28.8 us
    ppermute x6, starting transfers between devices, neighbours(): return lax.ppermute(value, tok, pairs)  27.9 us
    ppermute x3, starting transfers between devices, other_core(): return lax.ppermute(value, 'core', [(0, 1), (1, 0)])  13.9 us
    pallas_call x3, Pallas kernels, call_relation(): call(functools.partial(relation_kernel, T_AT[rel], S_AT[rel], S_OFF[rel],...  10.2 us
    ppermute x3, waiting for transfers between devices, other_core(): return lax.ppermute(value, 'core', [(0, 1), (1, 0)])  2.68 us
    pallas_call x1, Pallas kernels, body(): call(split_kernel, [shape(BLOCK, WIDTH_A, BF16)] * 2 + [shape(BLOCK, REL,...  2.59 us
    pallas_call x2, Pallas kernels, edges(): call(edges_kernel, out, [SMEM] + [VMEM] * 2, moved=2 << 20)  1.86 us
  transfers between devices with their start and end apart: 9, of which 3 were waited for; matrix products, arithmetic and copies ran while one was open for 0% of the time, Pallas kernels for 8%

profile of v5, /device:TPU:1, one launch (start us, length us, event | category | flops | bytes accessed | tf_op | source)
XLA Modules:
  0.0 91.7 jit_solution(10765589381055765008)
XLA Ops:
  0.6 2.6 %shard_map.111 = (bf16[128,1664]{1,0:T(8,128)(2,1)}, bf16[128,1664]{1,0:T(8,128)(2,1)}, bf16[128,896]{1,0:T(8,128)(2,1)}, bf16[128,896]{1,0:T(8,128)(2,1)}) custom-call(s32[1]{0:T(128)} %bitcast.core, bf16[128,1280]{1,0:T(8,128)(2,1)} %refs_0_.1, bf16[128,1280]{1,0:T(8,128)(2,1)} %refs_1_.1, bf16[128,1280]{1,0:T(8,128)(2,1)} %refs_2_.1, ...), custom_call_target="tpu_custom_call" | custom-call | bytes 4194304 | tf_op jit(solution)/shard_map/pallas_call | solution.py:414
  3.2 8.8 %collective-permute-start = (bf16[128,1664]{1,0:T(8,128)(2,1)}, bf16[128,1664]{1,0:T(8,128)(2,1)S(1)}, u32[]{:S(2)}, u32[]{:S(2)}) collective-permute-start(bf16[128,1664]{1,0:T(8,128)(2,1)} %get-tuple-element.39), channel_id=1, source_target_pairs={{0,4},{4,0},{1,5},{5,1},{2,6},{6,2},{3,7},{7,3},{8,12},{12,8},{9,1... | collective-permute-start | bytes 1277960 | tf_op jit(solution)/shard_map/ppermute | solution.py:406
  12.0 1.6 %collective-permute-done.recv.refs_1_ = bf16[128,1664]{1,0:T(8,128)(2,1)S(1)} collective-permute-done((bf16[128,1664]{1,0:T(8,128)(2,1)}, bf16[128,1664]{1,0:T(8,128)(2,1)S(1)}, u32[]{:S(2)}, u32[]{:S(2)}) %collective-permute-start) | collective-permute-done | bytes 426016 | tf_op jit(solution)/shard_map/ppermute | solution.py:406
  13.6 1.0 %copy-done = bf16[128,1664]{1,0:T(8,128)(2,1)S(1)} copy-done((bf16[128,1664]{1,0:T(8,128)(2,1)S(1)}, bf16[128,1664]{1,0:T(8,128)(2,1)}, u32[]{:S(2)}) %copy-start) | copy-done | bytes 426008
  14.6 1.0 %shard_map.112 = (bf16[192,1664]{1,0:T(8,128)(2,1)}, bf16[192,1664]{1,0:T(8,128)(2,1)S(1)}) custom-call(s32[1]{0:T(128)} %bitcast.core, bf16[128,1664]{1,0:T(8,128)(2,1)S(1)} %copy-done, bf16[128,1664]{1,0:T(8,128)(2,1)S(1)} %collective-permute-done.recv.refs_1_), custom_call_target="tpu_custom_call" | custom-call | bytes 2097152 | tf_op jit(solution)/shard_map/pallas_call | solution.py:141
  15.6 8.3 %collective-permute-start.1 = (bf16[192,1664]{1,0:T(8,128)(2,1)}, bf16[192,1664]{1,0:T(8,128)(2,1)S(1)}, u32[]{:S(2)}, u32[]{:S(2)}) collective-permute-start(bf16[192,1664]{1,0:T(8,128)(2,1)} %get-tuple-element.40), channel_id=1, source_target_pairs={{0,8},{4,508},{8,16},{12,4},{16,24},{20,12},{24,32},{28,20},{32,40... | collective-permute-start | bytes 1916936 | tf_op jit(solution)/shard_map/ppermute | solution.py:411
  23.9 1.9 %collective-permute-start.2 = (bf16[192,1664]{1,0:T(8,128)(2,1)S(1)}, bf16[192,1664]{1,0:T(8,128)(2,1)S(1)}, u32[]{:S(2)}, u32[]{:S(2)}) collective-permute-start(bf16[192,1664]{1,0:T(8,128)(2,1)S(1)} %get-tuple-element.45), channel_id=1, source_target_pairs={{0,504},{4,12},{8,0},{12,20},{16,8},{20,28},{24,16},{28,36},{32,24... | collective-permute-start | bytes 1916936 | tf_op jit(solution)/shard_map/ppermute | solution.py:411
  25.8 0.0 copy-done.5
  25.9 2.6 %collective-permute-start.3 = (bf16[128,896]{1,0:T(8,128)(2,1)S(1)}, bf16[128,896]{1,0:T(8,128)(2,1)S(1)}, u32[]{:S(2)}, u32[]{:S(2)}) collective-permute-start(bf16[128,896]{1,0:T(8,128)(2,1)S(1)} %copy-done.5), channel_id=1, source_target_pairs={{0,4},{4,0},{1,5},{5,1},{2,6},{6,2},{3,7},{7,3},{8,12},{12,8},{9,1... | collective-permute-start | bytes 688136 | tf_op jit(solution)/shard_map/ppermute | solution.py:406
  28.4 1.1 %collective-permute-done.3.recv.refs_1_ = bf16[128,896]{1,0:T(8,128)(2,1)S(1)} collective-permute-done((bf16[128,896]{1,0:T(8,128)(2,1)S(1)}, bf16[128,896]{1,0:T(8,128)(2,1)S(1)}, u32[]{:S(2)}, u32[]{:S(2)}) %collective-permute-start.3) | collective-permute-done | bytes 229408 | tf_op jit(solution)/shard_map/ppermute | solution.py:406
  29.5 0.9 shard_map.116
  30.4 1.9 %collective-permute-start.4 = (bf16[192,896]{1,0:T(8,128)(2,1)}, bf16[192,896]{1,0:T(8,128)(2,1)}, u32[]{:S(2)}, u32[]{:S(2)}) collective-permute-start(bf16[192,896]{1,0:T(8,128)(2,1)} %get-tuple-element.50), channel_id=1, source_target_pairs={{0,504},{4,12},{8,0},{12,20},{16,8},{20,28},{24,16},{28,36},{32,24... | collective-permute-start | bytes 1032200 | tf_op jit(solution)/shard_map/ppermute | solution.py:411
  32.4 6.7 %collective-permute-start.5 = (bf16[192,896]{1,0:T(8,128)(2,1)}, bf16[192,896]{1,0:T(8,128)(2,1)}, u32[]{:S(2)}, u32[]{:S(2)}) collective-permute-start(bf16[192,896]{1,0:T(8,128)(2,1)} %get-tuple-element.51), channel_id=1, source_target_pairs={{0,8},{4,508},{8,16},{12,4},{16,24},{20,12},{24,32},{28,20},{32,40... | collective-permute-start | bytes 1032200 | tf_op jit(solution)/shard_map/ppermute | solution.py:411
  39.1 0.2 shard_map.113
  39.3 0.0 collective-permute-done.1.refs_2_
  39.3 0.0 collective-permute-done.2.refs_3_
  39.3 3.1 %shard_map.114 = (bf16[192,256]{1,0:T(8,128)(2,1)S(1)}, f32[256,256]{1,0:T(8,128)S(1)}, bf16[192,256]{1,0:T(8,128)(2,1)S(1)}, f32[1,128]{1,0:T(1,128)S(1)}) custom-call(s32[1]{0:T(128)} %bitcast.core, s32[1,256]{1,0:T(1,128)S(1)} %get-tuple-element.43.starts, f32[1,256]{1,0:T(1,128)S(1)} %get-tuple-element.44.weights, f32[1,128]{1,0:T(1,128)S(1)} %broadcast_in_dim.3.loss_in, ...), custom_call_target="tpu_custom_call" | custom-call | flops 1342177280 | bytes 2097152 | tf_op jit(solution)/shard_map/pallas_call | solution.py:373
  42.4 3.0 %shard_map.115 = (bf16[192,256]{1,0:T(8,128)(2,1)S(1)}, f32[256,256]{1,0:T(8,128)S(1)}, bf16[192,256]{1,0:T(8,128)(2,1)S(1)}, f32[1,128]{1,0:T(1,128)S(1)}) custom-call(s32[1]{0:T(128)} %bitcast.core, s32[1,256]{1,0:T(1,128)S(1)} %get-tuple-element.43.starts, f32[1,256]{1,0:T(1,128)S(1)} %get-tuple-element.44.weights, ...), custom_call_target="tpu_custom_call" | custom-call | flops 1342177280 | bytes 2097152 | tf_op jit(solution)/shard_map/pallas_call | solution.py:373
  45.4 0.0 collective-permute-done.4.refs_2_
  45.4 0.3 collective-permute-done.5.refs_3_
  45.8 4.1 %shard_map.117 = (bf16[192,256]{1,0:T(8,128)(2,1)S(1)}, f32[256,256]{1,0:T(8,128)S(1)}, bf16[192,256]{1,0:T(8,128)(2,1)S(1)}, f32[1,128]{1,0:T(1,128)S(1)}) custom-call(s32[1]{0:T(128)} %bitcast.core, s32[1,256]{1,0:T(1,128)S(1)} %get-tuple-element.43.starts, f32[1,256]{1,0:T(1,128)S(1)} %get-tuple-element.44.weights, ...), custom_call_target="tpu_custom_call" | custom-call | flops 1342177280 | bytes 2097152 | tf_op jit(solution)/shard_map/pallas_call | solution.py:373
  49.9 0.1 shard_map.118
  50.0 7.1 %collective-permute-start.6 = (bf16[192,768]{1,0:T(8,128)(2,1)S(1)}, bf16[192,768]{1,0:T(8,128)(2,1)S(1)}, u32[]{:S(2)}, u32[]{:S(2)}) collective-permute-start(bf16[192,768]{1,0:T(8,128)(2,1)S(1)} %get-tuple-element.63), channel_id=1, source_target_pairs={{0,8},{4,508},{8,16},{12,4},{16,24},{20,12},{24,32},{28,20},{32,40... | collective-permute-start | bytes 884744 | tf_op jit(solution)/shard_map/ppermute | solution.py:411
  57.1 1.9 %collective-permute-start.7 = (bf16[192,768]{1,0:T(8,128)(2,1)S(1)}, bf16[192,768]{1,0:T(8,128)(2,1)S(1)}, u32[]{:S(2)}, u32[]{:S(2)}) collective-permute-start(bf16[192,768]{1,0:T(8,128)(2,1)S(1)} %get-tuple-element.64), channel_id=1, source_target_pairs={{0,504},{4,12},{8,0},{12,20},{16,8},{20,28},{24,16},{28,36},{32,24... | collective-permute-start | bytes 884744 | tf_op jit(solution)/shard_map/ppermute | solution.py:411
  59.0 13.8 %all_to_all.22 = f32[16,1,128]{2,1,0:T(1,128)S(1)} all-to-all(f32[16,1,128]{2,1,0:T(1,128)S(1)} %bitcast.18), channel_id=1, replica_groups=mesh['y'=8,'z'=4,'parity'=2,'core'=2,'head'=4] {'z','parity','core'}, dimensions={0} | all-to-all | bytes 16384 | tf_op jit(solution)/shard_map/all_to_all | solution.py:451
  72.9 0.0 collective-permute-done.6.one
  72.9 0.0 collective-permute-done.7.two
  72.9 0.2 shard_map.119
  73.1 2.6 %collective-permute-start.8 = (f32[128,768]{1,0:T(8,128)S(1)}, f32[128,768]{1,0:T(8,128)S(1)}, u32[]{:S(2)}, u32[]{:S(2)}) collective-permute-start(f32[128,768]{1,0:T(8,128)S(1)} %get-tuple-element.67), channel_id=1, source_target_pairs={{0,4},{4,0},{1,5},{5,1},{2,6},{6,2},{3,7},{7,3},{8,12},{12,8},{9,1... | collective-permute-start | bytes 1179656 | tf_op jit(solution)/shard_map/ppermute | solution.py:406
  75.7 15.0 %all_to_all.23 = f32[32,1,128]{2,1,0:T(1,128)S(1)} all-to-all(f32[32,1,128]{2,1,0:T(1,128)S(1)} %bitcast.17), channel_id=1, replica_groups=mesh['y'=8,'z'=4,'parity'=2,'core'=2,'head'=4] {'y','head'}, dimensions={0} | all-to-all | bytes 32768 | tf_op jit(solution)/shard_map/all_to_all | solution.py:451
  90.7 0.0 collective-permute-done.8.recv
  90.7 1.0 %shard_map.120 = (f32[128,384]{1,0:T(8,128)}, f32[128,384]{1,0:T(8,128)}, f32[128,384]{1,0:T(8,128)}, f32[1,1]{1,0:T(1,128)}) custom-call(s32[1]{0:T(128)} %bitcast.core, f32[32,128]{1,0:T(8,128)S(1)} %bitcast.13, f32[128,768]{1,0:T(8,128)S(1)} %get-tuple-element.66.keep, f32[128,768]{1,0:T(8,128)S(1)} %collective-permute-done.8.recv), custom_call_target="tpu_custom_call" | custom-call | bytes 1048576 | tf_op jit(solution)/shard_map/pallas_call | solution.py:471
  (11 shorter events, 0.0 us)
Async XLA Ops:
  3.2 10.4 %collective-permute-start = (bf16[128,1664]{1,0:T(8,128)(2,1)}, bf16[128,1664]{1,0:T(8,128)(2,1)S(1)}, u32[]{:S(2)}, u32[]{:S(2)}) collective-permute-start(bf16[128,1664]{1,0:T(8,128)(2,1)} %get-tuple-element.39), channel_id=1, source_target_pairs={{0,4},{4,0},{1,5},{5,1},{2,6},{6,2},{3,7},{7,3},{8,12},{12,8},{9,1... | collective-permute-start | bytes 1277960 | tf_op jit(solution)/shard_map/ppermute | solution.py:406
  13.6 1.0 %copy-start = (bf16[128,1664]{1,0:T(8,128)(2,1)S(1)}, bf16[128,1664]{1,0:T(8,128)(2,1)}, u32[]{:S(2)}) copy-start(bf16[128,1664]{1,0:T(8,128)(2,1)} %get-tuple-element.38.keep.refs_0_) | copy-start | bytes 1277956
  14.6 11.2 %copy-start.5 = (bf16[128,896]{1,0:T(8,128)(2,1)S(1)}, bf16[128,896]{1,0:T(8,128)(2,1)}, u32[]{:S(2)}) copy-start(bf16[128,896]{1,0:T(8,128)(2,1)} %get-tuple-element.49) | copy-start | bytes 688132
  14.6 14.9 %copy-start.2 = (bf16[128,896]{1,0:T(8,128)(2,1)S(1)}, bf16[128,896]{1,0:T(8,128)(2,1)}, u32[]{:S(2)}) copy-start(bf16[128,896]{1,0:T(8,128)(2,1)} %get-tuple-element.48.keep.refs_0_) | copy-start | bytes 688132
  14.6 24.4 %copy-start.4 = (f32[16384]{0:T(1024)S(1)}, f32[16384]{0:T(1024)}, u32[]{:S(2)}) copy-start(f32[16384]{0:T(1024)} %param.15) | copy-start | bytes 196612
  15.6 23.7 %copy-start.1 = (bf16[128,1664]{1,0:T(8,128)(2,1)S(1)}, bf16[128,1664]{1,0:T(8,128)(2,1)}, u32[]{:S(2)}) copy-start(bf16[128,1664]{1,0:T(8,128)(2,1)} %get-tuple-element.38.keep.refs_0_) | copy-start | bytes 1277956
  15.6 23.7 %collective-permute-start.1 = (bf16[192,1664]{1,0:T(8,128)(2,1)}, bf16[192,1664]{1,0:T(8,128)(2,1)S(1)}, u32[]{:S(2)}, u32[]{:S(2)}) collective-permute-start(bf16[192,1664]{1,0:T(8,128)(2,1)} %get-tuple-element.40), channel_id=1, source_target_pairs={{0,8},{4,508},{8,16},{12,4},{16,24},{20,12},{24,32},{28,20},{32,40... | collective-permute-start | bytes 1916936 | tf_op jit(solution)/shard_map/ppermute | solution.py:411
  23.9 15.4 %collective-permute-start.2 = (bf16[192,1664]{1,0:T(8,128)(2,1)S(1)}, bf16[192,1664]{1,0:T(8,128)(2,1)S(1)}, u32[]{:S(2)}, u32[]{:S(2)}) collective-permute-start(bf16[192,1664]{1,0:T(8,128)(2,1)S(1)} %get-tuple-element.45), channel_id=1, source_target_pairs={{0,504},{4,12},{8,0},{12,20},{16,8},{20,28},{24,16},{28,36},{32,24... | collective-permute-start | bytes 1916936 | tf_op jit(solution)/shard_map/ppermute | solution.py:411
  25.9 3.7 %collective-permute-start.3 = (bf16[128,896]{1,0:T(8,128)(2,1)S(1)}, bf16[128,896]{1,0:T(8,128)(2,1)S(1)}, u32[]{:S(2)}, u32[]{:S(2)}) collective-permute-start(bf16[128,896]{1,0:T(8,128)(2,1)S(1)} %copy-done.5), channel_id=1, source_target_pairs={{0,4},{4,0},{1,5},{5,1},{2,6},{6,2},{3,7},{7,3},{8,12},{12,8},{9,1... | collective-permute-start | bytes 688136 | tf_op jit(solution)/shard_map/ppermute | solution.py:406
  29.5 9.5 %copy-start.3 = (s32[16384]{0:T(1024)S(1)}, s32[16384]{0:T(1024)}, u32[]{:S(2)}) copy-start(s32[16384]{0:T(1024)} %param.14) | copy-start | bytes 196612
  30.4 15.0 %collective-permute-start.4 = (bf16[192,896]{1,0:T(8,128)(2,1)}, bf16[192,896]{1,0:T(8,128)(2,1)}, u32[]{:S(2)}, u32[]{:S(2)}) collective-permute-start(bf16[192,896]{1,0:T(8,128)(2,1)} %get-tuple-element.50), channel_id=1, source_target_pairs={{0,504},{4,12},{8,0},{12,20},{16,8},{20,28},{24,16},{28,36},{32,24... | collective-permute-start | bytes 1032200 | tf_op jit(solution)/shard_map/ppermute | solution.py:411
  32.4 13.4 %collective-permute-start.5 = (bf16[192,896]{1,0:T(8,128)(2,1)}, bf16[192,896]{1,0:T(8,128)(2,1)}, u32[]{:S(2)}, u32[]{:S(2)}) collective-permute-start(bf16[192,896]{1,0:T(8,128)(2,1)} %get-tuple-element.51), channel_id=1, source_target_pairs={{0,8},{4,508},{8,16},{12,4},{16,24},{20,12},{24,32},{28,20},{32,40... | collective-permute-start | bytes 1032200 | tf_op jit(solution)/shard_map/ppermute | solution.py:411
  50.0 22.9 %collective-permute-start.6 = (bf16[192,768]{1,0:T(8,128)(2,1)S(1)}, bf16[192,768]{1,0:T(8,128)(2,1)S(1)}, u32[]{:S(2)}, u32[]{:S(2)}) collective-permute-start(bf16[192,768]{1,0:T(8,128)(2,1)S(1)} %get-tuple-element.63), channel_id=1, source_target_pairs={{0,8},{4,508},{8,16},{12,4},{16,24},{20,12},{24,32},{28,20},{32,40... | collective-permute-start | bytes 884744 | tf_op jit(solution)/shard_map/ppermute | solution.py:411
  57.1 15.7 %collective-permute-start.7 = (bf16[192,768]{1,0:T(8,128)(2,1)S(1)}, bf16[192,768]{1,0:T(8,128)(2,1)S(1)}, u32[]{:S(2)}, u32[]{:S(2)}) collective-permute-start(bf16[192,768]{1,0:T(8,128)(2,1)S(1)} %get-tuple-element.64), channel_id=1, source_target_pairs={{0,504},{4,12},{8,0},{12,20},{16,8},{20,28},{24,16},{28,36},{32,24... | collective-permute-start | bytes 884744 | tf_op jit(solution)/shard_map/ppermute | solution.py:411
  73.1 17.6 %collective-permute-start.8 = (f32[128,768]{1,0:T(8,128)S(1)}, f32[128,768]{1,0:T(8,128)S(1)}, u32[]{:S(2)}, u32[]{:S(2)}) collective-permute-start(f32[128,768]{1,0:T(8,128)S(1)} %get-tuple-element.67), channel_id=1, source_target_pairs={{0,4},{4,0},{1,5},{5,1},{2,6},{6,2},{3,7},{7,3},{8,12},{12,8},{9,1... | collective-permute-start | bytes 1179656 | tf_op jit(solution)/shard_map/ppermute | solution.py:406

commit v6 on v5

--- a/solution.py
+++ b/solution.py
@@ -25,8 +25,10 @@
 SP = 256
 REL = TW + SP
 WIDTH_A = 2 * TW + 2 * SW
+WIDTH = WIDTH_A + REL
 T_AT = (0, TW, 0)
 S_AT = (2 * TW, 2 * TW + 128, TW)
+CHUNK_AT = (0, 0, WIDTH_A)
 S_OFF = (0, SW - 128, 0)
 CT = DT ** (-0.5) * math.log2(math.e)
 CS = DS ** (-0.5) * math.log2(math.e)
@@ -52,12 +54,7 @@
 
 
 def split_kernel(core, *refs):
-    arrays, (send_a, keep_a, send_b, keep_b), buffers, sems = (
-        refs[:6],
-        refs[6:10],
-        refs[10:16],
-        refs[16],
-    )
+    arrays, (send, keep), buffers, sems = refs[:6], refs[6:8], refs[8:14], refs[14]
     me = core[0]
     copies = [
         pltpu.make_async_copy(array, buffer, sems.at[i])
@@ -73,7 +70,7 @@
     ours, theirs = [], []
     for rel in range(3):
         teacher, student = buffers[rel], buffers[3 + rel]
-        keep, send, at = (keep_b, send_b, 0) if rel == 2 else (keep_a, send_a, rel * TW)
+        at = CHUNK_AT[rel] + T_AT[rel]
         keep[:, at : at + TW] = teacher[:, mine]
         send[:, at : at + TW] = teacher[:, other]
         low = jnp.where(lane < SW, student[:, :SP].astype(F32), 0.0)
@@ -81,13 +78,13 @@
         high = jnp.where(lane < SW, high, 0.0)
         ours.append(jnp.where(me == 0, low, high))
         theirs.append(jnp.where(me == 0, high, low))
-    for halves, out_a, out_b in ((ours, keep_a, keep_b), (theirs, send_a, send_b)):
+    for halves, out in ((ours, keep), (theirs, send)):
         second = pltpu.roll(halves[1], S_OFF[1], 1)
         at = 2 * TW
-        out_a[:, at : at + 128] = halves[0][:, :128].astype(BF16)
-        out_a[:, at + 128 : at + 256] = (halves[0][:, 128:] + second[:, :128]).astype(BF16)
-        out_a[:, at + 256 : at + 384] = second[:, 128:].astype(BF16)
-        out_b[:, TW:] = halves[2].astype(BF16)
+        out[:, at : at + 128] = halves[0][:, :128].astype(BF16)
+        out[:, at + 128 : at + 256] = (halves[0][:, 128:] + second[:, :128]).astype(BF16)
+        out[:, at + 256 : at + 384] = second[:, 128:].astype(BF16)
+        out[:, WIDTH_A + TW :] = halves[2].astype(BF16)
 
 
 def mask_kernel(chip, docs, rows, starts, weights):
@@ -118,27 +115,24 @@
     weights[...] = queries([row_of(rows, r) for r in range(3, 6)])
 
 
-def edges_kernel(core, keep, recv, one, two):
+def edges_kernel(core, keep, recv, *outs):
     half = HALO - BLOCK
-
-    def write(first, second, after, before):
-        after[:half, :] = first[BLOCK - half :, :]
-        after[half:, :] = second[...]
-        before[:BLOCK, :] = first[...]
-        before[BLOCK:, :] = second[:half, :]
-
-    @pl.when(core[0] == 0)
-    def _():
-        write(keep, recv, one, two)
-
-    @pl.when(core[0] != 0)
-    def _():
-        write(recv, keep, two, one)
-
-
-def edges(core, keep, recv):
-    out = [shape(HALO, keep.shape[1], BF16)] * 2
-    return call(edges_kernel, out, [SMEM] + [VMEM] * 2, moved=2 << 20)(core, keep, recv)
+    for chunk, cols in enumerate((slice(0, WIDTH_A), slice(WIDTH_A, WIDTH))):
+        one, two = outs[2 * chunk : 2 * chunk + 2]
+
+        def write(first, second, after, before):
+            after[:half, :] = first[BLOCK - half :, cols]
+            after[half:, :] = second[:, cols]
+            before[:BLOCK, :] = first[:, cols]
+            before[BLOCK:, :] = second[:half, cols]
+
+        @pl.when(core[0] == 0)
+        def _():
+            write(keep, recv, one, two)
+
+        @pl.when(core[0] != 0)
+        def _():
+            write(recv, keep, two, one)
 
 
 def fold(value, op):
@@ -147,10 +141,7 @@
 
 
 def relation_kernel(
-    t_at,
-    s_at,
-    s_off,
-    flipped,
+    rel,
     core,
     starts,
     weights,
@@ -158,13 +149,13 @@
     *refs,
 ):
     keep, recv, one, two = refs[:-12]
-    if flipped:
-        one, two = two, one
+    t_at, s_at, s_off = T_AT[rel], S_AT[rel], S_OFF[rel]
     grad_left, grad_own, grad_right, loss_out, win, bias, rt, rs, gt, qs, bt, kg = refs[-12:]
     me = core[0]
     def gather(at, rows, source):
-        win[at : at + rows, :TW] = source[:, t_at : t_at + TW]
-        win[at : at + rows, TW:] = source[:, s_at : s_at + SP]
+        base = CHUNK_AT[rel] if source.shape[1] == WIDTH else 0
+        win[at : at + rows, :TW] = source[:, base + t_at : base + t_at + TW]
+        win[at : at + rows, TW:] = source[:, base + s_at : base + s_at + SP]
 
     def gather_all(*sources):
         at = 0
@@ -327,36 +318,47 @@
         write(two, one)
 
 
-def merge_kernel(core, parts, o0, o1, o2, one, two, keep, send, copies, acc):
-    me = core[0]
+def merge_kernel(core, parts, o0, o1, o2, mine, other, keep, send, copies):
     copies[...] = jnp.broadcast_to(jnp.sum(parts[...], axis=0, keepdims=True), copies.shape)
+    half = HALO - BLOCK
     for rel, own in enumerate((o0, o1, o2)):
-        acc[:, rel * SP : (rel + 1) * SP] = own[...]
-
-    def add(from_before, from_after):
-        acc[:HALO, :] = acc[:HALO, :] + from_before[...].astype(F32)
-        acc[OWN - HALO :, :] = acc[OWN - HALO :, :] + from_after[...].astype(F32)
-
-    @pl.when(me == 0)
-    def _():
-        add(one, two)
-
-    @pl.when(me != 0)
-    def _():
-        add(two, one)
-
-    keep[...] = acc[pl.ds(pl.multiple_of(me * BLOCK, 128), BLOCK), :]
-    send[...] = acc[pl.ds(pl.multiple_of((1 - me) * BLOCK, 128), BLOCK), :]
+        cols = slice(rel * SP, (rel + 1) * SP)
+
+        @pl.when(core[0] == 0)
+        def _():
+            keep[:BLOCK, cols] = own[:BLOCK, :] + mine[:BLOCK, cols].astype(F32)
+            keep[BLOCK:, cols] = other[:BLOCK, cols].astype(F32)
+            send[:half, cols] = own[BLOCK : BLOCK + half, :] + mine[BLOCK:, cols].astype(F32)
+            send[half:BLOCK, cols] = own[BLOCK + half :, :]
+            send[BLOCK:, cols] = other[BLOCK:, cols].astype(F32)
+
+        @pl.when(core[0] != 0)
+        def _():
+            keep[:BLOCK, cols] = own[BLOCK:, :] + mine[half:, cols].astype(F32)
+            keep[BLOCK:, cols] = other[half:, cols].astype(F32)
+            send[: BLOCK - half, cols] = own[: BLOCK - half, :]
+            send[BLOCK - half : BLOCK, cols] = own[BLOCK - half : BLOCK, :] + mine[
+                :half, cols
+            ].astype(F32)
+            send[BLOCK:, cols] = other[:half, cols].astype(F32)
 
 
 def place_kernel(tokens, core, parts, keep, recv, oq, ok, ov, loss):
     me = core[0]
     total = jnp.sum(jnp.sum(parts[...], axis=0, keepdims=True), axis=1, keepdims=True)
     loss[...] = total * (1.0 / (3 * H * tokens))
+    half = HALO - BLOCK
     empty = jnp.zeros((BLOCK, 2 * SW - SP), F32)
+    gap = jnp.zeros((BLOCK - half, SP), F32)
     for rel, out in enumerate((oq, ok, ov)):
-        ours = jnp.concatenate([keep[:, rel * SP : (rel + 1) * SP], empty], axis=1)
-        theirs = jnp.concatenate([recv[:, rel * SP : (rel + 1) * SP], empty], axis=1)
+        cols = slice(rel * SP, (rel + 1) * SP)
+        late = recv[BLOCK:, cols]
+        first = jnp.concatenate([late, gap], axis=0)
+        last = jnp.concatenate([gap, late], axis=0)
+        ours = keep[:BLOCK, cols] + jnp.where(me == 0, last, first)
+        theirs = keep[BLOCK:, cols] + recv[:BLOCK, cols]
+        ours = jnp.concatenate([ours, empty], axis=1)
+        theirs = jnp.concatenate([theirs, empty], axis=1)
         low = jnp.where(me == 0, ours, theirs)
         high = jnp.where(me == 0, theirs, ours)
         off = S_OFF[rel]
@@ -371,7 +373,7 @@
 
 def call_relation(rel, core, starts, weight, loss, chunk):
     return call(
-        functools.partial(relation_kernel, T_AT[rel], S_AT[rel], S_OFF[rel], rel == 2),
+        functools.partial(relation_kernel, rel),
         [
             shape(HALO, SP, BF16),
             shape(OWN, SP, F32),
@@ -405,28 +407,31 @@
     def other_core(value):
         return lax.ppermute(value, "core", [(0, 1), (1, 0)])
 
-    def neighbours(value, way):
+    def neighbours(value, way, cross=0):
         step = (2 * way, -2 * way)
-        pairs = [(i, (i + step[i % 2]) % count) for i in range(count)]
+        pairs = [(i, ((i + step[i % 2]) % count) ^ cross) for i in range(count)]
         return lax.ppermute(value, tok, pairs)
 
     arrays = (teacher_q, teacher_k, teacher_v, student_q, student_k, student_v)
-    send_a, keep_a, send_b, keep_b = call(
+    send, keep = call(
         split_kernel,
-        [shape(BLOCK, WIDTH_A, BF16)] * 2 + [shape(BLOCK, REL, BF16)] * 2,
+        [shape(BLOCK, WIDTH, BF16)] * 2,
         [SMEM] + [HBM] * 6,
         scratch=[pltpu.VMEM(a.shape, BF16) for a in arrays] + [pltpu.SemaphoreType.DMA((6,))],
         moved=4 << 20,
         limit=56,
     )(core, *arrays)
-    recv_a = other_core(send_a)
-    recv_b = other_core(send_b)
-    edges_a = edges(core, keep_a, recv_a)
-    halo_a = [neighbours(edges_a[0], 1), neighbours(edges_a[1], -1)]
-    edges_b = edges(core, keep_b, recv_b)
-    halo_b = [neighbours(edges_b[1], -1), neighbours(edges_b[0], 1)]
-
-    doc_ids, row_weight, _ = lax.optimization_barrier((doc_ids, row_weight, edges_a[0]))
+    recv = other_core(send)
+    edges = call(
+        edges_kernel,
+        [shape(HALO, WIDTH_A, BF16)] * 2 + [shape(HALO, REL, BF16)] * 2,
+        [SMEM] + [VMEM] * 2,
+        moved=2 << 20,
+    )(core, keep, recv)
+    halo_a = [neighbours(edges[0], 1), neighbours(edges[1], -1)]
+    halo_b = [neighbours(edges[2], 1), neighbours(edges[3], -1)]
+
+    doc_ids, row_weight, _ = lax.optimization_barrier((doc_ids, row_weight, edges[0]))
     starts, weight = call(
         mask_kernel,
         [shape(1, OWN, jnp.int32), shape(1, OWN, F32)],
@@ -440,7 +445,7 @@
     loss = jnp.zeros((1, BLOCK), F32)
     grads = []
     for rel in range(3):
-        chunk = (keep_b, recv_b, *halo_b) if rel == 2 else (keep_a, recv_a, *halo_a)
+        chunk = (keep, recv, *(halo_b if rel == 2 else halo_a))
         *grad, loss = call_relation(rel, core, starts, weight, loss, chunk)
         grads.append(grad)
 
@@ -457,13 +462,12 @@
         moved=1 << 20,
     )(core, loss, *(g[0] for g in grads), *(g[2] for g in grads))
     one = neighbours(one, 1)
-    two = neighbours(two, -1)
+    two = neighbours(two, -1, 1)
     parts = exchange(parts, stages[0])
     kept, sent, parts = call(
         merge_kernel,
-        [shape(BLOCK, 3 * SP, F32)] * 2 + [copies[1]],
+        [shape(OWN, 3 * SP, F32), shape(HALO, 3 * SP, F32), copies[1]],
         [SMEM] + [VMEM] * 6,
-        scratch=[pltpu.VMEM((OWN, 3 * SP), F32)],
         moved=2 << 20,
     )(core, parts, *(g[1] for g in grads), one, two)
     received = other_core(sent)

time: 92.2 us -> 89.9 us (0.975)
  waiting for transfers between devices: 3.05 us -> 11.1 us
  starting transfers between devices: 41.8 us -> 35.8 us
  blocking collectives: 28.8 us -> 25.3 us
    ppermute x6, waiting for transfers between devices: 0.37 us -> 9.16 us  [neighbours(): return lax.ppermute(value, tok, pairs)]
    all_to_all x2, blocking collectives: 28.8 us -> 25.3 us  [exchange(): return lax.all_to_all(value, axes, 0, 0, tiled=True)]
    ppermute x6, starting transfers between devices: 27.9 us -> 24.4 us  [neighbours(): return lax.ppermute(value, tok, pairs)]
    ppermute x3 -> x2, starting transfers between devices: 13.9 us -> 11.4 us  [other_core(): return lax.ppermute(value, 'core', [(0, 1), (1, 0)])]
    ppermute x3 -> x2, waiting for transfers between devices: 2.68 us -> 1.92 us  [other_core(): return lax.ppermute(value, 'core', [(0, 1), (1, 0)])]
    pallas_call x7 -> x6, Pallas kernels: 14.9 us -> 14.2 us  [the longest x3 10.2 us: call_relation(): call(functools.partial(relation_kernel, rel), [shape(HALO, SP, BF16), sha...]
  transfers between devices with their start and end apart: 9 -> 8, of which waited for: 3 -> 4; matrix products, arithmetic and copies ran while one was open for 0% -> 0% of each run, Pallas kernels for 8% -> 7%
where the time goes in v6:
time: 89.9 us; the launch traced here: 89.4 us
  starting transfers between devices  35.8 us (40%)
  blocking collectives  25.3 us (28%)
  Pallas kernels  15.4 us (17%)
  waiting for transfers between devices  11.1 us (12%)
  local copies, waits for them, and re-layouts  1.1 us (1%)
    all_to_all x2, blocking collectives, exchange(): return lax.all_to_all(value, axes, 0, 0, tiled=True)  25.3 us
    ppermute x6, starting transfers between devices, neighbours(): return lax.ppermute(value, tok, pairs)  24.4 us
    ppermute x2, starting transfers between devices, other_core(): return lax.ppermute(value, 'core', [(0, 1), (1, 0)])  11.4 us
    pallas_call x3, Pallas kernels, call_relation(): call(functools.partial(relation_kernel, rel), [shape(HALO, SP, BF16), sha...  10.2 us
    ppermute x6, waiting for transfers between devices, neighbours(): return lax.ppermute(value, tok, pairs)  9.16 us
    pallas_call x1, Pallas kernels, body(): call(split_kernel, [shape(BLOCK, WIDTH, BF16)] * 2, [SMEM] + [HBM] * 6, s...  2.62 us
    ppermute x2, waiting for transfers between devices, other_core(): return lax.ppermute(value, 'core', [(0, 1), (1, 0)])  1.92 us
  transfers between devices with their start and end apart: 8, of which 4 were waited for; matrix products, arithmetic and copies ran while one was open for 0% of the time, Pallas kernels for 7%

profile of v6, /device:TPU:1, one launch (start us, length us, event | category | flops | bytes accessed | tf_op | source)
XLA Modules:
  0.0 89.4 jit_solution(7258256768543239670)
XLA Ops:
  0.6 2.6 %shard_map.111 = (bf16[128,2560]{1,0:T(8,128)(2,1)}, bf16[128,2560]{1,0:T(8,128)(2,1)}) custom-call(s32[1]{0:T(128)} %bitcast.core, bf16[128,1280]{1,0:T(8,128)(2,1)} %refs_0_.1, bf16[128,1280]{1,0:T(8,128)(2,1)} %refs_1_.1, bf16[128,1280]{1,0:T(8,128)(2,1)} %refs_2_.1, bf16[128,384]{1,0:T(8,128)(2,1)} %refs_3_.1, bf16[128,384]{1,0:T(8,128)(2,1)} %refs_4_.1, ...), custom_call_target="tpu_custom_call" | custom-call | bytes 4194304 | tf_op jit(solution)/shard_map/pallas_call | solution.py:416
  3.3 8.8 %collective-permute-start = (bf16[128,2560]{1,0:T(8,128)(2,1)}, bf16[128,2560]{1,0:T(8,128)(2,1)S(1)}, u32[]{:S(2)}, u32[]{:S(2)}) collective-permute-start(bf16[128,2560]{1,0:T(8,128)(2,1)} %get-tuple-element.37), channel_id=1, source_target_pairs={{0,4},{4,0},{1,5},{5,1},{2,6},{6,2},{3,7},{7,3},{8,12},{12,8},{9,1... | collective-permute-start | bytes 1966088 | tf_op jit(solution)/shard_map/ppermute | solution.py:408
  12.1 1.9 %collective-permute-done.recv.refs_1_ = bf16[128,2560]{1,0:T(8,128)(2,1)S(1)} collective-permute-done((bf16[128,2560]{1,0:T(8,128)(2,1)}, bf16[128,2560]{1,0:T(8,128)(2,1)S(1)}, u32[]{:S(2)}, u32[]{:S(2)}) %collective-permute-start) | collective-permute-done | bytes 655392 | tf_op jit(solution)/shard_map/ppermute | solution.py:408
  14.0 0.0 copy-start
  14.0 1.1 %copy-done = bf16[128,2560]{1,0:T(8,128)(2,1)S(1)} copy-done((bf16[128,2560]{1,0:T(8,128)(2,1)S(1)}, bf16[128,2560]{1,0:T(8,128)(2,1)}, u32[]{:S(2)}) %copy-start) | copy-done | bytes 655384
  15.1 1.2 %shard_map.112 = (bf16[192,1664]{1,0:T(8,128)(2,1)S(1)}, bf16[192,1664]{1,0:T(8,128)(2,1)}, bf16[192,896]{1,0:T(8,128)(2,1)}, bf16[192,896]{1,0:T(8,128)(2,1)}) custom-call(s32[1]{0:T(128)} %bitcast.core, bf16[128,2560]{1,0:T(8,128)(2,1)S(1)} %copy-done, bf16[128,2560]{1,0:T(8,128)(2,1)S(1)} %collective-permute-done.recv.refs_1_), custom_call_target="tpu_custom_call" | custom-call | bytes 2097152 | tf_op jit(solution)/shard_map/pallas_call | solution.py:425
  16.3 1.9 %collective-permute-start.2 = (bf16[192,1664]{1,0:T(8,128)(2,1)}, bf16[192,1664]{1,0:T(8,128)(2,1)S(1)}, u32[]{:S(2)}, u32[]{:S(2)}) collective-permute-start(bf16[192,1664]{1,0:T(8,128)(2,1)} %get-tuple-element.43), channel_id=1, source_target_pairs={{0,504},{4,12},{8,0},{12,20},{16,8},{20,28},{24,16},{28,36},{32,24... | collective-permute-start | bytes 1916936 | tf_op jit(solution)/shard_map/ppermute | solution.py:413
  18.2 8.2 %collective-permute-start.1 = (bf16[192,1664]{1,0:T(8,128)(2,1)S(1)}, bf16[192,1664]{1,0:T(8,128)(2,1)S(1)}, u32[]{:S(2)}, u32[]{:S(2)}) collective-permute-start(bf16[192,1664]{1,0:T(8,128)(2,1)S(1)} %get-tuple-element.38), channel_id=1, source_target_pairs={{0,8},{4,508},{8,16},{12,4},{16,24},{20,12},{24,32},{28,20},{32,40... | collective-permute-start | bytes 1916936 | tf_op jit(solution)/shard_map/ppermute | solution.py:413
  26.4 3.4 %collective-permute-start.3 = (bf16[192,896]{1,0:T(8,128)(2,1)}, bf16[192,896]{1,0:T(8,128)(2,1)}, u32[]{:S(2)}, u32[]{:S(2)}) collective-permute-start(bf16[192,896]{1,0:T(8,128)(2,1)} %get-tuple-element.46), channel_id=1, source_target_pairs={{0,8},{4,508},{8,16},{12,4},{16,24},{20,12},{24,32},{28,20},{32,40... | collective-permute-start | bytes 1032200 | tf_op jit(solution)/shard_map/ppermute | solution.py:413
  29.8 1.9 %collective-permute-start.4 = (bf16[192,896]{1,0:T(8,128)(2,1)}, bf16[192,896]{1,0:T(8,128)(2,1)}, u32[]{:S(2)}, u32[]{:S(2)}) collective-permute-start(bf16[192,896]{1,0:T(8,128)(2,1)} %get-tuple-element.47), channel_id=1, source_target_pairs={{0,504},{4,12},{8,0},{12,20},{16,8},{20,28},{24,16},{28,36},{32,24... | collective-permute-start | bytes 1032200 | tf_op jit(solution)/shard_map/ppermute | solution.py:413
  31.7 0.0 copy-done.2
  31.7 0.0 copy-done.3
  31.7 0.2 shard_map.113
  32.0 0.5 collective-permute-done.2.refs_3_
  32.5 8.1 %collective-permute-done.1.refs_2_ = bf16[192,1664]{1,0:T(8,128)(2,1)S(1)} collective-permute-done((bf16[192,1664]{1,0:T(8,128)(2,1)S(1)}, bf16[192,1664]{1,0:T(8,128)(2,1)S(1)}, u32[]{:S(2)}, u32[]{:S(2)}) %collective-permute-start.1) | collective-permute-done | bytes 639008 | tf_op jit(solution)/shard_map/ppermute | solution.py:413
  40.6 0.0 copy-done.1
  40.6 3.0 %shard_map.114 = (bf16[192,256]{1,0:T(8,128)(2,1)S(1)}, f32[256,256]{1,0:T(8,128)S(1)}, bf16[192,256]{1,0:T(8,128)(2,1)S(1)}, f32[1,128]{1,0:T(1,128)S(1)}) custom-call(s32[1]{0:T(128)} %bitcast.core, s32[1,256]{1,0:T(1,128)S(1)} %get-tuple-element.41.starts, f32[1,256]{1,0:T(1,128)S(1)} %get-tuple-element.42.weights, f32[1,128]{1,0:T(1,128)S(1)} %broadcast_in_dim.3.loss_in, ...), custom_call_target="tpu_custom_call" | custom-call | flops 1342177280 | bytes 2097152 | tf_op jit(solution)/shard_map/pallas_call | solution.py:375
  43.6 3.0 %shard_map.115 = (bf16[192,256]{1,0:T(8,128)(2,1)S(1)}, f32[256,256]{1,0:T(8,128)S(1)}, bf16[192,256]{1,0:T(8,128)(2,1)S(1)}, f32[1,128]{1,0:T(1,128)S(1)}) custom-call(s32[1]{0:T(128)} %bitcast.core, s32[1,256]{1,0:T(1,128)S(1)} %get-tuple-element.41.starts, f32[1,256]{1,0:T(1,128)S(1)} %get-tuple-element.42.weights, ...), custom_call_target="tpu_custom_call" | custom-call | flops 1342177280 | bytes 2097152 | tf_op jit(solution)/shard_map/pallas_call | solution.py:375
  46.6 0.5 collective-permute-done.3.refs_2_
  47.2 0.0 collective-permute-done.4.refs_3_
  47.2 4.1 %shard_map.116 = (bf16[192,256]{1,0:T(8,128)(2,1)S(1)}, f32[256,256]{1,0:T(8,128)S(1)}, bf16[192,256]{1,0:T(8,128)(2,1)S(1)}, f32[1,128]{1,0:T(1,128)S(1)}) custom-call(s32[1]{0:T(128)} %bitcast.core, s32[1,256]{1,0:T(1,128)S(1)} %get-tuple-element.41.starts, f32[1,256]{1,0:T(1,128)S(1)} %get-tuple-element.42.weights, ...), custom_call_target="tpu_custom_call" | custom-call | flops 1342177280 | bytes 2097152 | tf_op jit(solution)/shard_map/pallas_call | solution.py:375
  51.3 0.1 shard_map.117
  51.4 7.1 %collective-permute-start.5 = (bf16[192,768]{1,0:T(8,128)(2,1)S(1)}, bf16[192,768]{1,0:T(8,128)(2,1)S(1)}, u32[]{:S(2)}, u32[]{:S(2)}) collective-permute-start(bf16[192,768]{1,0:T(8,128)(2,1)S(1)} %get-tuple-element.59), channel_id=1, source_target_pairs={{0,8},{4,508},{8,16},{12,4},{16,24},{20,12},{24,32},{28,20},{32,40... | collective-permute-start | bytes 884744 | tf_op jit(solution)/shard_map/ppermute | solution.py:413
  58.5 1.9 %collective-permute-start.6 = (bf16[192,768]{1,0:T(8,128)(2,1)S(1)}, bf16[192,768]{1,0:T(8,128)(2,1)S(1)}, u32[]{:S(2)}, u32[]{:S(2)}) collective-permute-start(bf16[192,768]{1,0:T(8,128)(2,1)S(1)} %get-tuple-element.60), channel_id=1, source_target_pairs={{0,508},{4,8},{8,4},{12,16},{16,12},{20,24},{24,20},{28,32},{32,28... | collective-permute-start | bytes 884744 | tf_op jit(solution)/shard_map/ppermute | solution.py:413
  60.5 10.2 %all_to_all.22 = f32[16,1,128]{2,1,0:T(1,128)S(1)} all-to-all(f32[16,1,128]{2,1,0:T(1,128)S(1)} %bitcast.18), channel_id=1, replica_groups=mesh['y'=8,'z'=4,'parity'=2,'core'=2,'head'=4] {'z','parity','core'}, dimensions={0} | all-to-all | bytes 16384 | tf_op jit(solution)/shard_map/all_to_all | solution.py:456
  70.7 0.0 collective-permute-done.5.mine
  70.7 0.0 collective-permute-done.6.other
  70.7 0.1 shard_map.118
  70.8 2.6 %collective-permute-start.7 = (f32[192,768]{1,0:T(8,128)S(1)}, f32[192,768]{1,0:T(8,128)S(1)}, u32[]{:S(2)}, u32[]{:S(2)}) collective-permute-start(f32[192,768]{1,0:T(8,128)S(1)} %get-tuple-element.63), channel_id=1, source_target_pairs={{0,4},{4,0},{1,5},{5,1},{2,6},{6,2},{3,7},{7,3},{8,12},{12,8},{9,1... | collective-permute-start | bytes 1769480 | tf_op jit(solution)/shard_map/ppermute | solution.py:408
  73.4 15.0 %all_to_all.23 = f32[32,1,128]{2,1,0:T(1,128)S(1)} all-to-all(f32[32,1,128]{2,1,0:T(1,128)S(1)} %bitcast.17), channel_id=1, replica_groups=mesh['y'=8,'z'=4,'parity'=2,'core'=2,'head'=4] {'y','head'}, dimensions={0} | all-to-all | bytes 32768 | tf_op jit(solution)/shard_map/all_to_all | solution.py:456
  88.4 0.0 collective-permute-done.7.recv
  88.5 1.0 %shard_map.119 = (f32[128,384]{1,0:T(8,128)}, f32[128,384]{1,0:T(8,128)}, f32[128,384]{1,0:T(8,128)}, f32[1,1]{1,0:T(1,128)}) custom-call(s32[1]{0:T(128)} %bitcast.core, f32[32,128]{1,0:T(8,128)S(1)} %bitcast.13, f32[256,768]{1,0:T(8,128)S(1)} %get-tuple-element.62.keep, f32[192,768]{1,0:T(8,128)S(1)} %collective-permute-done.7.recv), custom_call_target="tpu_custom_call" | custom-call | bytes 1048576 | tf_op jit(solution)/shard_map/pallas_call | solution.py:475
  (4 shorter events, 0.0 us)
Async XLA Ops:
  3.3 10.7 %collective-permute-start = (bf16[128,2560]{1,0:T(8,128)(2,1)}, bf16[128,2560]{1,0:T(8,128)(2,1)S(1)}, u32[]{:S(2)}, u32[]{:S(2)}) collective-permute-start(bf16[128,2560]{1,0:T(8,128)(2,1)} %get-tuple-element.37), channel_id=1, source_target_pairs={{0,4},{4,0},{1,5},{5,1},{2,6},{6,2},{3,7},{7,3},{8,12},{12,8},{9,1... | collective-permute-start | bytes 1966088 | tf_op jit(solution)/shard_map/ppermute | solution.py:408
  14.0 1.1 %copy-start = (bf16[128,2560]{1,0:T(8,128)(2,1)S(1)}, bf16[128,2560]{1,0:T(8,128)(2,1)}, u32[]{:S(2)}) copy-start(bf16[128,2560]{1,0:T(8,128)(2,1)} %get-tuple-element.36.keep.refs_0_) | copy-start | bytes 1966084
  15.1 16.7 %copy-start.2 = (s32[16384]{0:T(1024)S(1)}, s32[16384]{0:T(1024)}, u32[]{:S(2)}) copy-start(s32[16384]{0:T(1024)} %param.14) | copy-start | bytes 196612
  15.1 16.7 %copy-start.3 = (f32[16384]{0:T(1024)S(1)}, f32[16384]{0:T(1024)}, u32[]{:S(2)}) copy-start(f32[16384]{0:T(1024)} %param.15) | copy-start | bytes 196612
  15.1 25.5 %copy-start.1 = (bf16[128,2560]{1,0:T(8,128)(2,1)S(1)}, bf16[128,2560]{1,0:T(8,128)(2,1)}, u32[]{:S(2)}) copy-start(bf16[128,2560]{1,0:T(8,128)(2,1)} %get-tuple-element.36.keep.refs_0_) | copy-start | bytes 1966084
  16.3 16.2 %collective-permute-start.2 = (bf16[192,1664]{1,0:T(8,128)(2,1)}, bf16[192,1664]{1,0:T(8,128)(2,1)S(1)}, u32[]{:S(2)}, u32[]{:S(2)}) collective-permute-start(bf16[192,1664]{1,0:T(8,128)(2,1)} %get-tuple-element.43), channel_id=1, source_target_pairs={{0,504},{4,12},{8,0},{12,20},{16,8},{20,28},{24,16},{28,36},{32,24... | collective-permute-start | bytes 1916936 | tf_op jit(solution)/shard_map/ppermute | solution.py:413
  18.2 22.4 %collective-permute-start.1 = (bf16[192,1664]{1,0:T(8,128)(2,1)S(1)}, bf16[192,1664]{1,0:T(8,128)(2,1)S(1)}, u32[]{:S(2)}, u32[]{:S(2)}) collective-permute-start(bf16[192,1664]{1,0:T(8,128)(2,1)S(1)} %get-tuple-element.38), channel_id=1, source_target_pairs={{0,8},{4,508},{8,16},{12,4},{16,24},{20,12},{24,32},{28,20},{32,40... | collective-permute-start | bytes 1916936 | tf_op jit(solution)/shard_map/ppermute | solution.py:413
  26.4 20.8 %collective-permute-start.3 = (bf16[192,896]{1,0:T(8,128)(2,1)}, bf16[192,896]{1,0:T(8,128)(2,1)}, u32[]{:S(2)}, u32[]{:S(2)}) collective-permute-start(bf16[192,896]{1,0:T(8,128)(2,1)} %get-tuple-element.46), channel_id=1, source_target_pairs={{0,8},{4,508},{8,16},{12,4},{16,24},{20,12},{24,32},{28,20},{32,40... | collective-permute-start | bytes 1032200 | tf_op jit(solution)/shard_map/ppermute | solution.py:413
  29.8 17.4 %collective-permute-start.4 = (bf16[192,896]{1,0:T(8,128)(2,1)}, bf16[192,896]{1,0:T(8,128)(2,1)}, u32[]{:S(2)}, u32[]{:S(2)}) collective-permute-start(bf16[192,896]{1,0:T(8,128)(2,1)} %get-tuple-element.47), channel_id=1, source_target_pairs={{0,504},{4,12},{8,0},{12,20},{16,8},{20,28},{24,16},{28,36},{32,24... | collective-permute-start | bytes 1032200 | tf_op jit(solution)/shard_map/ppermute | solution.py:413
  51.4 19.3 %collective-permute-start.5 = (bf16[192,768]{1,0:T(8,128)(2,1)S(1)}, bf16[192,768]{1,0:T(8,128)(2,1)S(1)}, u32[]{:S(2)}, u32[]{:S(2)}) collective-permute-start(bf16[192,768]{1,0:T(8,128)(2,1)S(1)} %get-tuple-element.59), channel_id=1, source_target_pairs={{0,8},{4,508},{8,16},{12,4},{16,24},{20,12},{24,32},{28,20},{32,40... | collective-permute-start | bytes 884744 | tf_op jit(solution)/shard_map/ppermute | solution.py:413
  58.5 12.2 %collective-permute-start.6 = (bf16[192,768]{1,0:T(8,128)(2,1)S(1)}, bf16[192,768]{1,0:T(8,128)(2,1)S(1)}, u32[]{:S(2)}, u32[]{:S(2)}) collective-permute-start(bf16[192,768]{1,0:T(8,128)(2,1)S(1)} %get-tuple-element.60), channel_id=1, source_target_pairs={{0,508},{4,8},{8,4},{12,16},{16,12},{20,24},{24,20},{28,32},{32,28... | collective-permute-start | bytes 884744 | tf_op jit(solution)/shard_map/ppermute | solution.py:413
  70.8 17.6 %collective-permute-start.7 = (f32[192,768]{1,0:T(8,128)S(1)}, f32[192,768]{1,0:T(8,128)S(1)}, u32[]{:S(2)}, u32[]{:S(2)}) collective-permute-start(f32[192,768]{1,0:T(8,128)S(1)} %get-tuple-element.63), channel_id=1, source_target_pairs={{0,4},{4,0},{1,5},{5,1},{2,6},{6,2},{3,7},{7,3},{8,12},{12,8},{9,1... | collective-permute-start | bytes 1769480 | tf_op jit(solution)/shard_map/ppermute | solution.py:408

commit v7 on v6

--- a/solution.py
+++ b/solution.py
@@ -24,12 +24,11 @@
 SW = HEADS * DS
 SP = 256
 REL = TW + SP
-WIDTH_A = 2 * TW + 2 * SW
-WIDTH = WIDTH_A + REL
-T_AT = (0, TW, 0)
-S_AT = (2 * TW, 2 * TW + 128, TW)
-CHUNK_AT = (0, 0, WIDTH_A)
-S_OFF = (0, SW - 128, 0)
+PART = 2 * TW
+WIDTH = 2 * PART
+T_AT = (0, PART, PART + TW)
+S_AT = (TW, TW + SP, TW + SP + 128)
+S_OFF = (0, 0, SW - 128)
 CT = DT ** (-0.5) * math.log2(math.e)
 CS = DS ** (-0.5) * math.log2(math.e)
 NT = (((1,), (1,)), ((), ()))
@@ -70,7 +69,7 @@
     ours, theirs = [], []
     for rel in range(3):
         teacher, student = buffers[rel], buffers[3 + rel]
-        at = CHUNK_AT[rel] + T_AT[rel]
+        at = T_AT[rel]
         keep[:, at : at + TW] = teacher[:, mine]
         send[:, at : at + TW] = teacher[:, other]
         low = jnp.where(lane < SW, student[:, :SP].astype(F32), 0.0)
@@ -79,12 +78,12 @@
         ours.append(jnp.where(me == 0, low, high))
         theirs.append(jnp.where(me == 0, high, low))
     for halves, out in ((ours, keep), (theirs, send)):
-        second = pltpu.roll(halves[1], S_OFF[1], 1)
-        at = 2 * TW
-        out[:, at : at + 128] = halves[0][:, :128].astype(BF16)
-        out[:, at + 128 : at + 256] = (halves[0][:, 128:] + second[:, :128]).astype(BF16)
+        out[:, TW : TW + SP] = halves[0].astype(BF16)
+        second = pltpu.roll(halves[2], S_OFF[2], 1)
+        at = S_AT[1]
+        out[:, at : at + 128] = halves[1][:, :128].astype(BF16)
+        out[:, at + 128 : at + 256] = (halves[1][:, 128:] + second[:, :128]).astype(BF16)
         out[:, at + 256 : at + 384] = second[:, 128:].astype(BF16)
-        out[:, WIDTH_A + TW :] = halves[2].astype(BF16)
 
 
 def mask_kernel(chip, docs, rows, starts, weights):
@@ -115,24 +114,32 @@
     weights[...] = queries([row_of(rows, r) for r in range(3, 6)])
 
 
-def edges_kernel(core, keep, recv, *outs):
+def edges_kernel(cols, core, keep, recv, *refs):
+    one, two = refs[-2:]
     half = HALO - BLOCK
-    for chunk, cols in enumerate((slice(0, WIDTH_A), slice(WIDTH_A, WIDTH))):
-        one, two = outs[2 * chunk : 2 * chunk + 2]
-
-        def write(first, second, after, before):
-            after[:half, :] = first[BLOCK - half :, cols]
-            after[half:, :] = second[:, cols]
-            before[:BLOCK, :] = first[:, cols]
-            before[BLOCK:, :] = second[:half, cols]
-
-        @pl.when(core[0] == 0)
-        def _():
-            write(keep, recv, one, two)
-
-        @pl.when(core[0] != 0)
-        def _():
-            write(recv, keep, two, one)
+
+    def write(first, second, after, before):
+        after[:half, :] = first[BLOCK - half :, cols]
+        after[half:, :] = second[:, cols]
+        before[:BLOCK, :] = first[:, cols]
+        before[BLOCK:, :] = second[:half, cols]
+
+    @pl.when(core[0] == 0)
+    def _():
+        write(keep, recv, one, two)
+
+    @pl.when(core[0] != 0)
+    def _():
+        write(recv, keep, two, one)
+
+
+def call_edges(cols, core, keep, recv, *after):
+    return call(
+        functools.partial(edges_kernel, cols),
+        [shape(HALO, cols.stop - cols.start, BF16)] * 2,
+        [SMEM] + [VMEM] * (2 + len(after)),
+        moved=2 << 20,
+    )(core, keep, recv, *after)
 
 
 def fold(value, op):
@@ -148,20 +155,21 @@
     loss_in,
     *refs,
 ):
-    keep, recv, one, two = refs[:-12]
+    keep, recv, *halo = refs[:-12]
+    grad_left, grad_own, grad_right, loss_out, win, bias, rt, rs, gt, qs, bt, kg = refs[-12:]
     t_at, s_at, s_off = T_AT[rel], S_AT[rel], S_OFF[rel]
-    grad_left, grad_own, grad_right, loss_out, win, bias, rt, rs, gt, qs, bt, kg = refs[-12:]
     me = core[0]
-    def gather(at, rows, source):
-        base = CHUNK_AT[rel] if source.shape[1] == WIDTH else 0
-        win[at : at + rows, :TW] = source[:, base + t_at : base + t_at + TW]
-        win[at : at + rows, TW:] = source[:, base + s_at : base + s_at + SP]
 
     def gather_all(*sources):
         at = 0
         for source in sources:
-            gather(at, source.shape[0], source)
-            at += source.shape[0]
+            t_source, s_source = source if isinstance(source, tuple) else (source, source)
+            rows, width = t_source.shape
+            win[at : at + rows, :TW] = t_source[:, t_at % width : t_at % width + TW]
+            win[at : at + rows, TW:] = s_source[:, s_at : s_at + SP]
+            at += rows
+
+    one, two = (halo[-2], halo[0]), (halo[-1], halo[1])
 
     @pl.when(me == 0)
     def _():
@@ -422,16 +430,9 @@
         limit=56,
     )(core, *arrays)
     recv = other_core(send)
-    edges = call(
-        edges_kernel,
-        [shape(HALO, WIDTH_A, BF16)] * 2 + [shape(HALO, REL, BF16)] * 2,
-        [SMEM] + [VMEM] * 2,
-        moved=2 << 20,
-    )(core, keep, recv)
-    halo_a = [neighbours(edges[0], 1), neighbours(edges[1], -1)]
-    halo_b = [neighbours(edges[2], 1), neighbours(edges[3], -1)]
-
-    doc_ids, row_weight, _ = lax.optimization_barrier((doc_ids, row_weight, edges[0]))
+    edges_a = call_edges(slice(0, PART), core, keep, recv)
+    halo_a = [neighbours(edges_a[0], 1), neighbours(edges_a[1], -1)]
+    doc_ids, row_weight, _ = lax.optimization_barrier((doc_ids, row_weight, edges_a[0]))
     starts, weight = call(
         mask_kernel,
         [shape(1, OWN, jnp.int32), shape(1, OWN, F32)],
@@ -442,10 +443,13 @@
         doc_ids.reshape(-1, BLOCK),
         row_weight.reshape(-1, BLOCK),
     )
+    edges_b = call_edges(slice(PART, WIDTH), core, keep, recv, weight)
+    halo_b = [neighbours(edges_b[0], 1), neighbours(edges_b[1], -1)]
+
     loss = jnp.zeros((1, BLOCK), F32)
     grads = []
     for rel in range(3):
-        chunk = (keep, recv, *(halo_b if rel == 2 else halo_a))
+        chunk = (keep, recv, *halo_a, *(halo_b if rel else ()))
         *grad, loss = call_relation(rel, core, starts, weight, loss, chunk)
         grads.append(grad)
 

time: 89.9 us -> 90.7 us (level)
  waiting for transfers between devices: 11.1 us -> 15.5 us
  starting transfers between devices: 35.8 us -> 33.5 us
  Pallas kernels: 15.4 us -> 13.3 us
    ppermute x6, waiting for transfers between devices: 9.16 us -> 13.5 us  [neighbours(): return lax.ppermute(value, tok, pairs)]
    ppermute x6, starting transfers between devices: 24.4 us -> 22.1 us  [neighbours(): return lax.ppermute(value, tok, pairs)]
    pallas_call x1 -> x2, Pallas kernels: 1.22 us -> 0.14 us  [call_edges(): call(functools.partial(edges_kernel, cols), [shape(HALO, cols.stop - cols...]
    pallas_call x3, Pallas kernels: 10.2 us -> 9.11 us  [call_relation(): call(functools.partial(relation_kernel, rel), [shape(HALO, SP, BF16), sha...]
  transfers between devices with their start and end apart: 8 -> 8, of which waited for: 4 -> 4; matrix products, arithmetic and copies ran while one was open for 0% -> 0% of each run, Pallas kernels for 7% -> 4%
where the time goes in v7:
time: 90.7 us; the launch traced here: 90.2 us
  starting transfers between devices  33.5 us (37%)
  blocking collectives  26.1 us (29%)
  waiting for transfers between devices  15.5 us (17%)
  Pallas kernels  13.3 us (15%)
  local copies, waits for them, and re-layouts  1.1 us (1%)
    all_to_all x2, blocking collectives, exchange(): return lax.all_to_all(value, axes, 0, 0, tiled=True)  26.1 us
    ppermute x6, starting transfers between devices, neighbours(): return lax.ppermute(value, tok, pairs)  22.1 us
    ppermute x6, waiting for transfers between devices, neighbours(): return lax.ppermute(value, tok, pairs)  13.5 us
    ppermute x2, starting transfers between devices, other_core(): return lax.ppermute(value, 'core', [(0, 1), (1, 0)])  11.3 us
    pallas_call x3, Pallas kernels, call_relation(): call(functools.partial(relation_kernel, rel), [shape(HALO, SP, BF16), sha...  9.11 us
    pallas_call x1, Pallas kernels, body(): call(split_kernel, [shape(BLOCK, WIDTH, BF16)] * 2, [SMEM] + [HBM] * 6, s...  2.63 us
    ppermute x2, waiting for transfers between devices, other_core(): return lax.ppermute(value, 'core', [(0, 1), (1, 0)])  1.92 us
  transfers between devices with their start and end apart: 8, of which 4 were waited for; matrix products, arithmetic and copies ran while one was open for 0% of the time, Pallas kernels for 4%

profile of v7, /device:TPU:1, one launch (start us, length us, event | category | flops | bytes accessed | tf_op | source)
XLA Modules:
  0.0 90.2 jit_solution(13753256514226207596)
XLA Ops:
  0.6 2.6 %shard_map.111 = (bf16[128,2560]{1,0:T(8,128)(2,1)}, bf16[128,2560]{1,0:T(8,128)(2,1)}) custom-call(s32[1]{0:T(128)} %bitcast.core, bf16[128,1280]{1,0:T(8,128)(2,1)} %refs_0_.1, bf16[128,1280]{1,0:T(8,128)(2,1)} %refs_1_.1, bf16[128,1280]{1,0:T(8,128)(2,1)} %refs_2_.1, bf16[128,384]{1,0:T(8,128)(2,1)} %refs_3_.1, bf16[128,384]{1,0:T(8,128)(2,1)} %refs_4_.1, ...), custom_call_target="tpu_custom_call" | custom-call | bytes 4194304 | tf_op jit(solution)/shard_map/pallas_call | solution.py:424
  3.3 8.8 %collective-permute-start = (bf16[128,2560]{1,0:T(8,128)(2,1)}, bf16[128,2560]{1,0:T(8,128)(2,1)S(1)}, u32[]{:S(2)}, u32[]{:S(2)}) collective-permute-start(bf16[128,2560]{1,0:T(8,128)(2,1)} %get-tuple-element.37), channel_id=1, source_target_pairs={{0,4},{4,0},{1,5},{5,1},{2,6},{6,2},{3,7},{7,3},{8,12},{12,8},{9,1... | collective-permute-start | bytes 1966088 | tf_op jit(solution)/shard_map/ppermute | solution.py:416
  12.1 1.9 %collective-permute-done.recv.refs_1_ = bf16[128,2560]{1,0:T(8,128)(2,1)S(1)} collective-permute-done((bf16[128,2560]{1,0:T(8,128)(2,1)}, bf16[128,2560]{1,0:T(8,128)(2,1)S(1)}, u32[]{:S(2)}, u32[]{:S(2)}) %collective-permute-start) | collective-permute-done | bytes 655392 | tf_op jit(solution)/shard_map/ppermute | solution.py:416
  14.0 1.1 %copy-done = bf16[128,2560]{1,0:T(8,128)(2,1)S(1)} copy-done((bf16[128,2560]{1,0:T(8,128)(2,1)S(1)}, bf16[128,2560]{1,0:T(8,128)(2,1)}, u32[]{:S(2)}) %copy-start) | copy-done | bytes 655384
  15.1 0.1 shard_map.112
  15.1 2.1 %collective-permute-start.2 = (bf16[192,1280]{1,0:T(8,128)(2,1)S(1)}, bf16[192,1280]{1,0:T(8,128)(2,1)S(1)}, u32[]{:S(2)}, u32[]{:S(2)}) collective-permute-start(bf16[192,1280]{1,0:T(8,128)(2,1)S(1)} %get-tuple-element.43), channel_id=1, source_target_pairs={{0,504},{4,12},{8,0},{12,20},{16,8},{20,28},{24,16},{28,36},{32,24... | collective-permute-start | bytes 1474568 | tf_op jit(solution)/shard_map/ppermute | solution.py:421
  17.2 8.2 %collective-permute-start.1 = (bf16[192,1280]{1,0:T(8,128)(2,1)S(1)}, bf16[192,1280]{1,0:T(8,128)(2,1)S(1)}, u32[]{:S(2)}, u32[]{:S(2)}) collective-permute-start(bf16[192,1280]{1,0:T(8,128)(2,1)S(1)} %get-tuple-element.38), channel_id=1, source_target_pairs={{0,8},{4,508},{8,16},{12,4},{16,24},{20,12},{24,32},{28,20},{32,40... | collective-permute-start | bytes 1474568 | tf_op jit(solution)/shard_map/ppermute | solution.py:421
  25.4 0.0 copy-done.2
  25.4 0.0 copy-done.3
  25.4 0.2 shard_map.113
  25.7 0.0 copy-done.1
  25.7 0.1 shard_map.115
  25.8 3.4 %collective-permute-start.3 = (bf16[192,1280]{1,0:T(8,128)(2,1)S(1)}, bf16[192,1280]{1,0:T(8,128)(2,1)S(1)}, u32[]{:S(2)}, u32[]{:S(2)}) collective-permute-start(bf16[192,1280]{1,0:T(8,128)(2,1)S(1)} %get-tuple-element.45), channel_id=1, source_target_pairs={{0,8},{4,508},{8,16},{12,4},{16,24},{20,12},{24,32},{28,20},{32,40... | collective-permute-start | bytes 1474568 | tf_op jit(solution)/shard_map/ppermute | solution.py:421
  29.1 1.9 %collective-permute-start.4 = (bf16[192,1280]{1,0:T(8,128)(2,1)S(1)}, bf16[192,1280]{1,0:T(8,128)(2,1)S(1)}, u32[]{:S(2)}, u32[]{:S(2)}) collective-permute-start(bf16[192,1280]{1,0:T(8,128)(2,1)S(1)} %get-tuple-element.46), channel_id=1, source_target_pairs={{0,504},{4,12},{8,0},{12,20},{16,8},{20,28},{24,16},{28,36},{32,24... | collective-permute-start | bytes 1474568 | tf_op jit(solution)/shard_map/ppermute | solution.py:421
  31.1 0.0 collective-permute-done.2.refs_3_
  31.1 4.3 %collective-permute-done.1.refs_2_ = bf16[192,1280]{1,0:T(8,128)(2,1)S(1)} collective-permute-done((bf16[192,1280]{1,0:T(8,128)(2,1)S(1)}, bf16[192,1280]{1,0:T(8,128)(2,1)S(1)}, u32[]{:S(2)}, u32[]{:S(2)}) %collective-permute-start.1) | collective-permute-done | bytes 491552 | tf_op jit(solution)/shard_map/ppermute | solution.py:421
  35.4 3.0 %shard_map.114 = (bf16[192,256]{1,0:T(8,128)(2,1)S(1)}, f32[256,256]{1,0:T(8,128)S(1)}, bf16[192,256]{1,0:T(8,128)(2,1)S(1)}, f32[1,128]{1,0:T(1,128)S(1)}) custom-call(s32[1]{0:T(128)} %bitcast.core, s32[1,256]{1,0:T(1,128)S(1)} %get-tuple-element.41.starts, f32[1,256]{1,0:T(1,128)S(1)} %get-tuple-element.42.weights.refs_0_, ...), custom_call_target="tpu_custom_call" | custom-call | flops 1342177280 | bytes 2097152 | tf_op jit(solution)/shard_map/pallas_call | solution.py:383
  38.4 6.5 %collective-permute-done.3.refs_4_ = bf16[192,1280]{1,0:T(8,128)(2,1)S(1)} collective-permute-done((bf16[192,1280]{1,0:T(8,128)(2,1)S(1)}, bf16[192,1280]{1,0:T(8,128)(2,1)S(1)}, u32[]{:S(2)}, u32[]{:S(2)}) %collective-permute-start.3) | collective-permute-done | bytes 491552 | tf_op jit(solution)/shard_map/ppermute | solution.py:421
  44.9 2.8 %collective-permute-done.4.refs_5_ = bf16[192,1280]{1,0:T(8,128)(2,1)S(1)} collective-permute-done((bf16[192,1280]{1,0:T(8,128)(2,1)S(1)}, bf16[192,1280]{1,0:T(8,128)(2,1)S(1)}, u32[]{:S(2)}, u32[]{:S(2)}) %collective-permute-start.4) | collective-permute-done | bytes 491552 | tf_op jit(solution)/shard_map/ppermute | solution.py:421
  47.7 3.0 %shard_map.116 = (bf16[192,256]{1,0:T(8,128)(2,1)S(1)}, f32[256,256]{1,0:T(8,128)S(1)}, bf16[192,256]{1,0:T(8,128)(2,1)S(1)}, f32[1,128]{1,0:T(1,128)S(1)}) custom-call(s32[1]{0:T(128)} %bitcast.core, s32[1,256]{1,0:T(1,128)S(1)} %get-tuple-element.41.starts, f32[1,256]{1,0:T(1,128)S(1)} %get-tuple-element.42.weights.refs_0_, ...), custom_call_target="tpu_custom_call" | custom-call | flops 1342177280 | bytes 2097152 | tf_op jit(solution)/shard_map/pallas_call | solution.py:383
  50.7 3.0 %shard_map.117 = (bf16[192,256]{1,0:T(8,128)(2,1)S(1)}, f32[256,256]{1,0:T(8,128)S(1)}, bf16[192,256]{1,0:T(8,128)(2,1)S(1)}, f32[1,128]{1,0:T(1,128)S(1)}) custom-call(s32[1]{0:T(128)} %bitcast.core, s32[1,256]{1,0:T(1,128)S(1)} %get-tuple-element.41.starts, f32[1,256]{1,0:T(1,128)S(1)} %get-tuple-element.42.weights.refs_0_, ...), custom_call_target="tpu_custom_call" | custom-call | flops 1342177280 | bytes 2097152 | tf_op jit(solution)/shard_map/pallas_call | solution.py:383
  53.7 0.1 shard_map.118
  53.8 4.7 %collective-permute-start.5 = (bf16[192,768]{1,0:T(8,128)(2,1)S(1)}, bf16[192,768]{1,0:T(8,128)(2,1)S(1)}, u32[]{:S(2)}, u32[]{:S(2)}) collective-permute-start(bf16[192,768]{1,0:T(8,128)(2,1)S(1)} %get-tuple-element.59), channel_id=1, source_target_pairs={{0,8},{4,508},{8,16},{12,4},{16,24},{20,12},{24,32},{28,20},{32,40... | collective-permute-start | bytes 884744 | tf_op jit(solution)/shard_map/ppermute | solution.py:421
  58.5 1.9 %collective-permute-start.6 = (bf16[192,768]{1,0:T(8,128)(2,1)S(1)}, bf16[192,768]{1,0:T(8,128)(2,1)S(1)}, u32[]{:S(2)}, u32[]{:S(2)}) collective-permute-start(bf16[192,768]{1,0:T(8,128)(2,1)S(1)} %get-tuple-element.60), channel_id=1, source_target_pairs={{0,508},{4,8},{8,4},{12,16},{16,12},{20,24},{24,20},{28,32},{32,28... | collective-permute-start | bytes 884744 | tf_op jit(solution)/shard_map/ppermute | solution.py:421
  60.4 10.2 %all_to_all.22 = f32[16,1,128]{2,1,0:T(1,128)S(1)} all-to-all(f32[16,1,128]{2,1,0:T(1,128)S(1)} %bitcast.18), channel_id=1, replica_groups=mesh['y'=8,'z'=4,'parity'=2,'core'=2,'head'=4] {'z','parity','core'}, dimensions={0} | all-to-all | bytes 16384 | tf_op jit(solution)/shard_map/all_to_all | solution.py:460
  70.6 0.0 collective-permute-done.5.mine
  70.6 0.0 collective-permute-done.6.other
  70.6 0.1 shard_map.119
  70.8 2.6 %collective-permute-start.7 = (f32[192,768]{1,0:T(8,128)S(1)}, f32[192,768]{1,0:T(8,128)S(1)}, u32[]{:S(2)}, u32[]{:S(2)}) collective-permute-start(f32[192,768]{1,0:T(8,128)S(1)} %get-tuple-element.63), channel_id=1, source_target_pairs={{0,4},{4,0},{1,5},{5,1},{2,6},{6,2},{3,7},{7,3},{8,12},{12,8},{9,1... | collective-permute-start | bytes 1769480 | tf_op jit(solution)/shard_map/ppermute | solution.py:416
  73.4 15.9 %all_to_all.23 = f32[32,1,128]{2,1,0:T(1,128)S(1)} all-to-all(f32[32,1,128]{2,1,0:T(1,128)S(1)} %bitcast.17), channel_id=1, replica_groups=mesh['y'=8,'z'=4,'parity'=2,'core'=2,'head'=4] {'y','head'}, dimensions={0} | all-to-all | bytes 32768 | tf_op jit(solution)/shard_map/all_to_all | solution.py:460
  89.2 0.0 collective-permute-done.7.recv
  89.2 1.0 %shard_map.120 = (f32[128,384]{1,0:T(8,128)}, f32[128,384]{1,0:T(8,128)}, f32[128,384]{1,0:T(8,128)}, f32[1,1]{1,0:T(1,128)}) custom-call(s32[1]{0:T(128)} %bitcast.core, f32[32,128]{1,0:T(8,128)S(1)} %bitcast.13, f32[256,768]{1,0:T(8,128)S(1)} %get-tuple-element.62.keep, f32[192,768]{1,0:T(8,128)S(1)} %collective-permute-done.7.recv), custom_call_target="tpu_custom_call" | custom-call | bytes 1048576 | tf_op jit(solution)/shard_map/pallas_call | solution.py:479
  (5 shorter events, 0.0 us)
Async XLA Ops:
  3.3 10.7 %collective-permute-start = (bf16[128,2560]{1,0:T(8,128)(2,1)}, bf16[128,2560]{1,0:T(8,128)(2,1)S(1)}, u32[]{:S(2)}, u32[]{:S(2)}) collective-permute-start(bf16[128,2560]{1,0:T(8,128)(2,1)} %get-tuple-element.37), channel_id=1, source_target_pairs={{0,4},{4,0},{1,5},{5,1},{2,6},{6,2},{3,7},{7,3},{8,12},{12,8},{9,1... | collective-permute-start | bytes 1966088 | tf_op jit(solution)/shard_map/ppermute | solution.py:416
  14.0 1.1 %copy-start = (bf16[128,2560]{1,0:T(8,128)(2,1)S(1)}, bf16[128,2560]{1,0:T(8,128)(2,1)}, u32[]{:S(2)}) copy-start(bf16[128,2560]{1,0:T(8,128)(2,1)} %get-tuple-element.36.keep.refs_0_) | copy-start | bytes 1966084
  15.1 10.4 %copy-start.2 = (s32[16384]{0:T(1024)S(1)}, s32[16384]{0:T(1024)}, u32[]{:S(2)}) copy-start(s32[16384]{0:T(1024)} %param.14) | copy-start | bytes 196612
  15.1 10.4 %copy-start.3 = (f32[16384]{0:T(1024)S(1)}, f32[16384]{0:T(1024)}, u32[]{:S(2)}) copy-start(f32[16384]{0:T(1024)} %param.15) | copy-start | bytes 196612
  15.1 10.6 %copy-start.1 = (bf16[128,2560]{1,0:T(8,128)(2,1)S(1)}, bf16[128,2560]{1,0:T(8,128)(2,1)}, u32[]{:S(2)}) copy-start(bf16[128,2560]{1,0:T(8,128)(2,1)} %get-tuple-element.36.keep.refs_0_) | copy-start | bytes 1966084
  15.1 15.9 %collective-permute-start.2 = (bf16[192,1280]{1,0:T(8,128)(2,1)S(1)}, bf16[192,1280]{1,0:T(8,128)(2,1)S(1)}, u32[]{:S(2)}, u32[]{:S(2)}) collective-permute-start(bf16[192,1280]{1,0:T(8,128)(2,1)S(1)} %get-tuple-element.43), channel_id=1, source_target_pairs={{0,504},{4,12},{8,0},{12,20},{16,8},{20,28},{24,16},{28,36},{32,24... | collective-permute-start | bytes 1474568 | tf_op jit(solution)/shard_map/ppermute | solution.py:421
  17.2 18.1 %collective-permute-start.1 = (bf16[192,1280]{1,0:T(8,128)(2,1)S(1)}, bf16[192,1280]{1,0:T(8,128)(2,1)S(1)}, u32[]{:S(2)}, u32[]{:S(2)}) collective-permute-start(bf16[192,1280]{1,0:T(8,128)(2,1)S(1)} %get-tuple-element.38), channel_id=1, source_target_pairs={{0,8},{4,508},{8,16},{12,4},{16,24},{20,12},{24,32},{28,20},{32,40... | collective-permute-start | bytes 1474568 | tf_op jit(solution)/shard_map/ppermute | solution.py:421
  25.8 19.1 %collective-permute-start.3 = (bf16[192,1280]{1,0:T(8,128)(2,1)S(1)}, bf16[192,1280]{1,0:T(8,128)(2,1)S(1)}, u32[]{:S(2)}, u32[]{:S(2)}) collective-permute-start(bf16[192,1280]{1,0:T(8,128)(2,1)S(1)} %get-tuple-element.45), channel_id=1, source_target_pairs={{0,8},{4,508},{8,16},{12,4},{16,24},{20,12},{24,32},{28,20},{32,40... | collective-permute-start | bytes 1474568 | tf_op jit(solution)/shard_map/ppermute | solution.py:421
  29.1 18.5 %collective-permute-start.4 = (bf16[192,1280]{1,0:T(8,128)(2,1)S(1)}, bf16[192,1280]{1,0:T(8,128)(2,1)S(1)}, u32[]{:S(2)}, u32[]{:S(2)}) collective-permute-start(bf16[192,1280]{1,0:T(8,128)(2,1)S(1)} %get-tuple-element.46), channel_id=1, source_target_pairs={{0,504},{4,12},{8,0},{12,20},{16,8},{20,28},{24,16},{28,36},{32,24... | collective-permute-start | bytes 1474568 | tf_op jit(solution)/shard_map/ppermute | solution.py:421
  53.8 16.8 %collective-permute-start.5 = (bf16[192,768]{1,0:T(8,128)(2,1)S(1)}, bf16[192,768]{1,0:T(8,128)(2,1)S(1)}, u32[]{:S(2)}, u32[]{:S(2)}) collective-permute-start(bf16[192,768]{1,0:T(8,128)(2,1)S(1)} %get-tuple-element.59), channel_id=1, source_target_pairs={{0,8},{4,508},{8,16},{12,4},{16,24},{20,12},{24,32},{28,20},{32,40... | collective-permute-start | bytes 884744 | tf_op jit(solution)/shard_map/ppermute | solution.py:421
  58.5 12.2 %collective-permute-start.6 = (bf16[192,768]{1,0:T(8,128)(2,1)S(1)}, bf16[192,768]{1,0:T(8,128)(2,1)S(1)}, u32[]{:S(2)}, u32[]{:S(2)}) collective-permute-start(bf16[192,768]{1,0:T(8,128)(2,1)S(1)} %get-tuple-element.60), channel_id=1, source_target_pairs={{0,508},{4,8},{8,4},{12,16},{16,12},{20,24},{24,20},{28,32},{32,28... | collective-permute-start | bytes 884744 | tf_op jit(solution)/shard_map/ppermute | solution.py:421
  70.8 18.4 %collective-permute-start.7 = (f32[192,768]{1,0:T(8,128)S(1)}, f32[192,768]{1,0:T(8,128)S(1)}, u32[]{:S(2)}, u32[]{:S(2)}) collective-permute-start(f32[192,768]{1,0:T(8,128)S(1)} %get-tuple-element.63), channel_id=1, source_target_pairs={{0,4},{4,0},{1,5},{5,1},{2,6},{6,2},{3,7},{7,3},{8,12},{12,8},{9,1... | collective-permute-start | bytes 1769480 | tf_op jit(solution)/shard_map/ppermute | solution.py:416

commit v8 on v7

--- a/solution.py
+++ b/solution.py
@@ -114,29 +114,34 @@
     weights[...] = queries([row_of(rows, r) for r in range(3, 6)])
 
 
-def edges_kernel(cols, core, keep, recv, *refs):
-    one, two = refs[-2:]
+def edges_kernel(way, core, keep, recv, *refs):
+    outs = refs[-2:] if way > 0 else refs[-1:]
     half = HALO - BLOCK
 
-    def write(first, second, after, before):
-        after[:half, :] = first[BLOCK - half :, cols]
-        after[half:, :] = second[:, cols]
-        before[:BLOCK, :] = first[:, cols]
-        before[BLOCK:, :] = second[:half, cols]
+    def write(first, second, late):
+        width = WIDTH // len(outs)
+        for part, out in enumerate(outs):
+            cols = slice(part * width, (part + 1) * width)
+            if late:
+                out[:half, :] = first[BLOCK - half :, cols]
+                out[half:, :] = second[:, cols]
+            else:
+                out[:BLOCK, :] = first[:, cols]
+                out[BLOCK:, :] = second[:half, cols]
 
     @pl.when(core[0] == 0)
     def _():
-        write(keep, recv, one, two)
+        write(keep, recv, way > 0)
 
     @pl.when(core[0] != 0)
     def _():
-        write(recv, keep, two, one)
-
-
-def call_edges(cols, core, keep, recv, *after):
+        write(recv, keep, way < 0)
+
+
+def call_edges(way, core, keep, recv, *after):
     return call(
-        functools.partial(edges_kernel, cols),
-        [shape(HALO, cols.stop - cols.start, BF16)] * 2,
+        functools.partial(edges_kernel, way),
+        [shape(HALO, PART, BF16)] * 2 if way > 0 else [shape(HALO, WIDTH, BF16)],
         [SMEM] + [VMEM] * (2 + len(after)),
         moved=2 << 20,
     )(core, keep, recv, *after)
@@ -155,7 +160,7 @@
     loss_in,
     *refs,
 ):
-    keep, recv, *halo = refs[:-12]
+    keep, recv, two, *one = refs[:-12]
     grad_left, grad_own, grad_right, loss_out, win, bias, rt, rs, gt, qs, bt, kg = refs[-12:]
     t_at, s_at, s_off = T_AT[rel], S_AT[rel], S_OFF[rel]
     me = core[0]
@@ -169,7 +174,7 @@
             win[at : at + rows, TW:] = s_source[:, s_at : s_at + SP]
             at += rows
 
-    one, two = (halo[-2], halo[0]), (halo[-1], halo[1])
+    one = (one[-1], one[0])
 
     @pl.when(me == 0)
     def _():
@@ -430,9 +435,9 @@
         limit=56,
     )(core, *arrays)
     recv = other_core(send)
-    edges_a = call_edges(slice(0, PART), core, keep, recv)
-    halo_a = [neighbours(edges_a[0], 1), neighbours(edges_a[1], -1)]
-    doc_ids, row_weight, _ = lax.optimization_barrier((doc_ids, row_weight, edges_a[0]))
+    (edges,) = call_edges(-1, core, keep, recv)
+    two = neighbours(edges, -1)
+    doc_ids, row_weight, _ = lax.optimization_barrier((doc_ids, row_weight, edges))
     starts, weight = call(
         mask_kernel,
         [shape(1, OWN, jnp.int32), shape(1, OWN, F32)],
@@ -443,13 +448,11 @@
         doc_ids.reshape(-1, BLOCK),
         row_weight.reshape(-1, BLOCK),
     )
-    edges_b = call_edges(slice(PART, WIDTH), core, keep, recv, weight)
-    halo_b = [neighbours(edges_b[0], 1), neighbours(edges_b[1], -1)]
-
+    one = [neighbours(edge, 1) for edge in call_edges(1, core, keep, recv, weight)]
     loss = jnp.zeros((1, BLOCK), F32)
     grads = []
     for rel in range(3):
-        chunk = (keep, recv, *halo_a, *(halo_b if rel else ()))
+        chunk = (keep, recv, two, *(one if rel else one[:1]))
         *grad, loss = call_relation(rel, core, starts, weight, loss, chunk)
         grads.append(grad)
 

time: 90.7 us -> 92.4 us (1.019)
  blocking collectives: 26.1 us -> 27.2 us
    all_to_all x2, blocking collectives: 26.1 us -> 27.2 us  [exchange(): return lax.all_to_all(value, axes, 0, 0, tiled=True)]
    ppermute x6 -> x5, starting transfers between devices: 22.1 us -> 22.7 us  [neighbours(): return lax.ppermute(value, tok, pairs)]
    ppermute x6 -> x5, waiting for transfers between devices: 13.5 us -> 13.7 us  [neighbours(): return lax.ppermute(value, tok, pairs)]
  transfers between devices with their start and end apart: 8 -> 7, of which waited for: 4 -> 4; matrix products, arithmetic and copies ran while one was open for 0% -> 0% of each run, Pallas kernels for 4% -> 4%
where the time goes in v8:
time: 92.4 us; the launch traced here: 92 us
  starting transfers between devices  34 us (37%)
  blocking collectives  27.2 us (29%)
  waiting for transfers between devices  15.6 us (17%)
  Pallas kernels  13.3 us (14%)
  local copies, waits for them, and re-layouts  1.1 us (1%)
    all_to_all x2, blocking collectives, exchange(): return lax.all_to_all(value, axes, 0, 0, tiled=True)  27.2 us
    ppermute x5, starting transfers between devices, neighbours(): return lax.ppermute(value, tok, pairs)  22.7 us
    ppermute x5, waiting for transfers between devices, neighbours(): return lax.ppermute(value, tok, pairs)  13.7 us
    ppermute x2, starting transfers between devices, other_core(): return lax.ppermute(value, 'core', [(0, 1), (1, 0)])  11.3 us
    pallas_call x3, Pallas kernels, call_relation(): call(functools.partial(relation_kernel, rel), [shape(HALO, SP, BF16), sha...  9.11 us
    pallas_call x1, Pallas kernels, body(): call(split_kernel, [shape(BLOCK, WIDTH, BF16)] * 2, [SMEM] + [HBM] * 6, s...  2.63 us
    ppermute x2, waiting for transfers between devices, other_core(): return lax.ppermute(value, 'core', [(0, 1), (1, 0)])  1.92 us
  transfers between devices with their start and end apart: 7, of which 4 were waited for; matrix products, arithmetic and copies ran while one was open for 0% of the time, Pallas kernels for 4%

profile of v8, /device:TPU:1, one launch (start us, length us, event | category | flops | bytes accessed | tf_op | source)
XLA Modules:
  0.0 92.0 jit_solution(4760851680559232438)
XLA Ops:
  0.6 2.6 %shard_map.111 = (bf16[128,2560]{1,0:T(8,128)(2,1)}, bf16[128,2560]{1,0:T(8,128)(2,1)}) custom-call(s32[1]{0:T(128)} %bitcast.core, bf16[128,1280]{1,0:T(8,128)(2,1)} %refs_0_.1, bf16[128,1280]{1,0:T(8,128)(2,1)} %refs_1_.1, bf16[128,1280]{1,0:T(8,128)(2,1)} %refs_2_.1, bf16[128,384]{1,0:T(8,128)(2,1)} %refs_3_.1, bf16[128,384]{1,0:T(8,128)(2,1)} %refs_4_.1, ...), custom_call_target="tpu_custom_call" | custom-call | bytes 4194304 | tf_op jit(solution)/shard_map/pallas_call | solution.py:429
  3.3 8.8 %collective-permute-start = (bf16[128,2560]{1,0:T(8,128)(2,1)}, bf16[128,2560]{1,0:T(8,128)(2,1)S(1)}, u32[]{:S(2)}, u32[]{:S(2)}) collective-permute-start(bf16[128,2560]{1,0:T(8,128)(2,1)} %get-tuple-element.35), channel_id=1, source_target_pairs={{0,4},{4,0},{1,5},{5,1},{2,6},{6,2},{3,7},{7,3},{8,12},{12,8},{9,1... | collective-permute-start | bytes 1966088 | tf_op jit(solution)/shard_map/ppermute | solution.py:421
  12.1 1.9 %collective-permute-done.recv.refs_1_ = bf16[128,2560]{1,0:T(8,128)(2,1)S(1)} collective-permute-done((bf16[128,2560]{1,0:T(8,128)(2,1)}, bf16[128,2560]{1,0:T(8,128)(2,1)S(1)}, u32[]{:S(2)}, u32[]{:S(2)}) %collective-permute-start) | collective-permute-done | bytes 655392 | tf_op jit(solution)/shard_map/ppermute | solution.py:421
  14.0 1.1 %copy-done = bf16[128,2560]{1,0:T(8,128)(2,1)S(1)} copy-done((bf16[128,2560]{1,0:T(8,128)(2,1)S(1)}, bf16[128,2560]{1,0:T(8,128)(2,1)}, u32[]{:S(2)}) %copy-start) | copy-done | bytes 655384
  15.1 0.0 copy-start.2
  15.1 0.0 copy-start.1
  15.1 0.1 shard_map.112
  15.1 2.1 %collective-permute-start.1 = (bf16[192,2560]{1,0:T(8,128)(2,1)S(1)}, bf16[192,2560]{1,0:T(8,128)(2,1)S(1)}, u32[]{:S(2)}, u32[]{:S(2)}) collective-permute-start(bf16[192,2560]{1,0:T(8,128)(2,1)S(1)} %shard_map.112), channel_id=1, source_target_pairs={{0,504},{4,12},{8,0},{12,20},{16,8},{20,28},{24,16},{28,36},{32,24... | collective-permute-start | bytes 2949128 | tf_op jit(solution)/shard_map/ppermute | solution.py:426
  17.2 0.0 copy-done.2
  17.2 0.0 copy-done.3
  17.2 0.2 shard_map.113
  17.5 0.0 copy-done.1
  17.5 0.1 shard_map.114
  17.5 8.2 %collective-permute-start.2 = (bf16[192,1280]{1,0:T(8,128)(2,1)S(1)}, bf16[192,1280]{1,0:T(8,128)(2,1)S(1)}, u32[]{:S(2)}, u32[]{:S(2)}) collective-permute-start(bf16[192,1280]{1,0:T(8,128)(2,1)S(1)} %get-tuple-element.40), channel_id=1, source_target_pairs={{0,8},{4,508},{8,16},{12,4},{16,24},{20,12},{24,32},{28,20},{32,40... | collective-permute-start | bytes 1474568 | tf_op jit(solution)/shard_map/ppermute | solution.py:426
  25.8 3.4 %collective-permute-start.3 = (bf16[192,1280]{1,0:T(8,128)(2,1)S(1)}, bf16[192,1280]{1,0:T(8,128)(2,1)S(1)}, u32[]{:S(2)}, u32[]{:S(2)}) collective-permute-start(bf16[192,1280]{1,0:T(8,128)(2,1)S(1)} %get-tuple-element.42), channel_id=1, source_target_pairs={{0,8},{4,508},{8,16},{12,4},{16,24},{20,12},{24,32},{28,20},{32,40... | collective-permute-start | bytes 1474568 | tf_op jit(solution)/shard_map/ppermute | solution.py:426
  29.1 7.7 %collective-permute-done.2.refs_3_ = bf16[192,1280]{1,0:T(8,128)(2,1)S(1)} collective-permute-done((bf16[192,1280]{1,0:T(8,128)(2,1)S(1)}, bf16[192,1280]{1,0:T(8,128)(2,1)S(1)}, u32[]{:S(2)}, u32[]{:S(2)}) %collective-permute-start.2) | collective-permute-done | bytes 491552 | tf_op jit(solution)/shard_map/ppermute | solution.py:426
  36.8 0.7 collective-permute-done.1.refs_2_
  37.6 3.0 %shard_map.115 = (bf16[192,256]{1,0:T(8,128)(2,1)S(1)}, f32[256,256]{1,0:T(8,128)S(1)}, bf16[192,256]{1,0:T(8,128)(2,1)S(1)}, f32[1,128]{1,0:T(1,128)S(1)}) custom-call(s32[1]{0:T(128)} %bitcast.core, s32[1,256]{1,0:T(1,128)S(1)} %get-tuple-element.38.starts, f32[1,256]{1,0:T(1,128)S(1)} %get-tuple-element.39.refs_0_.weights, ...), custom_call_target="tpu_custom_call" | custom-call | flops 1342177280 | bytes 2097152 | tf_op jit(solution)/shard_map/pallas_call | solution.py:388
  40.6 5.3 %collective-permute-done.3.refs_4_ = bf16[192,1280]{1,0:T(8,128)(2,1)S(1)} collective-permute-done((bf16[192,1280]{1,0:T(8,128)(2,1)S(1)}, bf16[192,1280]{1,0:T(8,128)(2,1)S(1)}, u32[]{:S(2)}, u32[]{:S(2)}) %collective-permute-start.3) | collective-permute-done | bytes 491552 | tf_op jit(solution)/shard_map/ppermute | solution.py:426
  45.9 3.0 %shard_map.116 = (bf16[192,256]{1,0:T(8,128)(2,1)S(1)}, f32[256,256]{1,0:T(8,128)S(1)}, bf16[192,256]{1,0:T(8,128)(2,1)S(1)}, f32[1,128]{1,0:T(1,128)S(1)}) custom-call(s32[1]{0:T(128)} %bitcast.core, s32[1,256]{1,0:T(1,128)S(1)} %get-tuple-element.38.starts, f32[1,256]{1,0:T(1,128)S(1)} %get-tuple-element.39.refs_0_.weights, ...), custom_call_target="tpu_custom_call" | custom-call | flops 1342177280 | bytes 2097152 | tf_op jit(solution)/shard_map/pallas_call | solution.py:388
  48.9 3.0 %shard_map.117 = (bf16[192,256]{1,0:T(8,128)(2,1)S(1)}, f32[256,256]{1,0:T(8,128)S(1)}, bf16[192,256]{1,0:T(8,128)(2,1)S(1)}, f32[1,128]{1,0:T(1,128)S(1)}) custom-call(s32[1]{0:T(128)} %bitcast.core, s32[1,256]{1,0:T(1,128)S(1)} %get-tuple-element.38.starts, f32[1,256]{1,0:T(1,128)S(1)} %get-tuple-element.39.refs_0_.weights, ...), custom_call_target="tpu_custom_call" | custom-call | flops 1342177280 | bytes 2097152 | tf_op jit(solution)/shard_map/pallas_call | solution.py:388
  52.0 0.1 shard_map.118
  52.0 7.1 %collective-permute-start.4 = (bf16[192,768]{1,0:T(8,128)(2,1)S(1)}, bf16[192,768]{1,0:T(8,128)(2,1)S(1)}, u32[]{:S(2)}, u32[]{:S(2)}) collective-permute-start(bf16[192,768]{1,0:T(8,128)(2,1)S(1)} %get-tuple-element.55), channel_id=1, source_target_pairs={{0,8},{4,508},{8,16},{12,4},{16,24},{20,12},{24,32},{28,20},{32,40... | collective-permute-start | bytes 884744 | tf_op jit(solution)/shard_map/ppermute | solution.py:426
  59.2 1.9 %collective-permute-start.5 = (bf16[192,768]{1,0:T(8,128)(2,1)S(1)}, bf16[192,768]{1,0:T(8,128)(2,1)S(1)}, u32[]{:S(2)}, u32[]{:S(2)}) collective-permute-start(bf16[192,768]{1,0:T(8,128)(2,1)S(1)} %get-tuple-element.56), channel_id=1, source_target_pairs={{0,508},{4,8},{8,4},{12,16},{16,12},{20,24},{24,20},{28,32},{32,28... | collective-permute-start | bytes 884744 | tf_op jit(solution)/shard_map/ppermute | solution.py:426
  61.1 10.2 %all_to_all.22 = f32[16,1,128]{2,1,0:T(1,128)S(1)} all-to-all(f32[16,1,128]{2,1,0:T(1,128)S(1)} %bitcast.18), channel_id=1, replica_groups=mesh['y'=8,'z'=4,'parity'=2,'core'=2,'head'=4] {'z','parity','core'}, dimensions={0} | all-to-all | bytes 16384 | tf_op jit(solution)/shard_map/all_to_all | solution.py:463
  71.3 0.0 collective-permute-done.4.mine
  71.3 0.0 collective-permute-done.5.other
  71.3 0.1 shard_map.119
  71.5 2.6 %collective-permute-start.6 = (f32[192,768]{1,0:T(8,128)S(1)}, f32[192,768]{1,0:T(8,128)S(1)}, u32[]{:S(2)}, u32[]{:S(2)}) collective-permute-start(f32[192,768]{1,0:T(8,128)S(1)} %get-tuple-element.59), channel_id=1, source_target_pairs={{0,4},{4,0},{1,5},{5,1},{2,6},{6,2},{3,7},{7,3},{8,12},{12,8},{9,1... | collective-permute-start | bytes 1769480 | tf_op jit(solution)/shard_map/ppermute | solution.py:421
  74.0 17.0 %all_to_all.23 = f32[32,1,128]{2,1,0:T(1,128)S(1)} all-to-all(f32[32,1,128]{2,1,0:T(1,128)S(1)} %bitcast.17), channel_id=1, replica_groups=mesh['y'=8,'z'=4,'parity'=2,'core'=2,'head'=4] {'y','head'}, dimensions={0} | all-to-all | bytes 32768 | tf_op jit(solution)/shard_map/all_to_all | solution.py:463
  91.0 0.0 collective-permute-done.6.recv
  91.0 1.0 %shard_map.120 = (f32[128,384]{1,0:T(8,128)}, f32[128,384]{1,0:T(8,128)}, f32[128,384]{1,0:T(8,128)}, f32[1,1]{1,0:T(1,128)}) custom-call(s32[1]{0:T(128)} %bitcast.core, f32[32,128]{1,0:T(8,128)S(1)} %bitcast.13, f32[256,768]{1,0:T(8,128)S(1)} %get-tuple-element.58.keep, f32[192,768]{1,0:T(8,128)S(1)} %collective-permute-done.6.recv), custom_call_target="tpu_custom_call" | custom-call | bytes 1048576 | tf_op jit(solution)/shard_map/pallas_call | solution.py:482
  (3 shorter events, 0.0 us)
Async XLA Ops:
  3.3 10.7 %collective-permute-start = (bf16[128,2560]{1,0:T(8,128)(2,1)}, bf16[128,2560]{1,0:T(8,128)(2,1)S(1)}, u32[]{:S(2)}, u32[]{:S(2)}) collective-permute-start(bf16[128,2560]{1,0:T(8,128)(2,1)} %get-tuple-element.35), channel_id=1, source_target_pairs={{0,4},{4,0},{1,5},{5,1},{2,6},{6,2},{3,7},{7,3},{8,12},{12,8},{9,1... | collective-permute-start | bytes 1966088 | tf_op jit(solution)/shard_map/ppermute | solution.py:421
  14.0 1.1 %copy-start = (bf16[128,2560]{1,0:T(8,128)(2,1)S(1)}, bf16[128,2560]{1,0:T(8,128)(2,1)}, u32[]{:S(2)}) copy-start(bf16[128,2560]{1,0:T(8,128)(2,1)} %get-tuple-element.34.keep.refs_0_) | copy-start | bytes 1966084
  15.1 2.1 %copy-start.2 = (s32[16384]{0:T(1024)S(1)}, s32[16384]{0:T(1024)}, u32[]{:S(2)}) copy-start(s32[16384]{0:T(1024)} %param.14) | copy-start | bytes 196612
  15.1 2.2 %copy-start.3 = (f32[16384]{0:T(1024)S(1)}, f32[16384]{0:T(1024)}, u32[]{:S(2)}) copy-start(f32[16384]{0:T(1024)} %param.15) | copy-start | bytes 196612
  15.1 2.4 %copy-start.1 = (bf16[128,2560]{1,0:T(8,128)(2,1)S(1)}, bf16[128,2560]{1,0:T(8,128)(2,1)}, u32[]{:S(2)}) copy-start(bf16[128,2560]{1,0:T(8,128)(2,1)} %get-tuple-element.34.keep.refs_0_) | copy-start | bytes 1966084
  15.1 22.4 %collective-permute-start.1 = (bf16[192,2560]{1,0:T(8,128)(2,1)S(1)}, bf16[192,2560]{1,0:T(8,128)(2,1)S(1)}, u32[]{:S(2)}, u32[]{:S(2)}) collective-permute-start(bf16[192,2560]{1,0:T(8,128)(2,1)S(1)} %shard_map.112), channel_id=1, source_target_pairs={{0,504},{4,12},{8,0},{12,20},{16,8},{20,28},{24,16},{28,36},{32,24... | collective-permute-start | bytes 2949128 | tf_op jit(solution)/shard_map/ppermute | solution.py:426
  17.5 19.3 %collective-permute-start.2 = (bf16[192,1280]{1,0:T(8,128)(2,1)S(1)}, bf16[192,1280]{1,0:T(8,128)(2,1)S(1)}, u32[]{:S(2)}, u32[]{:S(2)}) collective-permute-start(bf16[192,1280]{1,0:T(8,128)(2,1)S(1)} %get-tuple-element.40), channel_id=1, source_target_pairs={{0,8},{4,508},{8,16},{12,4},{16,24},{20,12},{24,32},{28,20},{32,40... | collective-permute-start | bytes 1474568 | tf_op jit(solution)/shard_map/ppermute | solution.py:426
  25.8 20.1 %collective-permute-start.3 = (bf16[192,1280]{1,0:T(8,128)(2,1)S(1)}, bf16[192,1280]{1,0:T(8,128)(2,1)S(1)}, u32[]{:S(2)}, u32[]{:S(2)}) collective-permute-start(bf16[192,1280]{1,0:T(8,128)(2,1)S(1)} %get-tuple-element.42), channel_id=1, source_target_pairs={{0,8},{4,508},{8,16},{12,4},{16,24},{20,12},{24,32},{28,20},{32,40... | collective-permute-start | bytes 1474568 | tf_op jit(solution)/shard_map/ppermute | solution.py:426
  52.0 19.3 %collective-permute-start.4 = (bf16[192,768]{1,0:T(8,128)(2,1)S(1)}, bf16[192,768]{1,0:T(8,128)(2,1)S(1)}, u32[]{:S(2)}, u32[]{:S(2)}) collective-permute-start(bf16[192,768]{1,0:T(8,128)(2,1)S(1)} %get-tuple-element.55), channel_id=1, source_target_pairs={{0,8},{4,508},{8,16},{12,4},{16,24},{20,12},{24,32},{28,20},{32,40... | collective-permute-start | bytes 884744 | tf_op jit(solution)/shard_map/ppermute | solution.py:426
  59.2 12.2 %collective-permute-start.5 = (bf16[192,768]{1,0:T(8,128)(2,1)S(1)}, bf16[192,768]{1,0:T(8,128)(2,1)S(1)}, u32[]{:S(2)}, u32[]{:S(2)}) collective-permute-start(bf16[192,768]{1,0:T(8,128)(2,1)S(1)} %get-tuple-element.56), channel_id=1, source_target_pairs={{0,508},{4,8},{8,4},{12,16},{16,12},{20,24},{24,20},{28,32},{32,28... | collective-permute-start | bytes 884744 | tf_op jit(solution)/shard_map/ppermute | solution.py:426
  71.5 19.6 %collective-permute-start.6 = (f32[192,768]{1,0:T(8,128)S(1)}, f32[192,768]{1,0:T(8,128)S(1)}, u32[]{:S(2)}, u32[]{:S(2)}) collective-permute-start(f32[192,768]{1,0:T(8,128)S(1)} %get-tuple-element.59), channel_id=1, source_target_pairs={{0,4},{4,0},{1,5},{5,1},{2,6},{6,2},{3,7},{7,3},{8,12},{12,8},{9,1... | collective-permute-start | bytes 1769480 | tf_op jit(solution)/shard_map/ppermute | solution.py:421

commit v9 on v8

--- a/solution.py
+++ b/solution.py
@@ -115,13 +115,12 @@
 
 
 def edges_kernel(way, core, keep, recv, *refs):
-    outs = refs[-2:] if way > 0 else refs[-1:]
+    outs = refs[-2:]
     half = HALO - BLOCK
 
     def write(first, second, late):
-        width = WIDTH // len(outs)
         for part, out in enumerate(outs):
-            cols = slice(part * width, (part + 1) * width)
+            cols = slice(part * PART, (part + 1) * PART)
             if late:
                 out[:half, :] = first[BLOCK - half :, cols]
                 out[half:, :] = second[:, cols]
@@ -141,7 +140,7 @@
 def call_edges(way, core, keep, recv, *after):
     return call(
         functools.partial(edges_kernel, way),
-        [shape(HALO, PART, BF16)] * 2 if way > 0 else [shape(HALO, WIDTH, BF16)],
+        [shape(HALO, PART, BF16)] * 2,
         [SMEM] + [VMEM] * (2 + len(after)),
         moved=2 << 20,
     )(core, keep, recv, *after)
@@ -160,7 +159,7 @@
     loss_in,
     *refs,
 ):
-    keep, recv, two, *one = refs[:-12]
+    keep, recv, *halo = refs[:-12]
     grad_left, grad_own, grad_right, loss_out, win, bias, rt, rs, gt, qs, bt, kg = refs[-12:]
     t_at, s_at, s_off = T_AT[rel], S_AT[rel], S_OFF[rel]
     me = core[0]
@@ -174,7 +173,7 @@
             win[at : at + rows, TW:] = s_source[:, s_at : s_at + SP]
             at += rows
 
-    one = (one[-1], one[0])
+    two, one = (halo[1 if rel else 0], halo[0]), (halo[-1], halo[2])
 
     @pl.when(me == 0)
     def _():
@@ -435,9 +434,9 @@
         limit=56,
     )(core, *arrays)
     recv = other_core(send)
-    (edges,) = call_edges(-1, core, keep, recv)
-    two = neighbours(edges, -1)
-    doc_ids, row_weight, _ = lax.optimization_barrier((doc_ids, row_weight, edges))
+    edges = call_edges(-1, core, keep, recv)
+    two = [neighbours(edge, -1) for edge in edges]
+    doc_ids, row_weight, _ = lax.optimization_barrier((doc_ids, row_weight, edges[0]))
     starts, weight = call(
         mask_kernel,
         [shape(1, OWN, jnp.int32), shape(1, OWN, F32)],
@@ -452,7 +451,7 @@
     loss = jnp.zeros((1, BLOCK), F32)
     grads = []
     for rel in range(3):
-        chunk = (keep, recv, two, *(one if rel else one[:1]))
+        chunk = (keep, recv, *two, *(one if rel else one[:1]))
         *grad, loss = call_relation(rel, core, starts, weight, loss, chunk)
         grads.append(grad)
 

time: 92.4 us -> 90.6 us (0.981)
  waiting for transfers between devices: 15.6 us -> 13.7 us
  blocking collectives: 27.2 us -> 25.3 us
  starting transfers between devices: 34 us -> 35.9 us
    ppermute x5 -> x6, starting transfers between devices: 22.7 us -> 24.6 us  [neighbours(): return lax.ppermute(value, tok, pairs)]
    ppermute x5 -> x6, waiting for transfers between devices: 13.7 us -> 11.8 us  [neighbours(): return lax.ppermute(value, tok, pairs)]
    all_to_all x2, blocking collectives: 27.2 us -> 25.3 us  [exchange(): return lax.all_to_all(value, axes, 0, 0, tiled=True)]
  transfers between devices with their start and end apart: 7 -> 8, of which waited for: 4 -> 4; matrix products, arithmetic and copies ran while one was open for 0% -> 0% of each run, Pallas kernels for 4% -> 4%
where the time goes in v9:
time: 90.6 us; the launch traced here: 90.1 us
  starting transfers between devices  35.9 us (40%)
  blocking collectives  25.3 us (28%)
  waiting for transfers between devices  13.7 us (15%)
  Pallas kernels  13.3 us (15%)
  local copies, waits for them, and re-layouts  1.1 us (1%)
    all_to_all x2, blocking collectives, exchange(): return lax.all_to_all(value, axes, 0, 0, tiled=True)  25.3 us
    ppermute x6, starting transfers between devices, neighbours(): return lax.ppermute(value, tok, pairs)  24.6 us
    ppermute x6, waiting for transfers between devices, neighbours(): return lax.ppermute(value, tok, pairs)  11.8 us
    ppermute x2, starting transfers between devices, other_core(): return lax.ppermute(value, 'core', [(0, 1), (1, 0)])  11.3 us
    pallas_call x3, Pallas kernels, call_relation(): call(functools.partial(relation_kernel, rel), [shape(HALO, SP, BF16), sha...  9.1 us
    pallas_call x1, Pallas kernels, body(): call(split_kernel, [shape(BLOCK, WIDTH, BF16)] * 2, [SMEM] + [HBM] * 6, s...  2.63 us
    ppermute x2, waiting for transfers between devices, other_core(): return lax.ppermute(value, 'core', [(0, 1), (1, 0)])  1.91 us
  transfers between devices with their start and end apart: 8, of which 4 were waited for; matrix products, arithmetic and copies ran while one was open for 0% of the time, Pallas kernels for 4%

profile of v9, /device:TPU:1, one launch (start us, length us, event | category | flops | bytes accessed | tf_op | source)
XLA Modules:
  0.0 90.1 jit_solution(2971070567011456116)
XLA Ops:
  0.6 2.6 %shard_map.111 = (bf16[128,2560]{1,0:T(8,128)(2,1)}, bf16[128,2560]{1,0:T(8,128)(2,1)}) custom-call(s32[1]{0:T(128)} %bitcast.core, bf16[128,1280]{1,0:T(8,128)(2,1)} %refs_0_.1, bf16[128,1280]{1,0:T(8,128)(2,1)} %refs_1_.1, bf16[128,1280]{1,0:T(8,128)(2,1)} %refs_2_.1, bf16[128,384]{1,0:T(8,128)(2,1)} %refs_3_.1, bf16[128,384]{1,0:T(8,128)(2,1)} %refs_4_.1, ...), custom_call_target="tpu_custom_call" | custom-call | bytes 4194304 | tf_op jit(solution)/shard_map/pallas_call | solution.py:428
  3.3 8.8 %collective-permute-start = (bf16[128,2560]{1,0:T(8,128)(2,1)}, bf16[128,2560]{1,0:T(8,128)(2,1)S(1)}, u32[]{:S(2)}, u32[]{:S(2)}) collective-permute-start(bf16[128,2560]{1,0:T(8,128)(2,1)} %get-tuple-element.37), channel_id=1, source_target_pairs={{0,4},{4,0},{1,5},{5,1},{2,6},{6,2},{3,7},{7,3},{8,12},{12,8},{9,1... | collective-permute-start | bytes 1966088 | tf_op jit(solution)/shard_map/ppermute | solution.py:420
  12.1 1.9 %collective-permute-done.recv.refs_1_ = bf16[128,2560]{1,0:T(8,128)(2,1)S(1)} collective-permute-done((bf16[128,2560]{1,0:T(8,128)(2,1)}, bf16[128,2560]{1,0:T(8,128)(2,1)S(1)}, u32[]{:S(2)}, u32[]{:S(2)}) %collective-permute-start) | collective-permute-done | bytes 655392 | tf_op jit(solution)/shard_map/ppermute | solution.py:420
  14.0 1.1 %copy-done = bf16[128,2560]{1,0:T(8,128)(2,1)S(1)} copy-done((bf16[128,2560]{1,0:T(8,128)(2,1)S(1)}, bf16[128,2560]{1,0:T(8,128)(2,1)}, u32[]{:S(2)}) %copy-start) | copy-done | bytes 655384
  15.1 0.1 shard_map.112
  15.1 2.1 %collective-permute-start.1 = (bf16[192,1280]{1,0:T(8,128)(2,1)S(1)}, bf16[192,1280]{1,0:T(8,128)(2,1)S(1)}, u32[]{:S(2)}, u32[]{:S(2)}) collective-permute-start(bf16[192,1280]{1,0:T(8,128)(2,1)S(1)} %get-tuple-element.38), channel_id=1, source_target_pairs={{0,504},{4,12},{8,0},{12,20},{16,8},{20,28},{24,16},{28,36},{32,24... | collective-permute-start | bytes 1474568 | tf_op jit(solution)/shard_map/ppermute | solution.py:425
  17.2 1.9 %collective-permute-start.2 = (bf16[192,1280]{1,0:T(8,128)(2,1)S(1)}, bf16[192,1280]{1,0:T(8,128)(2,1)S(1)}, u32[]{:S(2)}, u32[]{:S(2)}) collective-permute-start(bf16[192,1280]{1,0:T(8,128)(2,1)S(1)} %get-tuple-element.43), channel_id=1, source_target_pairs={{0,504},{4,12},{8,0},{12,20},{16,8},{20,28},{24,16},{28,36},{32,24... | collective-permute-start | bytes 1474568 | tf_op jit(solution)/shard_map/ppermute | solution.py:425
  19.1 0.0 copy-done.2
  19.1 0.0 copy-done.3
  19.2 0.2 shard_map.113
  19.4 0.0 copy-done.1
  19.4 0.1 shard_map.114
  19.5 8.2 %collective-permute-start.3 = (bf16[192,1280]{1,0:T(8,128)(2,1)S(1)}, bf16[192,1280]{1,0:T(8,128)(2,1)S(1)}, u32[]{:S(2)}, u32[]{:S(2)}) collective-permute-start(bf16[192,1280]{1,0:T(8,128)(2,1)S(1)} %get-tuple-element.44), channel_id=1, source_target_pairs={{0,8},{4,508},{8,16},{12,4},{16,24},{20,12},{24,32},{28,20},{32,40... | collective-permute-start | bytes 1474568 | tf_op jit(solution)/shard_map/ppermute | solution.py:425
  27.7 3.4 %collective-permute-start.4 = (bf16[192,1280]{1,0:T(8,128)(2,1)S(1)}, bf16[192,1280]{1,0:T(8,128)(2,1)S(1)}, u32[]{:S(2)}, u32[]{:S(2)}) collective-permute-start(bf16[192,1280]{1,0:T(8,128)(2,1)S(1)} %get-tuple-element.46), channel_id=1, source_target_pairs={{0,8},{4,508},{8,16},{12,4},{16,24},{20,12},{24,32},{28,20},{32,40... | collective-permute-start | bytes 1474568 | tf_op jit(solution)/shard_map/ppermute | solution.py:425
  31.1 3.9 %collective-permute-done.2.refs_3_ = bf16[192,1280]{1,0:T(8,128)(2,1)S(1)} collective-permute-done((bf16[192,1280]{1,0:T(8,128)(2,1)S(1)}, bf16[192,1280]{1,0:T(8,128)(2,1)S(1)}, u32[]{:S(2)}, u32[]{:S(2)}) %collective-permute-start.2) | collective-permute-done | bytes 491552 | tf_op jit(solution)/shard_map/ppermute | solution.py:425
  35.0 0.0 collective-permute-done.1.refs_2_
  35.0 3.8 %collective-permute-done.3.refs_4_ = bf16[192,1280]{1,0:T(8,128)(2,1)S(1)} collective-permute-done((bf16[192,1280]{1,0:T(8,128)(2,1)S(1)}, bf16[192,1280]{1,0:T(8,128)(2,1)S(1)}, u32[]{:S(2)}, u32[]{:S(2)}) %collective-permute-start.3) | collective-permute-done | bytes 491552 | tf_op jit(solution)/shard_map/ppermute | solution.py:425
  38.8 3.0 %shard_map.115 = (bf16[192,256]{1,0:T(8,128)(2,1)S(1)}, f32[256,256]{1,0:T(8,128)S(1)}, bf16[192,256]{1,0:T(8,128)(2,1)S(1)}, f32[1,128]{1,0:T(1,128)S(1)}) custom-call(s32[1]{0:T(128)} %bitcast.core, s32[1,256]{1,0:T(1,128)S(1)} %get-tuple-element.41.starts, f32[1,256]{1,0:T(1,128)S(1)} %get-tuple-element.42.refs_0_.weights, ...), custom_call_target="tpu_custom_call" | custom-call | flops 1342177280 | bytes 2097152 | tf_op jit(solution)/shard_map/pallas_call | solution.py:387
  41.8 4.1 %collective-permute-done.4.refs_5_ = bf16[192,1280]{1,0:T(8,128)(2,1)S(1)} collective-permute-done((bf16[192,1280]{1,0:T(8,128)(2,1)S(1)}, bf16[192,1280]{1,0:T(8,128)(2,1)S(1)}, u32[]{:S(2)}, u32[]{:S(2)}) %collective-permute-start.4) | collective-permute-done | bytes 491552 | tf_op jit(solution)/shard_map/ppermute | solution.py:425
  45.9 3.0 %shard_map.116 = (bf16[192,256]{1,0:T(8,128)(2,1)S(1)}, f32[256,256]{1,0:T(8,128)S(1)}, bf16[192,256]{1,0:T(8,128)(2,1)S(1)}, f32[1,128]{1,0:T(1,128)S(1)}) custom-call(s32[1]{0:T(128)} %bitcast.core, s32[1,256]{1,0:T(1,128)S(1)} %get-tuple-element.41.starts, f32[1,256]{1,0:T(1,128)S(1)} %get-tuple-element.42.refs_0_.weights, ...), custom_call_target="tpu_custom_call" | custom-call | flops 1342177280 | bytes 2097152 | tf_op jit(solution)/shard_map/pallas_call | solution.py:387
  48.9 3.0 %shard_map.117 = (bf16[192,256]{1,0:T(8,128)(2,1)S(1)}, f32[256,256]{1,0:T(8,128)S(1)}, bf16[192,256]{1,0:T(8,128)(2,1)S(1)}, f32[1,128]{1,0:T(1,128)S(1)}) custom-call(s32[1]{0:T(128)} %bitcast.core, s32[1,256]{1,0:T(1,128)S(1)} %get-tuple-element.41.starts, f32[1,256]{1,0:T(1,128)S(1)} %get-tuple-element.42.refs_0_.weights, ...), custom_call_target="tpu_custom_call" | custom-call | flops 1342177280 | bytes 2097152 | tf_op jit(solution)/shard_map/pallas_call | solution.py:387
  52.0 0.1 shard_map.118
  52.0 7.1 %collective-permute-start.5 = (bf16[192,768]{1,0:T(8,128)(2,1)S(1)}, bf16[192,768]{1,0:T(8,128)(2,1)S(1)}, u32[]{:S(2)}, u32[]{:S(2)}) collective-permute-start(bf16[192,768]{1,0:T(8,128)(2,1)S(1)} %get-tuple-element.59), channel_id=1, source_target_pairs={{0,8},{4,508},{8,16},{12,4},{16,24},{20,12},{24,32},{28,20},{32,40... | collective-permute-start | bytes 884744 | tf_op jit(solution)/shard_map/ppermute | solution.py:425
  59.2 1.9 %collective-permute-start.6 = (bf16[192,768]{1,0:T(8,128)(2,1)S(1)}, bf16[192,768]{1,0:T(8,128)(2,1)S(1)}, u32[]{:S(2)}, u32[]{:S(2)}) collective-permute-start(bf16[192,768]{1,0:T(8,128)(2,1)S(1)} %get-tuple-element.60), channel_id=1, source_target_pairs={{0,508},{4,8},{8,4},{12,16},{16,12},{20,24},{24,20},{28,32},{32,28... | collective-permute-start | bytes 884744 | tf_op jit(solution)/shard_map/ppermute | solution.py:425
  61.1 10.2 %all_to_all.22 = f32[16,1,128]{2,1,0:T(1,128)S(1)} all-to-all(f32[16,1,128]{2,1,0:T(1,128)S(1)} %bitcast.18), channel_id=1, replica_groups=mesh['y'=8,'z'=4,'parity'=2,'core'=2,'head'=4] {'z','parity','core'}, dimensions={0} | all-to-all | bytes 16384 | tf_op jit(solution)/shard_map/all_to_all | solution.py:462
  71.3 0.0 collective-permute-done.5.mine
  71.3 0.0 collective-permute-done.6.other
  71.3 0.1 shard_map.119
  71.5 2.6 %collective-permute-start.7 = (f32[192,768]{1,0:T(8,128)S(1)}, f32[192,768]{1,0:T(8,128)S(1)}, u32[]{:S(2)}, u32[]{:S(2)}) collective-permute-start(f32[192,768]{1,0:T(8,128)S(1)} %get-tuple-element.63), channel_id=1, source_target_pairs={{0,4},{4,0},{1,5},{5,1},{2,6},{6,2},{3,7},{7,3},{8,12},{12,8},{9,1... | collective-permute-start | bytes 1769480 | tf_op jit(solution)/shard_map/ppermute | solution.py:420
  74.0 15.1 %all_to_all.23 = f32[32,1,128]{2,1,0:T(1,128)S(1)} all-to-all(f32[32,1,128]{2,1,0:T(1,128)S(1)} %bitcast.17), channel_id=1, replica_groups=mesh['y'=8,'z'=4,'parity'=2,'core'=2,'head'=4] {'y','head'}, dimensions={0} | all-to-all | bytes 32768 | tf_op jit(solution)/shard_map/all_to_all | solution.py:462
  89.1 0.0 collective-permute-done.7.recv
  89.1 1.0 %shard_map.120 = (f32[128,384]{1,0:T(8,128)}, f32[128,384]{1,0:T(8,128)}, f32[128,384]{1,0:T(8,128)}, f32[1,1]{1,0:T(1,128)}) custom-call(s32[1]{0:T(128)} %bitcast.core, f32[32,128]{1,0:T(8,128)S(1)} %bitcast.13, f32[256,768]{1,0:T(8,128)S(1)} %get-tuple-element.62.keep, f32[192,768]{1,0:T(8,128)S(1)} %collective-permute-done.7.recv), custom_call_target="tpu_custom_call" | custom-call | bytes 1048576 | tf_op jit(solution)/shard_map/pallas_call | solution.py:481
  (5 shorter events, 0.0 us)
Async XLA Ops:
  3.3 10.7 %collective-permute-start = (bf16[128,2560]{1,0:T(8,128)(2,1)}, bf16[128,2560]{1,0:T(8,128)(2,1)S(1)}, u32[]{:S(2)}, u32[]{:S(2)}) collective-permute-start(bf16[128,2560]{1,0:T(8,128)(2,1)} %get-tuple-element.37), channel_id=1, source_target_pairs={{0,4},{4,0},{1,5},{5,1},{2,6},{6,2},{3,7},{7,3},{8,12},{12,8},{9,1... | collective-permute-start | bytes 1966088 | tf_op jit(solution)/shard_map/ppermute | solution.py:420
  14.0 1.1 %copy-start = (bf16[128,2560]{1,0:T(8,128)(2,1)S(1)}, bf16[128,2560]{1,0:T(8,128)(2,1)}, u32[]{:S(2)}) copy-start(bf16[128,2560]{1,0:T(8,128)(2,1)} %get-tuple-element.36.keep.refs_0_) | copy-start | bytes 1966084
  15.1 4.1 %copy-start.2 = (s32[16384]{0:T(1024)S(1)}, s32[16384]{0:T(1024)}, u32[]{:S(2)}) copy-start(s32[16384]{0:T(1024)} %param.14) | copy-start | bytes 196612
  15.1 4.1 %copy-start.3 = (f32[16384]{0:T(1024)S(1)}, f32[16384]{0:T(1024)}, u32[]{:S(2)}) copy-start(f32[16384]{0:T(1024)} %param.15) | copy-start | bytes 196612
  15.1 4.3 %copy-start.1 = (bf16[128,2560]{1,0:T(8,128)(2,1)S(1)}, bf16[128,2560]{1,0:T(8,128)(2,1)}, u32[]{:S(2)}) copy-start(bf16[128,2560]{1,0:T(8,128)(2,1)} %get-tuple-element.36.keep.refs_0_) | copy-start | bytes 1966084
  15.1 19.8 %collective-permute-start.1 = (bf16[192,1280]{1,0:T(8,128)(2,1)S(1)}, bf16[192,1280]{1,0:T(8,128)(2,1)S(1)}, u32[]{:S(2)}, u32[]{:S(2)}) collective-permute-start(bf16[192,1280]{1,0:T(8,128)(2,1)S(1)} %get-tuple-element.38), channel_id=1, source_target_pairs={{0,504},{4,12},{8,0},{12,20},{16,8},{20,28},{24,16},{28,36},{32,24... | collective-permute-start | bytes 1474568 | tf_op jit(solution)/shard_map/ppermute | solution.py:425
  17.2 17.8 %collective-permute-start.2 = (bf16[192,1280]{1,0:T(8,128)(2,1)S(1)}, bf16[192,1280]{1,0:T(8,128)(2,1)S(1)}, u32[]{:S(2)}, u32[]{:S(2)}) collective-permute-start(bf16[192,1280]{1,0:T(8,128)(2,1)S(1)} %get-tuple-element.43), channel_id=1, source_target_pairs={{0,504},{4,12},{8,0},{12,20},{16,8},{20,28},{24,16},{28,36},{32,24... | collective-permute-start | bytes 1474568 | tf_op jit(solution)/shard_map/ppermute | solution.py:425
  19.5 19.3 %collective-permute-start.3 = (bf16[192,1280]{1,0:T(8,128)(2,1)S(1)}, bf16[192,1280]{1,0:T(8,128)(2,1)S(1)}, u32[]{:S(2)}, u32[]{:S(2)}) collective-permute-start(bf16[192,1280]{1,0:T(8,128)(2,1)S(1)} %get-tuple-element.44), channel_id=1, source_target_pairs={{0,8},{4,508},{8,16},{12,4},{16,24},{20,12},{24,32},{28,20},{32,40... | collective-permute-start | bytes 1474568 | tf_op jit(solution)/shard_map/ppermute | solution.py:425
  27.7 18.2 %collective-permute-start.4 = (bf16[192,1280]{1,0:T(8,128)(2,1)S(1)}, bf16[192,1280]{1,0:T(8,128)(2,1)S(1)}, u32[]{:S(2)}, u32[]{:S(2)}) collective-permute-start(bf16[192,1280]{1,0:T(8,128)(2,1)S(1)} %get-tuple-element.46), channel_id=1, source_target_pairs={{0,8},{4,508},{8,16},{12,4},{16,24},{20,12},{24,32},{28,20},{32,40... | collective-permute-start | bytes 1474568 | tf_op jit(solution)/shard_map/ppermute | solution.py:425
  52.0 19.3 %collective-permute-start.5 = (bf16[192,768]{1,0:T(8,128)(2,1)S(1)}, bf16[192,768]{1,0:T(8,128)(2,1)S(1)}, u32[]{:S(2)}, u32[]{:S(2)}) collective-permute-start(bf16[192,768]{1,0:T(8,128)(2,1)S(1)} %get-tuple-element.59), channel_id=1, source_target_pairs={{0,8},{4,508},{8,16},{12,4},{16,24},{20,12},{24,32},{28,20},{32,40... | collective-permute-start | bytes 884744 | tf_op jit(solution)/shard_map/ppermute | solution.py:425
  59.2 12.2 %collective-permute-start.6 = (bf16[192,768]{1,0:T(8,128)(2,1)S(1)}, bf16[192,768]{1,0:T(8,128)(2,1)S(1)}, u32[]{:S(2)}, u32[]{:S(2)}) collective-permute-start(bf16[192,768]{1,0:T(8,128)(2,1)S(1)} %get-tuple-element.60), channel_id=1, source_target_pairs={{0,508},{4,8},{8,4},{12,16},{16,12},{20,24},{24,20},{28,32},{32,28... | collective-permute-start | bytes 884744 | tf_op jit(solution)/shard_map/ppermute | solution.py:425
  71.5 17.7 %collective-permute-start.7 = (f32[192,768]{1,0:T(8,128)S(1)}, f32[192,768]{1,0:T(8,128)S(1)}, u32[]{:S(2)}, u32[]{:S(2)}) collective-permute-start(f32[192,768]{1,0:T(8,128)S(1)} %get-tuple-element.63), channel_id=1, source_target_pairs={{0,4},{4,0},{1,5},{5,1},{2,6},{6,2},{3,7},{7,3},{8,12},{12,8},{9,1... | collective-permute-start | bytes 1769480 | tf_op jit(solution)/shard_map/ppermute | solution.py:420

commit v10 on v9

--- a/solution.py
+++ b/solution.py
@@ -52,9 +52,9 @@
     )
 
 
-def split_kernel(core, *refs):
-    arrays, (send, keep), buffers, sems = refs[:6], refs[6:8], refs[8:14], refs[14]
-    me = core[0]
+def split_kernel(own, core, *refs):
+    arrays, out, buffers, sems = refs[:6], refs[-8], refs[-7:-1], refs[-1]
+    which = core[0] if own else 1 - core[0]
     copies = [
         pltpu.make_async_copy(array, buffer, sems.at[i])
         for i, (array, buffer) in enumerate(zip(arrays, buffers))
@@ -64,26 +64,22 @@
     for copy in copies:
         copy.wait()
     lane = lax.broadcasted_iota(jnp.int32, (BLOCK, SP), 1)
-    mine = pl.ds(pl.multiple_of(me * TW, 128), TW)
-    other = pl.ds(pl.multiple_of((1 - me) * TW, 128), TW)
-    ours, theirs = [], []
+    cols = pl.ds(pl.multiple_of(which * TW, 128), TW)
+    halves = []
     for rel in range(3):
         teacher, student = buffers[rel], buffers[3 + rel]
         at = T_AT[rel]
-        keep[:, at : at + TW] = teacher[:, mine]
-        send[:, at : at + TW] = teacher[:, other]
+        out[:, at : at + TW] = teacher[:, cols]
         low = jnp.where(lane < SW, student[:, :SP].astype(F32), 0.0)
         high = pltpu.roll(student[:, 128:].astype(F32), SP - (SW - 128), 1)
         high = jnp.where(lane < SW, high, 0.0)
-        ours.append(jnp.where(me == 0, low, high))
-        theirs.append(jnp.where(me == 0, high, low))
-    for halves, out in ((ours, keep), (theirs, send)):
-        out[:, TW : TW + SP] = halves[0].astype(BF16)
-        second = pltpu.roll(halves[2], S_OFF[2], 1)
-        at = S_AT[1]
-        out[:, at : at + 128] = halves[1][:, :128].astype(BF16)
-        out[:, at + 128 : at + 256] = (halves[1][:, 128:] + second[:, :128]).astype(BF16)
-        out[:, at + 256 : at + 384] = second[:, 128:].astype(BF16)
+        halves.append(jnp.where(which == 0, low, high))
+    out[:, TW : TW + SP] = halves[0].astype(BF16)
+    second = pltpu.roll(halves[2], S_OFF[2], 1)
+    at = S_AT[1]
+    out[:, at : at + 128] = halves[1][:, :128].astype(BF16)
+    out[:, at + 128 : at + 256] = (halves[1][:, 128:] + second[:, :128]).astype(BF16)
+    out[:, at + 256 : at + 384] = second[:, 128:].astype(BF16)
 
 
 def mask_kernel(chip, docs, rows, starts, weights):
@@ -425,15 +421,20 @@
         return lax.ppermute(value, tok, pairs)
 
     arrays = (teacher_q, teacher_k, teacher_v, student_q, student_k, student_v)
-    send, keep = call(
-        split_kernel,
-        [shape(BLOCK, WIDTH, BF16)] * 2,
-        [SMEM] + [HBM] * 6,
-        scratch=[pltpu.VMEM(a.shape, BF16) for a in arrays] + [pltpu.SemaphoreType.DMA((6,))],
-        moved=4 << 20,
-        limit=56,
-    )(core, *arrays)
+
+    def split(own, *after):
+        return call(
+            functools.partial(split_kernel, own),
+            shape(BLOCK, WIDTH, BF16),
+            [SMEM] + [HBM] * (6 + len(after)),
+            scratch=[pltpu.VMEM(a.shape, BF16) for a in arrays] + [pltpu.SemaphoreType.DMA((6,))],
+            moved=4 << 20,
+            limit=56,
+        )(core, *arrays, *after)
+
+    send = split(False)
     recv = other_core(send)
+    keep = split(True, send)
     edges = call_edges(-1, core, keep, recv)
     two = [neighbours(edge, -1) for edge in edges]
     doc_ids, row_weight, _ = lax.optimization_barrier((doc_ids, row_weight, edges[0]))
@@ -455,7 +456,7 @@
         *grad, loss = call_relation(rel, core, starts, weight, loss, chunk)
         grads.append(grad)
 
-    stages = (("z", "parity", "core"), ("y", "head"))
+    stages = (("z", "parity", "core", "head"), ("y",))
     copies = [shape(lax.axis_size(axes), BLOCK, F32) for axes in stages]
 
     def exchange(value, axes):

time: 90.6 us -> 90.9 us (level)
  waiting for transfers between devices: 13.7 us -> 11.4 us
  Pallas kernels: 13.3 us -> 15.3 us
    pallas_call x1 -> x2, Pallas kernels: 2.63 us -> 4.74 us  [split(): call(functools.partial(split_kernel, own), shape(BLOCK, WIDTH, BF16), [SM...]
    ppermute x2, waiting for transfers between devices: 1.91 us -> 0.01 us  [other_core(): return lax.ppermute(value, 'core', [(0, 1), (1, 0)])]
  transfers between devices with their start and end apart: 8 -> 8, of which waited for: 4 -> 3; matrix products, arithmetic and copies ran while one was open for 0% -> 0% of each run, Pallas kernels for 4% -> 6%
where the time goes in v10:
time: 90.9 us; the launch traced here: 90.4 us
  starting transfers between devices  36.2 us (40%)
  blocking collectives  25.5 us (28%)
  Pallas kernels  15.3 us (17%)
  waiting for transfers between devices  11.4 us (13%)
  local copies, waits for them, and re-layouts  1.09 us (1%)
    all_to_all x2, blocking collectives, exchange(): return lax.all_to_all(value, axes, 0, 0, tiled=True)  25.5 us
    ppermute x6, starting transfers between devices, neighbours(): return lax.ppermute(value, tok, pairs)  24.6 us
    ppermute x2, starting transfers between devices, other_core(): return lax.ppermute(value, 'core', [(0, 1), (1, 0)])  11.6 us
    ppermute x6, waiting for transfers between devices, neighbours(): return lax.ppermute(value, tok, pairs)  11.4 us
    pallas_call x3, Pallas kernels, call_relation(): call(functools.partial(relation_kernel, rel), [shape(HALO, SP, BF16), sha...  9.1 us
    pallas_call x2, Pallas kernels, split(): call(functools.partial(split_kernel, own), shape(BLOCK, WIDTH, BF16), [SM...  4.74 us
  transfers between devices with their start and end apart: 8, of which 3 were waited for; matrix products, arithmetic and copies ran while one was open for 0% of the time, Pallas kernels for 6%

profile of v10, /device:TPU:1, one launch (start us, length us, event | category | flops | bytes accessed | tf_op | source)
XLA Modules:
  0.0 90.4 jit_solution(14051096697248585857)
XLA Ops:
  0.6 2.4 %shard_map.111.refs_6_ = bf16[128,2560]{1,0:T(8,128)(2,1)} custom-call(s32[1]{0:T(128)} %bitcast.core, bf16[128,1280]{1,0:T(8,128)(2,1)} %refs_0_.3, bf16[128,1280]{1,0:T(8,128)(2,1)} %refs_1_.3, bf16[128,1280]{1,0:T(8,128)(2,1)} %refs_2_.3, bf16[128,384]{1,0:T(8,128)(2,1)} %refs_3_.3, bf16[128,384]{1,0:T(8,128)(2,1)} %refs_4_.3, bf16[128,384]{1,0:T(8,128)(2,1)} %refs_5_.3), custom_call_target="tpu_custom_call" | custom-call | bytes 4194304 | tf_op jit(solution)/shard_map/pallas_call | solution.py:426
  3.0 8.8 %collective-permute-start = (bf16[128,2560]{1,0:T(8,128)(2,1)}, bf16[128,2560]{1,0:T(8,128)(2,1)S(1)}, u32[]{:S(2)}, u32[]{:S(2)}) collective-permute-start(bf16[128,2560]{1,0:T(8,128)(2,1)} %shard_map.111.refs_6_), channel_id=1, source_target_pairs={{0,4},{4,0},{1,5},{5,1},{2,6},{6,2},{3,7},{7,3},{8,12},{12,8},{9,1... | collective-permute-start | bytes 1966088 | tf_op jit(solution)/shard_map/ppermute | solution.py:416
  11.8 2.4 %shard_map.112.keep.refs_0_ = bf16[128,2560]{1,0:T(8,128)(2,1)} custom-call(s32[1]{0:T(128)} %bitcast.core, bf16[128,1280]{1,0:T(8,128)(2,1)} %refs_0_.3, bf16[128,1280]{1,0:T(8,128)(2,1)} %refs_1_.3, bf16[128,1280]{1,0:T(8,128)(2,1)} %refs_2_.3, bf16[128,384]{1,0:T(8,128)(2,1)} %refs_3_.3, bf16[128,384]{1,0:T(8,128)(2,1)} %refs_4_.3, ...), custom_call_target="tpu_custom_call" | custom-call | bytes 4194304 | tf_op jit(solution)/shard_map/pallas_call | solution.py:426
  14.2 0.0 collective-permute-done.recv.refs_1_
  14.2 0.0 copy-start
  14.2 1.1 %copy-done = bf16[128,2560]{1,0:T(8,128)(2,1)S(1)} copy-done((bf16[128,2560]{1,0:T(8,128)(2,1)S(1)}, bf16[128,2560]{1,0:T(8,128)(2,1)}, u32[]{:S(2)}) %copy-start) | copy-done | bytes 655384
  15.3 0.1 shard_map.113
  15.4 2.1 %collective-permute-start.1 = (bf16[192,1280]{1,0:T(8,128)(2,1)S(1)}, bf16[192,1280]{1,0:T(8,128)(2,1)S(1)}, u32[]{:S(2)}, u32[]{:S(2)}) collective-permute-start(bf16[192,1280]{1,0:T(8,128)(2,1)S(1)} %get-tuple-element.34), channel_id=1, source_target_pairs={{0,504},{4,12},{8,0},{12,20},{16,8},{20,28},{24,16},{28,36},{32,24... | collective-permute-start | bytes 1474568 | tf_op jit(solution)/shard_map/ppermute | solution.py:421
  17.4 1.9 %collective-permute-start.2 = (bf16[192,1280]{1,0:T(8,128)(2,1)S(1)}, bf16[192,1280]{1,0:T(8,128)(2,1)S(1)}, u32[]{:S(2)}, u32[]{:S(2)}) collective-permute-start(bf16[192,1280]{1,0:T(8,128)(2,1)S(1)} %get-tuple-element.39), channel_id=1, source_target_pairs={{0,504},{4,12},{8,0},{12,20},{16,8},{20,28},{24,16},{28,36},{32,24... | collective-permute-start | bytes 1474568 | tf_op jit(solution)/shard_map/ppermute | solution.py:421
  19.4 0.0 copy-done.2
  19.4 0.2 shard_map.114
  19.6 0.1 shard_map.115
  19.7 8.2 %collective-permute-start.3 = (bf16[192,1280]{1,0:T(8,128)(2,1)S(1)}, bf16[192,1280]{1,0:T(8,128)(2,1)S(1)}, u32[]{:S(2)}, u32[]{:S(2)}) collective-permute-start(bf16[192,1280]{1,0:T(8,128)(2,1)S(1)} %get-tuple-element.40), channel_id=1, source_target_pairs={{0,8},{4,508},{8,16},{12,4},{16,24},{20,12},{24,32},{28,20},{32,40... | collective-permute-start | bytes 1474568 | tf_op jit(solution)/shard_map/ppermute | solution.py:421
  27.9 3.4 %collective-permute-start.4 = (bf16[192,1280]{1,0:T(8,128)(2,1)S(1)}, bf16[192,1280]{1,0:T(8,128)(2,1)S(1)}, u32[]{:S(2)}, u32[]{:S(2)}) collective-permute-start(bf16[192,1280]{1,0:T(8,128)(2,1)S(1)} %get-tuple-element.42), channel_id=1, source_target_pairs={{0,8},{4,508},{8,16},{12,4},{16,24},{20,12},{24,32},{28,20},{32,40... | collective-permute-start | bytes 1474568 | tf_op jit(solution)/shard_map/ppermute | solution.py:421
  31.3 4.4 %collective-permute-done.2.refs_3_ = bf16[192,1280]{1,0:T(8,128)(2,1)S(1)} collective-permute-done((bf16[192,1280]{1,0:T(8,128)(2,1)S(1)}, bf16[192,1280]{1,0:T(8,128)(2,1)S(1)}, u32[]{:S(2)}, u32[]{:S(2)}) %collective-permute-start.2) | collective-permute-done | bytes 491552 | tf_op jit(solution)/shard_map/ppermute | solution.py:421
  35.7 0.0 collective-permute-done.1.refs_2_
  35.7 3.3 %collective-permute-done.3.refs_4_ = bf16[192,1280]{1,0:T(8,128)(2,1)S(1)} collective-permute-done((bf16[192,1280]{1,0:T(8,128)(2,1)S(1)}, bf16[192,1280]{1,0:T(8,128)(2,1)S(1)}, u32[]{:S(2)}, u32[]{:S(2)}) %collective-permute-start.3) | collective-permute-done | bytes 491552 | tf_op jit(solution)/shard_map/ppermute | solution.py:421
  39.0 3.0 %shard_map.116 = (bf16[192,256]{1,0:T(8,128)(2,1)S(1)}, f32[256,256]{1,0:T(8,128)S(1)}, bf16[192,256]{1,0:T(8,128)(2,1)S(1)}, f32[1,128]{1,0:T(1,128)S(1)}) custom-call(s32[1]{0:T(128)} %bitcast.core, s32[1,256]{1,0:T(1,128)S(1)} %get-tuple-element.37.starts, f32[1,256]{1,0:T(1,128)S(1)} %get-tuple-element.38.refs_0_.weights, ...), custom_call_target="tpu_custom_call" | custom-call | flops 1342177280 | bytes 2097152 | tf_op jit(solution)/shard_map/pallas_call | solution.py:383
  42.0 3.7 %collective-permute-done.4.refs_5_ = bf16[192,1280]{1,0:T(8,128)(2,1)S(1)} collective-permute-done((bf16[192,1280]{1,0:T(8,128)(2,1)S(1)}, bf16[192,1280]{1,0:T(8,128)(2,1)S(1)}, u32[]{:S(2)}, u32[]{:S(2)}) %collective-permute-start.4) | collective-permute-done | bytes 491552 | tf_op jit(solution)/shard_map/ppermute | solution.py:421
  45.7 3.0 %shard_map.117 = (bf16[192,256]{1,0:T(8,128)(2,1)S(1)}, f32[256,256]{1,0:T(8,128)S(1)}, bf16[192,256]{1,0:T(8,128)(2,1)S(1)}, f32[1,128]{1,0:T(1,128)S(1)}) custom-call(s32[1]{0:T(128)} %bitcast.core, s32[1,256]{1,0:T(1,128)S(1)} %get-tuple-element.37.starts, f32[1,256]{1,0:T(1,128)S(1)} %get-tuple-element.38.refs_0_.weights, ...), custom_call_target="tpu_custom_call" | custom-call | flops 1342177280 | bytes 2097152 | tf_op jit(solution)/shard_map/pallas_call | solution.py:383
  48.8 3.0 %shard_map.118 = (bf16[192,256]{1,0:T(8,128)(2,1)S(1)}, f32[256,256]{1,0:T(8,128)S(1)}, bf16[192,256]{1,0:T(8,128)(2,1)S(1)}, f32[1,128]{1,0:T(1,128)S(1)}) custom-call(s32[1]{0:T(128)} %bitcast.core, s32[1,256]{1,0:T(1,128)S(1)} %get-tuple-element.37.starts, f32[1,256]{1,0:T(1,128)S(1)} %get-tuple-element.38.refs_0_.weights, ...), custom_call_target="tpu_custom_call" | custom-call | flops 1342177280 | bytes 2097152 | tf_op jit(solution)/shard_map/pallas_call | solution.py:383
  51.8 0.1 shard_map.119
  51.9 7.1 %collective-permute-start.5 = (bf16[192,768]{1,0:T(8,128)(2,1)S(1)}, bf16[192,768]{1,0:T(8,128)(2,1)S(1)}, u32[]{:S(2)}, u32[]{:S(2)}) collective-permute-start(bf16[192,768]{1,0:T(8,128)(2,1)S(1)} %get-tuple-element.55), channel_id=1, source_target_pairs={{0,8},{4,508},{8,16},{12,4},{16,24},{20,12},{24,32},{28,20},{32,40... | collective-permute-start | bytes 884744 | tf_op jit(solution)/shard_map/ppermute | solution.py:421
  59.0 1.9 %collective-permute-start.6 = (bf16[192,768]{1,0:T(8,128)(2,1)S(1)}, bf16[192,768]{1,0:T(8,128)(2,1)S(1)}, u32[]{:S(2)}, u32[]{:S(2)}) collective-permute-start(bf16[192,768]{1,0:T(8,128)(2,1)S(1)} %get-tuple-element.56), channel_id=1, source_target_pairs={{0,508},{4,8},{8,4},{12,16},{16,12},{20,24},{24,20},{28,32},{32,28... | collective-permute-start | bytes 884744 | tf_op jit(solution)/shard_map/ppermute | solution.py:421
  60.9 15.4 %all_to_all.22 = f32[64,1,128]{2,1,0:T(1,128)S(1)} all-to-all(f32[64,1,128]{2,1,0:T(1,128)S(1)} %bitcast.16), channel_id=1, replica_groups=mesh['y'=8,'z'=4,'parity'=2,'core'=2,'head'=4] {'z','parity','core','head'}, dimensions={0} | all-to-all | bytes 65536 | tf_op jit(solution)/shard_map/all_to_all | solution.py:463
  76.3 0.0 collective-permute-done.5.mine
  76.3 0.0 collective-permute-done.6.other
  76.3 0.1 shard_map.120
  76.5 2.8 %collective-permute-start.7 = (f32[192,768]{1,0:T(8,128)S(1)}, f32[192,768]{1,0:T(8,128)S(1)}, u32[]{:S(2)}, u32[]{:S(2)}) collective-permute-start(f32[192,768]{1,0:T(8,128)S(1)} %get-tuple-element.59), channel_id=1, source_target_pairs={{0,4},{4,0},{1,5},{5,1},{2,6},{6,2},{3,7},{7,3},{8,12},{12,8},{9,1... | collective-permute-start | bytes 1769480 | tf_op jit(solution)/shard_map/ppermute | solution.py:416
  79.3 10.1 %all_to_all.23 = f32[8,1,128]{2,1,0:T(1,128)S(1)} all-to-all(f32[8,1,128]{2,1,0:T(1,128)S(1)} %bitcast.18), channel_id=1, replica_groups=mesh['y'=8,'z'=4,'parity'=2,'core'=2,'head'=4] {'y'}, dimensions={0} | all-to-all | bytes 8192 | tf_op jit(solution)/shard_map/all_to_all | solution.py:463
  89.5 0.0 collective-permute-done.7.recv
  89.5 0.9 %shard_map.121 = (f32[128,384]{1,0:T(8,128)}, f32[128,384]{1,0:T(8,128)}, f32[128,384]{1,0:T(8,128)}, f32[1,1]{1,0:T(1,128)}) custom-call(s32[1]{0:T(128)} %bitcast.core, f32[8,128]{1,0:T(8,128)S(1)} %bitcast.17, f32[256,768]{1,0:T(8,128)S(1)} %get-tuple-element.58.keep, f32[192,768]{1,0:T(8,128)S(1)} %collective-permute-done.7.recv), custom_call_target="tpu_custom_call" | custom-call | bytes 1048576 | tf_op jit(solution)/shard_map/pallas_call | solution.py:482
  (6 shorter events, 0.0 us)
Async XLA Ops:
  3.0 11.2 %collective-permute-start = (bf16[128,2560]{1,0:T(8,128)(2,1)}, bf16[128,2560]{1,0:T(8,128)(2,1)S(1)}, u32[]{:S(2)}, u32[]{:S(2)}) collective-permute-start(bf16[128,2560]{1,0:T(8,128)(2,1)} %shard_map.111.refs_6_), channel_id=1, source_target_pairs={{0,4},{4,0},{1,5},{5,1},{2,6},{6,2},{3,7},{7,3},{8,12},{12,8},{9,1... | collective-permute-start | bytes 1966088 | tf_op jit(solution)/shard_map/ppermute | solution.py:416
  14.2 1.1 %copy-start = (bf16[128,2560]{1,0:T(8,128)(2,1)S(1)}, bf16[128,2560]{1,0:T(8,128)(2,1)}, u32[]{:S(2)}) copy-start(bf16[128,2560]{1,0:T(8,128)(2,1)} %shard_map.112.keep.refs_0_) | copy-start | bytes 1966084
  15.3 4.1 %copy-start.2 = (s32[16384]{0:T(1024)S(1)}, s32[16384]{0:T(1024)}, u32[]{:S(2)}) copy-start(s32[16384]{0:T(1024)} %param.14) | copy-start | bytes 196612
  15.3 4.1 %copy-start.3 = (f32[16384]{0:T(1024)S(1)}, f32[16384]{0:T(1024)}, u32[]{:S(2)}) copy-start(f32[16384]{0:T(1024)} %param.15) | copy-start | bytes 196612
  15.3 4.3 %copy-start.1 = (bf16[128,2560]{1,0:T(8,128)(2,1)S(1)}, bf16[128,2560]{1,0:T(8,128)(2,1)}, u32[]{:S(2)}) copy-start(bf16[128,2560]{1,0:T(8,128)(2,1)} %shard_map.112.keep.refs_0_) | copy-start | bytes 1966084
  15.4 20.3 %collective-permute-start.1 = (bf16[192,1280]{1,0:T(8,128)(2,1)S(1)}, bf16[192,1280]{1,0:T(8,128)(2,1)S(1)}, u32[]{:S(2)}, u32[]{:S(2)}) collective-permute-start(bf16[192,1280]{1,0:T(8,128)(2,1)S(1)} %get-tuple-element.34), channel_id=1, source_target_pairs={{0,504},{4,12},{8,0},{12,20},{16,8},{20,28},{24,16},{28,36},{32,24... | collective-permute-start | bytes 1474568 | tf_op jit(solution)/shard_map/ppermute | solution.py:421
  17.4 18.3 %collective-permute-start.2 = (bf16[192,1280]{1,0:T(8,128)(2,1)S(1)}, bf16[192,1280]{1,0:T(8,128)(2,1)S(1)}, u32[]{:S(2)}, u32[]{:S(2)}) collective-permute-start(bf16[192,1280]{1,0:T(8,128)(2,1)S(1)} %get-tuple-element.39), channel_id=1, source_target_pairs={{0,504},{4,12},{8,0},{12,20},{16,8},{20,28},{24,16},{28,36},{32,24... | collective-permute-start | bytes 1474568 | tf_op jit(solution)/shard_map/ppermute | solution.py:421
  19.7 19.3 %collective-permute-start.3 = (bf16[192,1280]{1,0:T(8,128)(2,1)S(1)}, bf16[192,1280]{1,0:T(8,128)(2,1)S(1)}, u32[]{:S(2)}, u32[]{:S(2)}) collective-permute-start(bf16[192,1280]{1,0:T(8,128)(2,1)S(1)} %get-tuple-element.40), channel_id=1, source_target_pairs={{0,8},{4,508},{8,16},{12,4},{16,24},{20,12},{24,32},{28,20},{32,40... | collective-permute-start | bytes 1474568 | tf_op jit(solution)/shard_map/ppermute | solution.py:421
  27.9 17.8 %collective-permute-start.4 = (bf16[192,1280]{1,0:T(8,128)(2,1)S(1)}, bf16[192,1280]{1,0:T(8,128)(2,1)S(1)}, u32[]{:S(2)}, u32[]{:S(2)}) collective-permute-start(bf16[192,1280]{1,0:T(8,128)(2,1)S(1)} %get-tuple-element.42), channel_id=1, source_target_pairs={{0,8},{4,508},{8,16},{12,4},{16,24},{20,12},{24,32},{28,20},{32,40... | collective-permute-start | bytes 1474568 | tf_op jit(solution)/shard_map/ppermute | solution.py:421
  51.9 24.5 %collective-permute-start.5 = (bf16[192,768]{1,0:T(8,128)(2,1)S(1)}, bf16[192,768]{1,0:T(8,128)(2,1)S(1)}, u32[]{:S(2)}, u32[]{:S(2)}) collective-permute-start(bf16[192,768]{1,0:T(8,128)(2,1)S(1)} %get-tuple-element.55), channel_id=1, source_target_pairs={{0,8},{4,508},{8,16},{12,4},{16,24},{20,12},{24,32},{28,20},{32,40... | collective-permute-start | bytes 884744 | tf_op jit(solution)/shard_map/ppermute | solution.py:421
  59.0 17.3 %collective-permute-start.6 = (bf16[192,768]{1,0:T(8,128)(2,1)S(1)}, bf16[192,768]{1,0:T(8,128)(2,1)S(1)}, u32[]{:S(2)}, u32[]{:S(2)}) collective-permute-start(bf16[192,768]{1,0:T(8,128)(2,1)S(1)} %get-tuple-element.56), channel_id=1, source_target_pairs={{0,508},{4,8},{8,4},{12,16},{16,12},{20,24},{24,20},{28,32},{32,28... | collective-permute-start | bytes 884744 | tf_op jit(solution)/shard_map/ppermute | solution.py:421
  76.5 13.0 %collective-permute-start.7 = (f32[192,768]{1,0:T(8,128)S(1)}, f32[192,768]{1,0:T(8,128)S(1)}, u32[]{:S(2)}, u32[]{:S(2)}) collective-permute-start(f32[192,768]{1,0:T(8,128)S(1)} %get-tuple-element.59), channel_id=1, source_target_pairs={{0,4},{4,0},{1,5},{5,1},{2,6},{6,2},{3,7},{7,3},{8,12},{12,8},{9,1... | collective-permute-start | bytes 1769480 | tf_op jit(solution)/shard_map/ppermute | solution.py:416

commit v11 on v7

--- a/solution.py
+++ b/solution.py
@@ -24,11 +24,12 @@
 SW = HEADS * DS
 SP = 256
 REL = TW + SP
-PART = 2 * TW
-WIDTH = 2 * PART
-T_AT = (0, PART, PART + TW)
-S_AT = (TW, TW + SP, TW + SP + 128)
-S_OFF = (0, 0, SW - 128)
+WIDTH_A = 2 * TW + 2 * SW
+WIDTH = WIDTH_A + REL
+T_AT = (0, TW, 0)
+S_AT = (2 * TW, 2 * TW + 128, TW)
+CHUNK_AT = (0, 0, WIDTH_A)
+S_OFF = (0, SW - 128, 0)
 CT = DT ** (-0.5) * math.log2(math.e)
 CS = DS ** (-0.5) * math.log2(math.e)
 NT = (((1,), (1,)), ((), ()))
@@ -69,7 +70,7 @@
     ours, theirs = [], []
     for rel in range(3):
         teacher, student = buffers[rel], buffers[3 + rel]
-        at = T_AT[rel]
+        at = CHUNK_AT[rel] + T_AT[rel]
         keep[:, at : at + TW] = teacher[:, mine]
         send[:, at : at + TW] = teacher[:, other]
         low = jnp.where(lane < SW, student[:, :SP].astype(F32), 0.0)
@@ -78,12 +79,12 @@
         ours.append(jnp.where(me == 0, low, high))
         theirs.append(jnp.where(me == 0, high, low))
     for halves, out in ((ours, keep), (theirs, send)):
-        out[:, TW : TW + SP] = halves[0].astype(BF16)
-        second = pltpu.roll(halves[2], S_OFF[2], 1)
-        at = S_AT[1]
-        out[:, at : at + 128] = halves[1][:, :128].astype(BF16)
-        out[:, at + 128 : at + 256] = (halves[1][:, 128:] + second[:, :128]).astype(BF16)
+        second = pltpu.roll(halves[1], S_OFF[1], 1)
+        at = 2 * TW
+        out[:, at : at + 128] = halves[0][:, :128].astype(BF16)
+        out[:, at + 128 : at + 256] = (halves[0][:, 128:] + second[:, :128]).astype(BF16)
         out[:, at + 256 : at + 384] = second[:, 128:].astype(BF16)
+        out[:, WIDTH_A + TW :] = halves[2].astype(BF16)
 
 
 def mask_kernel(chip, docs, rows, starts, weights):
@@ -155,21 +156,20 @@
     loss_in,
     *refs,
 ):
-    keep, recv, *halo = refs[:-12]
+    keep, recv, one, two = refs[:-12]
+    t_at, s_at, s_off = T_AT[rel], S_AT[rel], S_OFF[rel]
     grad_left, grad_own, grad_right, loss_out, win, bias, rt, rs, gt, qs, bt, kg = refs[-12:]
-    t_at, s_at, s_off = T_AT[rel], S_AT[rel], S_OFF[rel]
     me = core[0]
+    def gather(at, rows, source):
+        base = CHUNK_AT[rel] if source.shape[1] == WIDTH else 0
+        win[at : at + rows, :TW] = source[:, base + t_at : base + t_at + TW]
+        win[at : at + rows, TW:] = source[:, base + s_at : base + s_at + SP]
 
     def gather_all(*sources):
         at = 0
         for source in sources:
-            t_source, s_source = source if isinstance(source, tuple) else (source, source)
-            rows, width = t_source.shape
-            win[at : at + rows, :TW] = t_source[:, t_at % width : t_at % width + TW]
-            win[at : at + rows, TW:] = s_source[:, s_at : s_at + SP]
-            at += rows
-
-    one, two = (halo[-2], halo[0]), (halo[-1], halo[1])
+            gather(at, source.shape[0], source)
+            at += source.shape[0]
 
     @pl.when(me == 0)
     def _():
@@ -430,7 +430,7 @@
         limit=56,
     )(core, *arrays)
     recv = other_core(send)
-    edges_a = call_edges(slice(0, PART), core, keep, recv)
+    edges_a = call_edges(slice(0, WIDTH_A), core, keep, recv)
     halo_a = [neighbours(edges_a[0], 1), neighbours(edges_a[1], -1)]
     doc_ids, row_weight, _ = lax.optimization_barrier((doc_ids, row_weight, edges_a[0]))
     starts, weight = call(
@@ -443,13 +443,12 @@
         doc_ids.reshape(-1, BLOCK),
         row_weight.reshape(-1, BLOCK),
     )
-    edges_b = call_edges(slice(PART, WIDTH), core, keep, recv, weight)
+    edges_b = call_edges(slice(WIDTH_A, WIDTH), core, keep, recv, weight)
     halo_b = [neighbours(edges_b[0], 1), neighbours(edges_b[1], -1)]
-
     loss = jnp.zeros((1, BLOCK), F32)
     grads = []
     for rel in range(3):
-        chunk = (keep, recv, *halo_a, *(halo_b if rel else ()))
+        chunk = (keep, recv, *(halo_b if rel == 2 else halo_a))
         *grad, loss = call_relation(rel, core, starts, weight, loss, chunk)
         grads.append(grad)
 

time: 90.7 us -> 88.4 us (0.975)
  waiting for transfers between devices: 15.5 us -> 10.9 us
  starting transfers between devices: 33.5 us -> 35.8 us
    ppermute x6, waiting for transfers between devices: 13.5 us -> 8.97 us  [neighbours(): return lax.ppermute(value, tok, pairs)]
    ppermute x6, starting transfers between devices: 22.1 us -> 24.4 us  [neighbours(): return lax.ppermute(value, tok, pairs)]
  transfers between devices with their start and end apart: 8 -> 8, of which waited for: 4 -> 4; matrix products, arithmetic and copies ran while one was open for 0% -> 0% of each run, Pallas kernels for 4% -> 7%
where the time goes in v11:
time: 88.4 us; the launch traced here: 87.9 us
  starting transfers between devices  35.8 us (40%)
  blocking collectives  25.3 us (29%)
  Pallas kernels  14.1 us (16%)
  waiting for transfers between devices  10.9 us (12%)
  local copies, waits for them, and re-layouts  1.1 us (1%)
    all_to_all x2, blocking collectives, exchange(): return lax.all_to_all(value, axes, 0, 0, tiled=True)  25.3 us
    ppermute x6, starting transfers between devices, neighbours(): return lax.ppermute(value, tok, pairs)  24.4 us
    ppermute x2, starting transfers between devices, other_core(): return lax.ppermute(value, 'core', [(0, 1), (1, 0)])  11.4 us
    pallas_call x3, Pallas kernels, call_relation(): call(functools.partial(relation_kernel, rel), [shape(HALO, SP, BF16), sha...  9.1 us
    ppermute x6, waiting for transfers between devices, neighbours(): return lax.ppermute(value, tok, pairs)  8.97 us
    pallas_call x1, Pallas kernels, body(): call(split_kernel, [shape(BLOCK, WIDTH, BF16)] * 2, [SMEM] + [HBM] * 6, s...  2.61 us
    ppermute x2, waiting for transfers between devices, other_core(): return lax.ppermute(value, 'core', [(0, 1), (1, 0)])  1.92 us
  transfers between devices with their start and end apart: 8, of which 4 were waited for; matrix products, arithmetic and copies ran while one was open for 0% of the time, Pallas kernels for 7%

profile of v11, /device:TPU:1, one launch (start us, length us, event | category | flops | bytes accessed | tf_op | source)
XLA Modules:
  0.0 87.9 jit_solution(5647249325026857615)
XLA Ops:
  0.6 2.6 %shard_map.111 = (bf16[128,2560]{1,0:T(8,128)(2,1)}, bf16[128,2560]{1,0:T(8,128)(2,1)}) custom-call(s32[1]{0:T(128)} %bitcast.core, bf16[128,1280]{1,0:T(8,128)(2,1)} %refs_0_.1, bf16[128,1280]{1,0:T(8,128)(2,1)} %refs_1_.1, bf16[128,1280]{1,0:T(8,128)(2,1)} %refs_2_.1, bf16[128,384]{1,0:T(8,128)(2,1)} %refs_3_.1, bf16[128,384]{1,0:T(8,128)(2,1)} %refs_4_.1, ...), custom_call_target="tpu_custom_call" | custom-call | bytes 4194304 | tf_op jit(solution)/shard_map/pallas_call | solution.py:424
  3.3 8.8 %collective-permute-start = (bf16[128,2560]{1,0:T(8,128)(2,1)}, bf16[128,2560]{1,0:T(8,128)(2,1)S(1)}, u32[]{:S(2)}, u32[]{:S(2)}) collective-permute-start(bf16[128,2560]{1,0:T(8,128)(2,1)} %get-tuple-element.37), channel_id=1, source_target_pairs={{0,4},{4,0},{1,5},{5,1},{2,6},{6,2},{3,7},{7,3},{8,12},{12,8},{9,1... | collective-permute-start | bytes 1966088 | tf_op jit(solution)/shard_map/ppermute | solution.py:416
  12.1 1.9 %collective-permute-done.recv.refs_1_ = bf16[128,2560]{1,0:T(8,128)(2,1)S(1)} collective-permute-done((bf16[128,2560]{1,0:T(8,128)(2,1)}, bf16[128,2560]{1,0:T(8,128)(2,1)S(1)}, u32[]{:S(2)}, u32[]{:S(2)}) %collective-permute-start) | collective-permute-done | bytes 655392 | tf_op jit(solution)/shard_map/ppermute | solution.py:416
  14.0 1.1 %copy-done = bf16[128,2560]{1,0:T(8,128)(2,1)S(1)} copy-done((bf16[128,2560]{1,0:T(8,128)(2,1)S(1)}, bf16[128,2560]{1,0:T(8,128)(2,1)}, u32[]{:S(2)}) %copy-start) | copy-done | bytes 655384
  15.1 0.9 %shard_map.112 = (bf16[192,1664]{1,0:T(8,128)(2,1)S(1)}, bf16[192,1664]{1,0:T(8,128)(2,1)}) custom-call(s32[1]{0:T(128)} %bitcast.core, bf16[128,2560]{1,0:T(8,128)(2,1)S(1)} %copy-done, bf16[128,2560]{1,0:T(8,128)(2,1)S(1)} %collective-permute-done.recv.refs_1_), custom_call_target="tpu_custom_call" | custom-call | bytes 2097152 | tf_op jit(solution)/shard_map/pallas_call | solution.py:138
  16.0 1.9 %collective-permute-start.2 = (bf16[192,1664]{1,0:T(8,128)(2,1)}, bf16[192,1664]{1,0:T(8,128)(2,1)S(1)}, u32[]{:S(2)}, u32[]{:S(2)}) collective-permute-start(bf16[192,1664]{1,0:T(8,128)(2,1)} %get-tuple-element.43), channel_id=1, source_target_pairs={{0,504},{4,12},{8,0},{12,20},{16,8},{20,28},{24,16},{28,36},{32,24... | collective-permute-start | bytes 1916936 | tf_op jit(solution)/shard_map/ppermute | solution.py:421
  17.9 8.2 %collective-permute-start.1 = (bf16[192,1664]{1,0:T(8,128)(2,1)S(1)}, bf16[192,1664]{1,0:T(8,128)(2,1)S(1)}, u32[]{:S(2)}, u32[]{:S(2)}) collective-permute-start(bf16[192,1664]{1,0:T(8,128)(2,1)S(1)} %get-tuple-element.38), channel_id=1, source_target_pairs={{0,8},{4,508},{8,16},{12,4},{16,24},{20,12},{24,32},{28,20},{32,40... | collective-permute-start | bytes 1916936 | tf_op jit(solution)/shard_map/ppermute | solution.py:421
  26.1 0.0 copy-done.2
  26.1 0.0 copy-done.3
  26.2 0.2 shard_map.113
  26.4 0.0 copy-done.1
  26.4 0.1 shard_map.116
  26.5 3.4 %collective-permute-start.3 = (bf16[192,896]{1,0:T(8,128)(2,1)S(1)}, bf16[192,896]{1,0:T(8,128)(2,1)S(1)}, u32[]{:S(2)}, u32[]{:S(2)}) collective-permute-start(bf16[192,896]{1,0:T(8,128)(2,1)S(1)} %get-tuple-element.46), channel_id=1, source_target_pairs={{0,8},{4,508},{8,16},{12,4},{16,24},{20,12},{24,32},{28,20},{32,40... | collective-permute-start | bytes 1032200 | tf_op jit(solution)/shard_map/ppermute | solution.py:421
  29.8 1.9 %collective-permute-start.4 = (bf16[192,896]{1,0:T(8,128)(2,1)S(1)}, bf16[192,896]{1,0:T(8,128)(2,1)S(1)}, u32[]{:S(2)}, u32[]{:S(2)}) collective-permute-start(bf16[192,896]{1,0:T(8,128)(2,1)S(1)} %get-tuple-element.47), channel_id=1, source_target_pairs={{0,504},{4,12},{8,0},{12,20},{16,8},{20,28},{24,16},{28,36},{32,24... | collective-permute-start | bytes 1032200 | tf_op jit(solution)/shard_map/ppermute | solution.py:421
  31.8 0.4 collective-permute-done.2.refs_3_
  32.2 8.1 %collective-permute-done.1.refs_2_ = bf16[192,1664]{1,0:T(8,128)(2,1)S(1)} collective-permute-done((bf16[192,1664]{1,0:T(8,128)(2,1)S(1)}, bf16[192,1664]{1,0:T(8,128)(2,1)S(1)}, u32[]{:S(2)}, u32[]{:S(2)}) %collective-permute-start.1) | collective-permute-done | bytes 639008 | tf_op jit(solution)/shard_map/ppermute | solution.py:421
  40.3 3.0 %shard_map.114 = (bf16[192,256]{1,0:T(8,128)(2,1)S(1)}, f32[256,256]{1,0:T(8,128)S(1)}, bf16[192,256]{1,0:T(8,128)(2,1)S(1)}, f32[1,128]{1,0:T(1,128)S(1)}) custom-call(s32[1]{0:T(128)} %bitcast.core, s32[1,256]{1,0:T(1,128)S(1)} %get-tuple-element.41.starts, f32[1,256]{1,0:T(1,128)S(1)} %get-tuple-element.42.weights.refs_0_, ...), custom_call_target="tpu_custom_call" | custom-call | flops 1342177280 | bytes 2097152 | tf_op jit(solution)/shard_map/pallas_call | solution.py:383
  43.3 3.0 %shard_map.115 = (bf16[192,256]{1,0:T(8,128)(2,1)S(1)}, f32[256,256]{1,0:T(8,128)S(1)}, bf16[192,256]{1,0:T(8,128)(2,1)S(1)}, f32[1,128]{1,0:T(1,128)S(1)}) custom-call(s32[1]{0:T(128)} %bitcast.core, s32[1,256]{1,0:T(1,128)S(1)} %get-tuple-element.41.starts, f32[1,256]{1,0:T(1,128)S(1)} %get-tuple-element.42.weights.refs_0_, ...), custom_call_target="tpu_custom_call" | custom-call | flops 1342177280 | bytes 2097152 | tf_op jit(solution)/shard_map/pallas_call | solution.py:383
  46.4 0.4 collective-permute-done.3.refs_2_
  46.8 0.0 collective-permute-done.4.refs_3_
  46.8 3.0 %shard_map.117 = (bf16[192,256]{1,0:T(8,128)(2,1)S(1)}, f32[256,256]{1,0:T(8,128)S(1)}, bf16[192,256]{1,0:T(8,128)(2,1)S(1)}, f32[1,128]{1,0:T(1,128)S(1)}) custom-call(s32[1]{0:T(128)} %bitcast.core, s32[1,256]{1,0:T(1,128)S(1)} %get-tuple-element.41.starts, f32[1,256]{1,0:T(1,128)S(1)} %get-tuple-element.42.weights.refs_0_, ...), custom_call_target="tpu_custom_call" | custom-call | flops 1342177280 | bytes 2097152 | tf_op jit(solution)/shard_map/pallas_call | solution.py:383
  49.9 0.1 shard_map.118
  49.9 7.1 %collective-permute-start.5 = (bf16[192,768]{1,0:T(8,128)(2,1)S(1)}, bf16[192,768]{1,0:T(8,128)(2,1)S(1)}, u32[]{:S(2)}, u32[]{:S(2)}) collective-permute-start(bf16[192,768]{1,0:T(8,128)(2,1)S(1)} %get-tuple-element.59), channel_id=1, source_target_pairs={{0,8},{4,508},{8,16},{12,4},{16,24},{20,12},{24,32},{28,20},{32,40... | collective-permute-start | bytes 884744 | tf_op jit(solution)/shard_map/ppermute | solution.py:421
  57.1 1.9 %collective-permute-start.6 = (bf16[192,768]{1,0:T(8,128)(2,1)S(1)}, bf16[192,768]{1,0:T(8,128)(2,1)S(1)}, u32[]{:S(2)}, u32[]{:S(2)}) collective-permute-start(bf16[192,768]{1,0:T(8,128)(2,1)S(1)} %get-tuple-element.60), channel_id=1, source_target_pairs={{0,508},{4,8},{8,4},{12,16},{16,12},{20,24},{24,20},{28,32},{32,28... | collective-permute-start | bytes 884744 | tf_op jit(solution)/shard_map/ppermute | solution.py:421
  59.0 10.2 %all_to_all.22 = f32[16,1,128]{2,1,0:T(1,128)S(1)} all-to-all(f32[16,1,128]{2,1,0:T(1,128)S(1)} %bitcast.18), channel_id=1, replica_groups=mesh['y'=8,'z'=4,'parity'=2,'core'=2,'head'=4] {'z','parity','core'}, dimensions={0} | all-to-all | bytes 16384 | tf_op jit(solution)/shard_map/all_to_all | solution.py:459
  69.2 0.0 collective-permute-done.5.mine
  69.2 0.0 collective-permute-done.6.other
  69.2 0.1 shard_map.119
  69.4 2.6 %collective-permute-start.7 = (f32[192,768]{1,0:T(8,128)S(1)}, f32[192,768]{1,0:T(8,128)S(1)}, u32[]{:S(2)}, u32[]{:S(2)}) collective-permute-start(f32[192,768]{1,0:T(8,128)S(1)} %get-tuple-element.63), channel_id=1, source_target_pairs={{0,4},{4,0},{1,5},{5,1},{2,6},{6,2},{3,7},{7,3},{8,12},{12,8},{9,1... | collective-permute-start | bytes 1769480 | tf_op jit(solution)/shard_map/ppermute | solution.py:416
  71.9 15.0 %all_to_all.23 = f32[32,1,128]{2,1,0:T(1,128)S(1)} all-to-all(f32[32,1,128]{2,1,0:T(1,128)S(1)} %bitcast.17), channel_id=1, replica_groups=mesh['y'=8,'z'=4,'parity'=2,'core'=2,'head'=4] {'y','head'}, dimensions={0} | all-to-all | bytes 32768 | tf_op jit(solution)/shard_map/all_to_all | solution.py:459
  87.0 0.0 collective-permute-done.7.recv
  87.0 1.0 %shard_map.120 = (f32[128,384]{1,0:T(8,128)}, f32[128,384]{1,0:T(8,128)}, f32[128,384]{1,0:T(8,128)}, f32[1,1]{1,0:T(1,128)}) custom-call(s32[1]{0:T(128)} %bitcast.core, f32[32,128]{1,0:T(8,128)S(1)} %bitcast.13, f32[256,768]{1,0:T(8,128)S(1)} %get-tuple-element.62.keep, f32[192,768]{1,0:T(8,128)S(1)} %collective-permute-done.7.recv), custom_call_target="tpu_custom_call" | custom-call | bytes 1048576 | tf_op jit(solution)/shard_map/pallas_call | solution.py:478
  (5 shorter events, 0.0 us)
Async XLA Ops:
  3.3 10.7 %collective-permute-start = (bf16[128,2560]{1,0:T(8,128)(2,1)}, bf16[128,2560]{1,0:T(8,128)(2,1)S(1)}, u32[]{:S(2)}, u32[]{:S(2)}) collective-permute-start(bf16[128,2560]{1,0:T(8,128)(2,1)} %get-tuple-element.37), channel_id=1, source_target_pairs={{0,4},{4,0},{1,5},{5,1},{2,6},{6,2},{3,7},{7,3},{8,12},{12,8},{9,1... | collective-permute-start | bytes 1966088 | tf_op jit(solution)/shard_map/ppermute | solution.py:416
  14.0 1.1 %copy-start = (bf16[128,2560]{1,0:T(8,128)(2,1)S(1)}, bf16[128,2560]{1,0:T(8,128)(2,1)}, u32[]{:S(2)}) copy-start(bf16[128,2560]{1,0:T(8,128)(2,1)} %get-tuple-element.36.keep.refs_0_) | copy-start | bytes 1966084
  15.1 11.1 %copy-start.2 = (s32[16384]{0:T(1024)S(1)}, s32[16384]{0:T(1024)}, u32[]{:S(2)}) copy-start(s32[16384]{0:T(1024)} %param.14) | copy-start | bytes 196612
  15.1 11.1 %copy-start.3 = (f32[16384]{0:T(1024)S(1)}, f32[16384]{0:T(1024)}, u32[]{:S(2)}) copy-start(f32[16384]{0:T(1024)} %param.15) | copy-start | bytes 196612
  15.1 11.3 %copy-start.1 = (bf16[128,2560]{1,0:T(8,128)(2,1)S(1)}, bf16[128,2560]{1,0:T(8,128)(2,1)}, u32[]{:S(2)}) copy-start(bf16[128,2560]{1,0:T(8,128)(2,1)} %get-tuple-element.36.keep.refs_0_) | copy-start | bytes 1966084
  16.0 16.2 %collective-permute-start.2 = (bf16[192,1664]{1,0:T(8,128)(2,1)}, bf16[192,1664]{1,0:T(8,128)(2,1)S(1)}, u32[]{:S(2)}, u32[]{:S(2)}) collective-permute-start(bf16[192,1664]{1,0:T(8,128)(2,1)} %get-tuple-element.43), channel_id=1, source_target_pairs={{0,504},{4,12},{8,0},{12,20},{16,8},{20,28},{24,16},{28,36},{32,24... | collective-permute-start | bytes 1916936 | tf_op jit(solution)/shard_map/ppermute | solution.py:421
  17.9 22.4 %collective-permute-start.1 = (bf16[192,1664]{1,0:T(8,128)(2,1)S(1)}, bf16[192,1664]{1,0:T(8,128)(2,1)S(1)}, u32[]{:S(2)}, u32[]{:S(2)}) collective-permute-start(bf16[192,1664]{1,0:T(8,128)(2,1)S(1)} %get-tuple-element.38), channel_id=1, source_target_pairs={{0,8},{4,508},{8,16},{12,4},{16,24},{20,12},{24,32},{28,20},{32,40... | collective-permute-start | bytes 1916936 | tf_op jit(solution)/shard_map/ppermute | solution.py:421
  26.5 20.3 %collective-permute-start.3 = (bf16[192,896]{1,0:T(8,128)(2,1)S(1)}, bf16[192,896]{1,0:T(8,128)(2,1)S(1)}, u32[]{:S(2)}, u32[]{:S(2)}) collective-permute-start(bf16[192,896]{1,0:T(8,128)(2,1)S(1)} %get-tuple-element.46), channel_id=1, source_target_pairs={{0,8},{4,508},{8,16},{12,4},{16,24},{20,12},{24,32},{28,20},{32,40... | collective-permute-start | bytes 1032200 | tf_op jit(solution)/shard_map/ppermute | solution.py:421
  29.8 17.0 %collective-permute-start.4 = (bf16[192,896]{1,0:T(8,128)(2,1)S(1)}, bf16[192,896]{1,0:T(8,128)(2,1)S(1)}, u32[]{:S(2)}, u32[]{:S(2)}) collective-permute-start(bf16[192,896]{1,0:T(8,128)(2,1)S(1)} %get-tuple-element.47), channel_id=1, source_target_pairs={{0,504},{4,12},{8,0},{12,20},{16,8},{20,28},{24,16},{28,36},{32,24... | collective-permute-start | bytes 1032200 | tf_op jit(solution)/shard_map/ppermute | solution.py:421
  49.9 19.3 %collective-permute-start.5 = (bf16[192,768]{1,0:T(8,128)(2,1)S(1)}, bf16[192,768]{1,0:T(8,128)(2,1)S(1)}, u32[]{:S(2)}, u32[]{:S(2)}) collective-permute-start(bf16[192,768]{1,0:T(8,128)(2,1)S(1)} %get-tuple-element.59), channel_id=1, source_target_pairs={{0,8},{4,508},{8,16},{12,4},{16,24},{20,12},{24,32},{28,20},{32,40... | collective-permute-start | bytes 884744 | tf_op jit(solution)/shard_map/ppermute | solution.py:421
  57.1 12.2 %collective-permute-start.6 = (bf16[192,768]{1,0:T(8,128)(2,1)S(1)}, bf16[192,768]{1,0:T(8,128)(2,1)S(1)}, u32[]{:S(2)}, u32[]{:S(2)}) collective-permute-start(bf16[192,768]{1,0:T(8,128)(2,1)S(1)} %get-tuple-element.60), channel_id=1, source_target_pairs={{0,508},{4,8},{8,4},{12,16},{16,12},{20,24},{24,20},{28,32},{32,28... | collective-permute-start | bytes 884744 | tf_op jit(solution)/shard_map/ppermute | solution.py:421
  69.4 17.6 %collective-permute-start.7 = (f32[192,768]{1,0:T(8,128)S(1)}, f32[192,768]{1,0:T(8,128)S(1)}, u32[]{:S(2)}, u32[]{:S(2)}) collective-permute-start(f32[192,768]{1,0:T(8,128)S(1)} %get-tuple-element.63), channel_id=1, source_target_pairs={{0,4},{4,0},{1,5},{5,1},{2,6},{6,2},{3,7},{7,3},{8,12},{12,8},{9,1... | collective-permute-start | bytes 1769480 | tf_op jit(solution)/shard_map/ppermute | solution.py:416

commit v12 on v11

--- a/solution.py
+++ b/solution.py
@@ -134,6 +134,36 @@
         write(recv, keep, two, one)
 
 
+def edge_kernel(way, cols, core, keep, recv, *refs):
+    out = refs[-1]
+    half = HALO - BLOCK
+
+    def write(first, second, late):
+        if late:
+            out[:half, :] = first[BLOCK - half :, cols]
+            out[half:, :] = second[:, cols]
+        else:
+            out[:BLOCK, :] = first[:, cols]
+            out[BLOCK:, :] = second[:half, cols]
+
+    @pl.when(core[0] == 0)
+    def _():
+        write(keep, recv, way > 0)
+
+    @pl.when(core[0] != 0)
+    def _():
+        write(recv, keep, way < 0)
+
+
+def call_edge(way, cols, core, keep, recv):
+    return call(
+        functools.partial(edge_kernel, way, cols),
+        shape(HALO, cols.stop - cols.start, BF16),
+        [SMEM] + [VMEM] * 2,
+        moved=1 << 20,
+    )(core, keep, recv)
+
+
 def call_edges(cols, core, keep, recv, *after):
     return call(
         functools.partial(edges_kernel, cols),
@@ -157,6 +187,8 @@
     *refs,
 ):
     keep, recv, one, two = refs[:-12]
+    if rel == 2:
+        one, two = two, one
     t_at, s_at, s_off = T_AT[rel], S_AT[rel], S_OFF[rel]
     grad_left, grad_own, grad_right, loss_out, win, bias, rt, rs, gt, qs, bt, kg = refs[-12:]
     me = core[0]
@@ -430,7 +462,9 @@
         limit=56,
     )(core, *arrays)
     recv = other_core(send)
-    edges_a = call_edges(slice(0, WIDTH_A), core, keep, recv)
+    back = call_edge(-1, slice(0, WIDTH_A), core, keep, recv)
+    keep, recv, back = lax.optimization_barrier((keep, recv, back))
+    edges_a = call_edge(1, slice(0, WIDTH_A), core, keep, recv), back
     halo_a = [neighbours(edges_a[0], 1), neighbours(edges_a[1], -1)]
     doc_ids, row_weight, _ = lax.optimization_barrier((doc_ids, row_weight, edges_a[0]))
     starts, weight = call(
@@ -444,7 +478,7 @@
         row_weight.reshape(-1, BLOCK),
     )
     edges_b = call_edges(slice(WIDTH_A, WIDTH), core, keep, recv, weight)
-    halo_b = [neighbours(edges_b[0], 1), neighbours(edges_b[1], -1)]
+    halo_b = [neighbours(edges_b[1], -1), neighbours(edges_b[0], 1)]
     loss = jnp.zeros((1, BLOCK), F32)
     grads = []
     for rel in range(3):

time: 88.4 us -> 91 us (1.029)
  waiting for transfers between devices: 10.9 us -> 6.71 us
  blocking collectives: 25.3 us -> 29.3 us
  starting transfers between devices: 35.8 us -> 37.1 us
  Pallas kernels: 14.1 us -> 15.4 us
    ppermute x6, waiting for transfers between devices: 8.97 us -> 4.8 us  [neighbours(): return lax.ppermute(value, tok, pairs)]
    all_to_all x2, blocking collectives: 25.3 us -> 29.3 us  [exchange(): return lax.all_to_all(value, axes, 0, 0, tiled=True)]
    pallas_call x3, Pallas kernels: 9.1 us -> 11.3 us  [call_relation(): call(functools.partial(relation_kernel, rel), [shape(HALO, SP, BF16), sha...]
    ppermute x6, starting transfers between devices: 24.4 us -> 25.7 us  [neighbours(): return lax.ppermute(value, tok, pairs)]
    pallas_call x2 -> x1, Pallas kernels: 1 us -> 0.06 us  [call_edges(): call(functools.partial(edges_kernel, cols), [shape(HALO, cols.stop - cols...]
  transfers between devices with their start and end apart: 8 -> 8, of which waited for: 4 -> 3; matrix products, arithmetic and copies ran while one was open for 0% -> 0% of each run, Pallas kernels for 7% -> 9%
where the time goes in v12:
time: 91 us; the launch traced here: 90.4 us
  starting transfers between devices  37.1 us (41%)
  blocking collectives  29.3 us (32%)
  Pallas kernels  15.4 us (17%)
  waiting for transfers between devices  6.71 us (7%)
  local copies, waits for them, and re-layouts  1.11 us (1%)
    all_to_all x2, blocking collectives, exchange(): return lax.all_to_all(value, axes, 0, 0, tiled=True)  29.3 us
    ppermute x6, starting transfers between devices, neighbours(): return lax.ppermute(value, tok, pairs)  25.7 us
    ppermute x2, starting transfers between devices, other_core(): return lax.ppermute(value, 'core', [(0, 1), (1, 0)])  11.4 us
    pallas_call x3, Pallas kernels, call_relation(): call(functools.partial(relation_kernel, rel), [shape(HALO, SP, BF16), sha...  11.3 us
    ppermute x6, waiting for transfers between devices, neighbours(): return lax.ppermute(value, tok, pairs)  4.8 us
    pallas_call x1, Pallas kernels, body(): call(split_kernel, [shape(BLOCK, WIDTH, BF16)] * 2, [SMEM] + [HBM] * 6, s...  2.62 us
    ppermute x2, waiting for transfers between devices, other_core(): return lax.ppermute(value, 'core', [(0, 1), (1, 0)])  1.92 us
  transfers between devices with their start and end apart: 8, of which 3 were waited for; matrix products, arithmetic and copies ran while one was open for 0% of the time, Pallas kernels for 9%

profile of v12, /device:TPU:1, one launch (start us, length us, event | category | flops | bytes accessed | tf_op | source)
XLA Modules:
  0.0 90.4 jit_solution(6140283677080843523)
XLA Ops:
  0.6 2.6 %shard_map.111 = (bf16[128,2560]{1,0:T(8,128)(2,1)}, bf16[128,2560]{1,0:T(8,128)(2,1)}) custom-call(s32[1]{0:T(128)} %bitcast.core, bf16[128,1280]{1,0:T(8,128)(2,1)} %refs_0_.1, bf16[128,1280]{1,0:T(8,128)(2,1)} %refs_1_.1, bf16[128,1280]{1,0:T(8,128)(2,1)} %refs_2_.1, bf16[128,384]{1,0:T(8,128)(2,1)} %refs_3_.1, bf16[128,384]{1,0:T(8,128)(2,1)} %refs_4_.1, ...), custom_call_target="tpu_custom_call" | custom-call | bytes 4194304 | tf_op jit(solution)/shard_map/pallas_call | solution.py:456
  3.3 8.8 %collective-permute-start = (bf16[128,2560]{1,0:T(8,128)(2,1)}, bf16[128,2560]{1,0:T(8,128)(2,1)S(1)}, u32[]{:S(2)}, u32[]{:S(2)}) collective-permute-start(bf16[128,2560]{1,0:T(8,128)(2,1)} %get-tuple-element.38), channel_id=1, source_target_pairs={{0,4},{4,0},{1,5},{5,1},{2,6},{6,2},{3,7},{7,3},{8,12},{12,8},{9,1... | collective-permute-start | bytes 1966088 | tf_op jit(solution)/shard_map/ppermute | solution.py:448
  12.1 1.9 %collective-permute-done.recv.refs_1_ = bf16[128,2560]{1,0:T(8,128)(2,1)S(1)} collective-permute-done((bf16[128,2560]{1,0:T(8,128)(2,1)}, bf16[128,2560]{1,0:T(8,128)(2,1)S(1)}, u32[]{:S(2)}, u32[]{:S(2)}) %collective-permute-start) | collective-permute-done | bytes 655392 | tf_op jit(solution)/shard_map/ppermute | solution.py:448
  14.0 1.1 %copy-done = bf16[128,2560]{1,0:T(8,128)(2,1)S(1)} copy-done((bf16[128,2560]{1,0:T(8,128)(2,1)S(1)}, bf16[128,2560]{1,0:T(8,128)(2,1)}, u32[]{:S(2)}) %copy-start) | copy-done | bytes 655384
  15.1 0.0 copy-start.2
  15.1 0.0 copy-start.3
  15.1 0.0 copy-start.1
  15.1 0.1 shard_map.113
  15.2 8.3 %collective-permute-start.1 = (bf16[192,1664]{1,0:T(8,128)(2,1)S(1)}, bf16[192,1664]{1,0:T(8,128)(2,1)S(1)}, u32[]{:S(2)}, u32[]{:S(2)}) collective-permute-start(bf16[192,1664]{1,0:T(8,128)(2,1)S(1)} %shard_map.113), channel_id=1, source_target_pairs={{0,8},{4,508},{8,16},{12,4},{16,24},{20,12},{24,32},{28,20},{32,40... | collective-permute-start | bytes 1916936 | tf_op jit(solution)/shard_map/ppermute | solution.py:453
  23.6 1.9 %collective-permute-start.2 = (bf16[192,1664]{1,0:T(8,128)(2,1)S(1)}, bf16[192,1664]{1,0:T(8,128)(2,1)}, u32[]{:S(2)}, u32[]{:S(2)}) collective-permute-start(bf16[192,1664]{1,0:T(8,128)(2,1)S(1)} %shard_map.112), channel_id=1, source_target_pairs={{0,504},{4,12},{8,0},{12,20},{16,8},{20,28},{24,16},{28,36},{32,24... | collective-permute-start | bytes 1916936 | tf_op jit(solution)/shard_map/ppermute | solution.py:453
  25.5 0.2 shard_map.114
  25.7 0.1 shard_map.117
  25.8 1.9 %collective-permute-start.3 = (bf16[192,896]{1,0:T(8,128)(2,1)S(1)}, bf16[192,896]{1,0:T(8,128)(2,1)S(1)}, u32[]{:S(2)}, u32[]{:S(2)}) collective-permute-start(bf16[192,896]{1,0:T(8,128)(2,1)S(1)} %get-tuple-element.48), channel_id=1, source_target_pairs={{0,504},{4,12},{8,0},{12,20},{16,8},{20,28},{24,16},{28,36},{32,24... | collective-permute-start | bytes 1032200 | tf_op jit(solution)/shard_map/ppermute | solution.py:453
  27.7 6.7 %collective-permute-start.4 = (bf16[192,896]{1,0:T(8,128)(2,1)S(1)}, bf16[192,896]{1,0:T(8,128)(2,1)S(1)}, u32[]{:S(2)}, u32[]{:S(2)}) collective-permute-start(bf16[192,896]{1,0:T(8,128)(2,1)S(1)} %get-tuple-element.49), channel_id=1, source_target_pairs={{0,8},{4,508},{8,16},{12,4},{16,24},{20,12},{24,32},{28,20},{32,40... | collective-permute-start | bytes 1032200 | tf_op jit(solution)/shard_map/ppermute | solution.py:453
  34.4 0.5 collective-permute-done.1.refs_2_
  34.9 4.3 %collective-permute-done.2.refs_3_ = bf16[192,1664]{1,0:T(8,128)(2,1)} collective-permute-done((bf16[192,1664]{1,0:T(8,128)(2,1)S(1)}, bf16[192,1664]{1,0:T(8,128)(2,1)}, u32[]{:S(2)}, u32[]{:S(2)}) %collective-permute-start.2) | collective-permute-done | bytes 639008 | tf_op jit(solution)/shard_map/ppermute | solution.py:453
  39.2 4.1 %shard_map.115 = (bf16[192,256]{1,0:T(8,128)(2,1)S(1)}, f32[256,256]{1,0:T(8,128)S(1)}, bf16[192,256]{1,0:T(8,128)(2,1)S(1)}, f32[1,128]{1,0:T(1,128)S(1)}) custom-call(s32[1]{0:T(128)} %bitcast.core, s32[1,256]{1,0:T(1,128)S(1)} %get-tuple-element.43.starts, f32[1,256]{1,0:T(1,128)S(1)} %get-tuple-element.44.weights.refs_0_, ...), custom_call_target="tpu_custom_call" | custom-call | flops 1342177280 | bytes 2097152 | tf_op jit(solution)/shard_map/pallas_call | solution.py:415
  43.4 4.1 %shard_map.116 = (bf16[192,256]{1,0:T(8,128)(2,1)S(1)}, f32[256,256]{1,0:T(8,128)S(1)}, bf16[192,256]{1,0:T(8,128)(2,1)S(1)}, f32[1,128]{1,0:T(1,128)S(1)}) custom-call(s32[1]{0:T(128)} %bitcast.core, s32[1,256]{1,0:T(1,128)S(1)} %get-tuple-element.43.starts, f32[1,256]{1,0:T(1,128)S(1)} %get-tuple-element.44.weights.refs_0_, ...), custom_call_target="tpu_custom_call" | custom-call | flops 1342177280 | bytes 2097152 | tf_op jit(solution)/shard_map/pallas_call | solution.py:415
  47.5 0.0 collective-permute-done.3.refs_2_
  47.5 0.0 collective-permute-done.4.refs_3_
  47.5 3.1 %shard_map.118 = (bf16[192,256]{1,0:T(8,128)(2,1)S(1)}, f32[256,256]{1,0:T(8,128)S(1)}, bf16[192,256]{1,0:T(8,128)(2,1)S(1)}, f32[1,128]{1,0:T(1,128)S(1)}) custom-call(s32[1]{0:T(128)} %bitcast.core, s32[1,256]{1,0:T(1,128)S(1)} %get-tuple-element.43.starts, f32[1,256]{1,0:T(1,128)S(1)} %get-tuple-element.44.weights.refs_0_, ...), custom_call_target="tpu_custom_call" | custom-call | flops 1342177280 | bytes 2097152 | tf_op jit(solution)/shard_map/pallas_call | solution.py:415
  50.5 0.1 shard_map.119
  50.6 5.0 %collective-permute-start.5 = (bf16[192,768]{1,0:T(8,128)(2,1)S(1)}, bf16[192,768]{1,0:T(8,128)(2,1)S(1)}, u32[]{:S(2)}, u32[]{:S(2)}) collective-permute-start(bf16[192,768]{1,0:T(8,128)(2,1)S(1)} %get-tuple-element.61), channel_id=1, source_target_pairs={{0,8},{4,508},{8,16},{12,4},{16,24},{20,12},{24,32},{28,20},{32,40... | collective-permute-start | bytes 884744 | tf_op jit(solution)/shard_map/ppermute | solution.py:453
  55.6 1.9 %collective-permute-start.6 = (bf16[192,768]{1,0:T(8,128)(2,1)S(1)}, bf16[192,768]{1,0:T(8,128)(2,1)S(1)}, u32[]{:S(2)}, u32[]{:S(2)}) collective-permute-start(bf16[192,768]{1,0:T(8,128)(2,1)S(1)} %get-tuple-element.62), channel_id=1, source_target_pairs={{0,508},{4,8},{8,4},{12,16},{16,12},{20,24},{24,20},{28,32},{32,28... | collective-permute-start | bytes 884744 | tf_op jit(solution)/shard_map/ppermute | solution.py:453
  57.5 11.2 %all_to_all.22 = f32[16,1,128]{2,1,0:T(1,128)S(1)} all-to-all(f32[16,1,128]{2,1,0:T(1,128)S(1)} %bitcast.18), channel_id=1, replica_groups=mesh['y'=8,'z'=4,'parity'=2,'core'=2,'head'=4] {'z','parity','core'}, dimensions={0} | all-to-all | bytes 16384 | tf_op jit(solution)/shard_map/all_to_all | solution.py:493
  68.7 0.0 collective-permute-done.5.mine
  68.7 0.0 collective-permute-done.6.other
  68.7 0.1 shard_map.120
  68.8 2.6 %collective-permute-start.7 = (f32[192,768]{1,0:T(8,128)S(1)}, f32[192,768]{1,0:T(8,128)S(1)}, u32[]{:S(2)}, u32[]{:S(2)}) collective-permute-start(f32[192,768]{1,0:T(8,128)S(1)} %get-tuple-element.65), channel_id=1, source_target_pairs={{0,4},{4,0},{1,5},{5,1},{2,6},{6,2},{3,7},{7,3},{8,12},{12,8},{9,1... | collective-permute-start | bytes 1769480 | tf_op jit(solution)/shard_map/ppermute | solution.py:448
  71.4 18.1 %all_to_all.23 = f32[32,1,128]{2,1,0:T(1,128)S(1)} all-to-all(f32[32,1,128]{2,1,0:T(1,128)S(1)} %bitcast.17), channel_id=1, replica_groups=mesh['y'=8,'z'=4,'parity'=2,'core'=2,'head'=4] {'y','head'}, dimensions={0} | all-to-all | bytes 32768 | tf_op jit(solution)/shard_map/all_to_all | solution.py:493
  89.5 0.0 collective-permute-done.7.recv
  89.5 1.0 %shard_map.121 = (f32[128,384]{1,0:T(8,128)}, f32[128,384]{1,0:T(8,128)}, f32[128,384]{1,0:T(8,128)}, f32[1,1]{1,0:T(1,128)}) custom-call(s32[1]{0:T(128)} %bitcast.core, f32[32,128]{1,0:T(8,128)S(1)} %bitcast.13, f32[256,768]{1,0:T(8,128)S(1)} %get-tuple-element.64.keep, f32[192,768]{1,0:T(8,128)S(1)} %collective-permute-done.7.recv), custom_call_target="tpu_custom_call" | custom-call | bytes 1048576 | tf_op jit(solution)/shard_map/pallas_call | solution.py:512
  (6 shorter events, 0.1 us)
Async XLA Ops:
  3.3 10.7 %collective-permute-start = (bf16[128,2560]{1,0:T(8,128)(2,1)}, bf16[128,2560]{1,0:T(8,128)(2,1)S(1)}, u32[]{:S(2)}, u32[]{:S(2)}) collective-permute-start(bf16[128,2560]{1,0:T(8,128)(2,1)} %get-tuple-element.38), channel_id=1, source_target_pairs={{0,4},{4,0},{1,5},{5,1},{2,6},{6,2},{3,7},{7,3},{8,12},{12,8},{9,1... | collective-permute-start | bytes 1966088 | tf_op jit(solution)/shard_map/ppermute | solution.py:448
  14.0 1.1 %copy-start = (bf16[128,2560]{1,0:T(8,128)(2,1)S(1)}, bf16[128,2560]{1,0:T(8,128)(2,1)}, u32[]{:S(2)}) copy-start(bf16[128,2560]{1,0:T(8,128)(2,1)} %get-tuple-element.39.keep.refs_0_) | copy-start | bytes 1966084
  15.1 10.4 %copy-start.2 = (s32[16384]{0:T(1024)S(1)}, s32[16384]{0:T(1024)}, u32[]{:S(2)}) copy-start(s32[16384]{0:T(1024)} %param.14) | copy-start | bytes 196612
  15.1 10.4 %copy-start.3 = (f32[16384]{0:T(1024)S(1)}, f32[16384]{0:T(1024)}, u32[]{:S(2)}) copy-start(f32[16384]{0:T(1024)} %param.15) | copy-start | bytes 196612
  15.1 10.6 %copy-start.1 = (bf16[128,2560]{1,0:T(8,128)(2,1)S(1)}, bf16[128,2560]{1,0:T(8,128)(2,1)}, u32[]{:S(2)}) copy-start(bf16[128,2560]{1,0:T(8,128)(2,1)} %get-tuple-element.39.keep.refs_0_) | copy-start | bytes 1966084
  15.2 19.7 %collective-permute-start.1 = (bf16[192,1664]{1,0:T(8,128)(2,1)S(1)}, bf16[192,1664]{1,0:T(8,128)(2,1)S(1)}, u32[]{:S(2)}, u32[]{:S(2)}) collective-permute-start(bf16[192,1664]{1,0:T(8,128)(2,1)S(1)} %shard_map.113), channel_id=1, source_target_pairs={{0,8},{4,508},{8,16},{12,4},{16,24},{20,12},{24,32},{28,20},{32,40... | collective-permute-start | bytes 1916936 | tf_op jit(solution)/shard_map/ppermute | solution.py:453
  23.6 15.7 %collective-permute-start.2 = (bf16[192,1664]{1,0:T(8,128)(2,1)S(1)}, bf16[192,1664]{1,0:T(8,128)(2,1)}, u32[]{:S(2)}, u32[]{:S(2)}) collective-permute-start(bf16[192,1664]{1,0:T(8,128)(2,1)S(1)} %shard_map.112), channel_id=1, source_target_pairs={{0,504},{4,12},{8,0},{12,20},{16,8},{20,28},{24,16},{28,36},{32,24... | collective-permute-start | bytes 1916936 | tf_op jit(solution)/shard_map/ppermute | solution.py:453
  25.8 21.6 %collective-permute-start.3 = (bf16[192,896]{1,0:T(8,128)(2,1)S(1)}, bf16[192,896]{1,0:T(8,128)(2,1)S(1)}, u32[]{:S(2)}, u32[]{:S(2)}) collective-permute-start(bf16[192,896]{1,0:T(8,128)(2,1)S(1)} %get-tuple-element.48), channel_id=1, source_target_pairs={{0,504},{4,12},{8,0},{12,20},{16,8},{20,28},{24,16},{28,36},{32,24... | collective-permute-start | bytes 1032200 | tf_op jit(solution)/shard_map/ppermute | solution.py:453
  27.7 19.7 %collective-permute-start.4 = (bf16[192,896]{1,0:T(8,128)(2,1)S(1)}, bf16[192,896]{1,0:T(8,128)(2,1)S(1)}, u32[]{:S(2)}, u32[]{:S(2)}) collective-permute-start(bf16[192,896]{1,0:T(8,128)(2,1)S(1)} %get-tuple-element.49), channel_id=1, source_target_pairs={{0,8},{4,508},{8,16},{12,4},{16,24},{20,12},{24,32},{28,20},{32,40... | collective-permute-start | bytes 1032200 | tf_op jit(solution)/shard_map/ppermute | solution.py:453
  50.6 18.1 %collective-permute-start.5 = (bf16[192,768]{1,0:T(8,128)(2,1)S(1)}, bf16[192,768]{1,0:T(8,128)(2,1)S(1)}, u32[]{:S(2)}, u32[]{:S(2)}) collective-permute-start(bf16[192,768]{1,0:T(8,128)(2,1)S(1)} %get-tuple-element.61), channel_id=1, source_target_pairs={{0,8},{4,508},{8,16},{12,4},{16,24},{20,12},{24,32},{28,20},{32,40... | collective-permute-start | bytes 884744 | tf_op jit(solution)/shard_map/ppermute | solution.py:453
  55.6 13.2 %collective-permute-start.6 = (bf16[192,768]{1,0:T(8,128)(2,1)S(1)}, bf16[192,768]{1,0:T(8,128)(2,1)S(1)}, u32[]{:S(2)}, u32[]{:S(2)}) collective-permute-start(bf16[192,768]{1,0:T(8,128)(2,1)S(1)} %get-tuple-element.62), channel_id=1, source_target_pairs={{0,508},{4,8},{8,4},{12,16},{16,12},{20,24},{24,20},{28,32},{32,28... | collective-permute-start | bytes 884744 | tf_op jit(solution)/shard_map/ppermute | solution.py:453
  68.8 20.6 %collective-permute-start.7 = (f32[192,768]{1,0:T(8,128)S(1)}, f32[192,768]{1,0:T(8,128)S(1)}, u32[]{:S(2)}, u32[]{:S(2)}) collective-permute-start(f32[192,768]{1,0:T(8,128)S(1)} %get-tuple-element.65), channel_id=1, source_target_pairs={{0,4},{4,0},{1,5},{5,1},{2,6},{6,2},{3,7},{7,3},{8,12},{12,8},{9,1... | collective-permute-start | bytes 1769480 | tf_op jit(solution)/shard_map/ppermute | solution.py:448
